TPU v7x, 256 devices: a whole 4x4x8 slice. The times are simulated.
256 devices in a mesh: grp: 4 (over y), dev: 64 (over x, z, core).
Axes of the slice: x: 4, y: 4, z: 8, core: 2. Of those that a mesh axis runs over, the one named last changes fastest.
Arguments:
- a_blocks: bfloat16 [32768, 4, 64, 64], P(('grp', 'dev')), may hold values from -6 to 6
- r_blocks: bfloat16 [32768, 64, 64], P(('grp', 'dev')), may hold values from -0.75 to 0.75
- p_blocks: bfloat16 [32768, 64, 64], P(('grp', 'dev')), may hold values from -0.75 to 0.75
- neighbours: int32 [32768, 3], P(('grp', 'dev')), may hold values from 0 to 319, as said below
- send_rows: int32 [256, 64, 3], P(('grp', 'dev')), may hold values from 0 to 127
- parent: int32 [32768], P(('grp', 'dev')), may hold values from 0 to 4095, as said below
- slot: int32 [32768, 4], P(('grp', 'dev')), may hold values from 0 to 6
Outputs:
- coarse_operator: float32 [4096, 7, 64, 64], P(('grp', 'dev'))
Inputs may be any that keep to these rules, and one draw needn't show every extreme that they name: `neighbours`: with the notation of the steps: entries of device n below 128 are its own elements; every value from 128 to 319 appears exactly once among the entries of each device. The element at local position j of device n has its parent among the 16 coarse rows c * 16 to c * 16 + 15 of device c = (j // 32) * 64 + n % 64; each coarse row is the parent of an element in each of those blocks of 32 positions that point to it.
All inputs are finite; a program needn't handle non-finite values.
Results may differ from a plain program's by a relative error of at most 0.0029.
Values may be sent and summed in bfloat16 or wider, within the bound.
No kernel may reach another device: no remote copies, remote signals or barrier semaphores. Data moves between devices by JAX's collectives and lax.ppermute only.
A program may use at most 128 MiB of HBM per device.

v0:
```python
import jax
import jax.numpy as jnp
from jax import lax
from jax.sharding import PartitionSpec as P

B = 64
S = 7
CR_DEV = 16


def on_device(a_blocks, r_blocks, p_blocks, neighbours, send_rows, parent, slot):
    elements = a_blocks.shape[0]
    stencil = a_blocks.shape[1]
    groups = lax.axis_size("grp")
    outgoing = jnp.take(p_blocks, send_rows[0].reshape(-1), axis=0)
    incoming = lax.all_to_all(outgoing, "dev", split_axis=0, concat_axis=0, tiled=True)
    extended = jnp.concatenate([p_blocks, incoming], 0)
    own_index = jnp.arange(elements, dtype=jnp.int32)[:, None]
    full_index = jnp.concatenate([own_index, neighbours], 1)
    gathered = jnp.take(extended, full_index, axis=0)
    applied = jnp.einsum(
        "ekab,ekbc->ekac", a_blocks, gathered, preferred_element_type=jnp.float32
    ).astype(jnp.bfloat16)
    local_row = parent % CR_DEV
    products = jnp.einsum("eab,ekbc->ekac", r_blocks, applied, preferred_element_type=jnp.float32)
    group_span = elements // groups
    target = jnp.arange(elements, dtype=jnp.int32) // group_span
    segment_ids = ((target * CR_DEV + local_row)[:, None] * S + slot).reshape(-1)
    partial_sums = jax.ops.segment_sum(
        products.reshape(elements * stencil, B, B), segment_ids, num_segments=groups * CR_DEV * S
    )
    coarse = lax.psum_scatter(
        partial_sums.reshape(groups * CR_DEV, S, B, B), "grp", scatter_dimension=0, tiled=True
    )
    return coarse


def solution(mesh):
    return jax.shard_map(
        on_device,
        mesh=mesh,
        in_specs=(
            P(("grp", "dev"), None, None, None),
            P(("grp", "dev"), None, None),
            P(("grp", "dev"), None, None),
            P(("grp", "dev"), None),
            P(("grp", "dev"), None, None),
            P(("grp", "dev")),
            P(("grp", "dev"), None),
        ),
        out_specs=P(("grp", "dev"), None, None, None),
        check_vma=False,
    )
```

profile of v0, /device:TPU:1, one launch (start us, length us, event | category | flops | bytes accessed | tf_op | source)
XLA Modules:
  0.0 365.1 jit_solution(1562925460367797528)
XLA Ops:
  6.5 0.8 copy.12
  7.3 0.1 reshape_squeeze.6
  7.4 0.1 reshape_squeeze.5
  7.6 3.9 %copy.15 = bf16[128,64,64]{2,1,0:T(8,128)(2,1)S(1)} copy(bf16[128,64,64]{0,2,1:T(8,128)(2,1)} %param.9) | data formatting | bytes 2097152 | tf_op args[2]
  11.6 2.7 gather_fusion
  14.3 0.0 copy-start.2
  14.3 0.0 copy-start.4
  14.3 0.0 copy-start.3
  14.3 0.0 copy-start.1
  14.3 3.5 broadcast_select_fusion
  17.8 6.2 %reshape.145 = bf16[64,2,6144]{2,1,0:T(2,128)(2,1)} reshape(bf16[192,64,64]{2,1,0:T(8,128)(2,1)} %broadcast_select_fusion) | data formatting | bytes 3145728
  24.1 13.2 %all-to-all-start = ((bf16[64,2,6144]{2,1,0:T(2,128)(2,1)}), bf16[64,2,6144]{2,1,0:T(2,128)(2,1)}, u32[]{:S(2)}, u32[]{:S(2)}) async-start(bf16[64,2,6144]{2,1,0:T(2,128)(2,1)} %reshape.145), calls=%async_computation | async-start | bytes 3145728 | tf_op jit(solution)/shard_map/all_to_all | solution.py:16
  37.2 0.0 reduce-scatter.2.cloned.1.call-start
  37.3 0.0 copy-done.2
  37.3 0.1 copy.11
  37.4 0.0 copy-done.4
  37.5 0.0 copy-done.3
  37.5 0.1 copy.10
  37.6 0.1 reshape.136
  37.7 0.1 copy.16
  37.9 0.1 reshape.128
  38.0 0.0 copy-done.1
  38.0 4.0 %copy.20 = bf16[128,64,64,1]{2,1,3,0:T(8,128)(2,1)} copy(bf16[128,64,64,1]{0,2,1,3:T(8,128)(2,1)S(1)} %bitcast.18) | data formatting | bytes 2097152 | tf_op args[1]
  42.0 15.7 %copy.19 = bf16[128,4,64,64]{2,3,1,0:T(8,128)(2,1)} copy(bf16[128,4,64,64]{0,3,2,1:T(8,128)(2,1)} %param.7) | data formatting | bytes 8388608 | tf_op args[0]
  57.7 19.3 %all-to-all-done = bf16[64,2,6144]{2,1,0:T(2,128)(2,1)} async-done(((bf16[64,2,6144]{2,1,0:T(2,128)(2,1)}), bf16[64,2,6144]{2,1,0:T(2,128)(2,1)}, u32[]{:S(2)}, u32[]{:S(2)}) %all-to-all-start) | async-done | bytes 1572896 | tf_op jit(solution)/shard_map/all_to_all | solution.py:16
  77.0 6.3 %reshape.146 = bf16[192,64,64]{2,1,0:T(8,128)(2,1)} reshape(bf16[64,2,6144]{2,1,0:T(2,128)(2,1)} %all-to-all-done) | data formatting | bytes 3145728
  83.3 5.2 %pad_maximum_fusion = bf16[320,64,64]{2,1,0:T(8,128)(2,1)} fusion(bf16[192,64,64]{2,1,0:T(8,128)(2,1)} %reshape.146, bf16[128,64,64]{2,1,0:T(8,128)(2,1)S(1)} %copy.15), kind=kLoop, calls=%fused_computation.9 | loop fusion | flops 1310720 | bytes 5242880 | tf_op jit(solution)/shard_map/concatenate | solution.py:17
  88.5 0.0 copy-start
  88.5 22.3 %gather_fusion.1 = bf16[512,64,64]{2,1,0:T(8,128)(2,1)} fusion(bf16[320,64,64]{2,1,0:T(8,128)(2,1)} %pad_maximum_fusion, s32[1024]{0:T(1024)S(1)} %pad_clamp_fusion), kind=kCustom, calls=%fused_computation.1 | custom fusion | bytes 8390656 | tf_op jit(solution)/shard_map/jit(_take)/gather | solution.py:20
  110.8 0.0 copy-done
  110.8 13.0 %fusion = f32[128,4,64,64]{3,2,1,0:T(8,128)} fusion(bf16[128,64,64,1]{2,1,3,0:T(8,128)(2,1)S(1)} %copy-done, bf16[128,4,64,64]{2,3,1,0:T(8,128)(2,1)} %copy.19, bf16[128,4,64,64]{3,2,1,0:T(8,128)(2,1)} %bitcast.17, pred[128,4]{1,0:T(8,128)(4,1)S(1)} %copy.11), kind=kOutput, calls=%fused_computation.3 | convolution fusion | flops 541065216 | bytes 17826304 | tf_op jit(solution)/shard_map/eab,ekbc->ekac/dot_general | solution.py:25
  123.8 17.7 %copy.18 = f32[512,64,64]{2,1,0:T(8,128)} copy(f32[512,64,64]{1,2,0:T(8,128)} %bitcast.16) | data formatting | bytes 16777216 | tf_op jit(solution)/shard_map/reshape | solution.py:30
  141.5 7.1 %broadcast_in_dim.25 = f32[448,64,64]{2,1,0:T(8,128)} broadcast(f32[]{:T(128)} %constant.52.clone.1), dimensions={} | broadcast | bytes 7340036 | tf_op jit(solution)/shard_map/broadcast_in_dim | solution.py:29
  148.6 78.2 %scatter_fusion = f32[448,64,64]{2,1,0:T(8,128)} fusion(f32[448,64,64]{2,1,0:T(8,128)} %broadcast_in_dim.25, s32[512]{0:T(512)S(1)} %reshape.136, f32[512,64,64]{2,1,0:T(8,128)} %copy.18), kind=kCustom, calls=%fused_computation.2 | custom fusion | flops 2097152 | bytes 25167872 | tf_op jit(solution)/shard_map/scatter-add | solution.py:29
  226.8 0.0 reduce-scatter.2.cloned.1.call-update
  226.8 131.5 %reduce-scatter.2.cloned.1.call-done = f32[16,7,64,64]{3,2,1,0:T(8,128)} async-done(((f32[64,7,64,64]{3,2,1,0:T(8,128)}), f32[16,7,64,64]{3,2,1,0:T(8,128)}) %reduce-scatter.2.cloned.1.call-update) | async-done | bytes 1835024 | tf_op jit(solution)/shard_map/reduce_scatter | solution.py:32
  (10 shorter events, 0.1 us)
Async XLA Ops:
  14.3 23.0 %copy-start.2 = (s32[128,3]{0,1:T(4,128)S(1)}, s32[128,3]{0,1:T(4,128)}, u32[]{:S(2)}) copy-start(s32[128,3]{0,1:T(4,128)} %param.10) | copy-start | bytes 4612
  14.3 23.2 %copy-start.4 = (s32[128]{0:T(128)S(1)}, s32[128]{0:T(128)}, u32[]{:S(2)}) copy-start(s32[128]{0:T(128)} %param.12) | copy-start | bytes 1540
  14.3 23.2 %copy-start.3 = (s32[128,4]{0,1:T(4,128)S(1)}, s32[128,4]{0,1:T(4,128)}, u32[]{:S(2)}) copy-start(s32[128,4]{0,1:T(4,128)} %param.13) | copy-start | bytes 6148
  14.3 23.7 %copy-start.1 = (bf16[128,64,64]{0,2,1:T(8,128)(2,1)S(1)}, bf16[128,64,64]{0,2,1:T(8,128)(2,1)}, u32[]{:S(2)}) copy-start(bf16[128,64,64]{0,2,1:T(8,128)(2,1)} %param.8) | copy-start | bytes 3145732
  24.1 52.9 %all-to-all-start = ((bf16[64,2,6144]{2,1,0:T(2,128)(2,1)}), bf16[64,2,6144]{2,1,0:T(2,128)(2,1)}, u32[]{:S(2)}, u32[]{:S(2)}) async-start(bf16[64,2,6144]{2,1,0:T(2,128)(2,1)} %reshape.145), calls=%async_computation | async-start | bytes 3145728 | tf_op jit(solution)/shard_map/all_to_all | solution.py:16
  37.2 321.1 %reduce-scatter.2.cloned.1.call-start = ((), (), s32[]{:S(2)}) async-start(), calls=%async_computation.2 | async-start | bytes 18350080 | tf_op jit(solution)/shard_map/reduce_scatter | solution.py:32
  88.5 22.3 %copy-start = (bf16[128,64,64,1]{2,1,3,0:T(8,128)(2,1)S(1)}, bf16[128,64,64,1]{2,1,3,0:T(8,128)(2,1)}, u32[]{:S(2)}) copy-start(bf16[128,64,64,1]{2,1,3,0:T(8,128)(2,1)} %copy.20) | copy-start | bytes 3145732
Sparse Core Ops, SparseCore 0:
  226.9 131.3 reduce-scatter.1
where the time goes:
time: 367 us; the launch traced here: 365 us
  waiting for transfers between devices  151 us (41%)
  local copies, waits for them, and re-layouts  87.6 us (24%)
  other arithmetic  87 us (24%)
  between operations  13.5 us (4%)
  starting transfers between devices  13.2 us (4%)
  matrix products  13 us (4%)
    reduce_scatter x1, waiting for transfers between devices, on_device(): lax.psum_scatter(partial_sums.reshape(groups * CR_DEV, S, B, B), 'grp', s...  131 us
    scatter-add x1, other arithmetic, on_device(): jax.ops.segment_sum(products.reshape(elements * stencil, B, B), segment_i...  78.2 us
    unnamed x16, local copies, waits for them, and re-layouts  37 us
    gather x1, local copies, waits for them, and re-layouts, on_device(): gathered = jnp.take(extended, full_index, axis=0)  22.3 us
    all_to_all x1, waiting for transfers between devices, on_device(): lax.all_to_all(outgoing, 'dev', split_axis=0, concat_axis=0, tiled=True)  19.3 us
    reshape x1, local copies, waits for them, and re-layouts, on_device(): products.reshape(elements * stencil, B, B)  17.7 us
    all_to_all x1, starting transfers between devices, on_device(): lax.all_to_all(outgoing, 'dev', split_axis=0, concat_axis=0, tiled=True)  13.2 us
    dot_general x1, matrix products, on_device(): jnp.einsum('eab,ekbc->ekac', r_blocks, applied, preferred_element_type=jn...  13 us
  transfers between devices with their start and end apart: 2, of which 2 were waited for; matrix products, arithmetic and copies ran while one was open for 6% of the time, Pallas kernels for 0%

commit v1 on v0

v1 whole, which is shorter than its diff:
```python
import functools

import jax
import jax.numpy as jnp
from jax import lax
from jax.experimental import pallas as pl
from jax.experimental.pallas import tpu as pltpu
from jax.sharding import PartitionSpec as P

MB = 1 << 20
F32 = jnp.float32
BF16 = jnp.bfloat16
VM = pltpu.VMEM
SM = pltpu.SMEM

E = 128
SPAN = 32
ROWS = 16
SLOTS = 7
BLOCKS = ROWS * SLOTS
HALF = BLOCKS // 2
FAR = 192
NEAR = 4 * E - FAR
CAP = 3 * SPAN
GROUP = 32
AREA = CAP + GROUP


def rows_at(index, size):
    return pl.ds(pl.multiple_of(index * size, size), size)


def transpose_slabs(slab_of, steps, stride, wide):
    @pl.loop(0, steps, unroll=8)
    def _(i):
        wide[pl.ds(i, E, stride=stride), :] = slab_of(i).astype(F32).T


def send_kernel(rows, p_ref, out_ref, packed, wide):
    transpose_slabs(
        lambda i: jnp.concatenate([p_ref[rows_at(i, 64), :], p_ref[rows_at(i + 32, 64), :]], 0), 32, 40, wide
    )
    packed[...] = wide[...].reshape(E, 40, 128)[:, :32].astype(BF16)

    @pl.loop(0, 64, unroll=4)
    def _(peer):
        for s in range(3):
            out_ref[peer * 3 + s] = packed[rows[s, peer]]


def send_blocks(rows, p_t):
    return pl.pallas_call(
        send_kernel,
        out_shape=jax.ShapeDtypeStruct((FAR, 32, 128), BF16),
        in_specs=[pl.BlockSpec(memory_space=SM), pl.BlockSpec(memory_space=VM)],
        out_specs=pl.BlockSpec(memory_space=VM),
        scratch_shapes=[VM((E, 32, 128), BF16), VM((E * 40, 128), F32)],
        compiler_params=pltpu.CompilerParams(vmem_limit_bytes=16 * MB),
        name="send_blocks",
    )(rows, p_t)


def term_of(pair, doubled):
    applied = jnp.dot(pair[:, :64], doubled, preferred_element_type=F32).astype(BF16)
    term = jnp.dot(pair[:, 64:], applied, preferred_element_type=F32)
    low = lax.broadcasted_iota(jnp.int32, (32, 128), 1) < 64
    return jnp.where(low, term[:32], term[32:])


def near_kernel(
    neighbours, slot, parent, a_ref, r_ref, p_ref,
    far_pairs, sums, counts, far_blocks, far_sums,
    pairs, doubled, wide, near_pairs, near_blocks, near_sums, far_list,
):
    def two(i):
        block = p_ref[rows_at(i, 64), :]
        return jnp.concatenate([block, block], 0)

    transpose_slabs(two, 64, 72, wide)
    doubled[...] = wide[...].reshape(E, 72, 128)[:, :64].astype(BF16)

    @pl.loop(0, 4)
    def _(k):
        transpose_slabs(
            lambda i: jnp.concatenate([a_ref[rows_at(k * 64 + i, 64), :], r_ref[rows_at(i, 64), :]], 0), 64, 72, wide
        )
        pairs[rows_at(k, E)] = wide[...].reshape(E, 72, 128)[:, :64].astype(BF16)

    sums[...] = jnp.zeros_like(sums)

    near = 0
    for j in range(4):
        start = j * AREA

        def element(i, carry):
            near, far = carry
            e = j * SPAN + i
            base = (parent[0, e] % ROWS) * SLOTS
            near_pairs[near] = e
            near_blocks[near] = e
            near_sums[near] = j * BLOCKS + base + slot[0, e]
            near = near + 1
            for k in range(1, 4):
                code = neighbours[k - 1, e]
                block_sum = base + slot[k, e]
                near_pairs[near] = k * E + e
                near_blocks[near] = code
                near_sums[near] = j * BLOCKS + block_sum
                far_list[far] = k * E + e
                far_blocks[far] = code - E
                far_sums[far] = block_sum
                here = (code < E).astype(jnp.int32)
                near = near + here
                far = far + (1 - here)
            return near, far

        near, far = lax.fori_loop(0, SPAN, element, (near, start))
        many = far - start
        counts[j] = many

        def keep(i, carry):
            far_pairs[j, i] = pairs[far_list[start + i]]
            return carry

        lax.fori_loop(0, many, keep, 0)

        def pad(i, carry):
            far_pairs[j, i] = jnp.zeros((64, 128), BF16)
            far_blocks[start + i] = 0
            far_sums[start + i] = 0
            return carry

        lax.fori_loop(many, (many + GROUP - 1) // GROUP * GROUP, pad, 0)

    @pl.loop(0, NEAR // GROUP)
    def _(g):
        found = [
            term_of(pairs[near_pairs[g * GROUP + u]], doubled[near_blocks[g * GROUP + u]]) for u in range(GROUP)
        ]
        for u in range(GROUP):
            sums[near_sums[g * GROUP + u]] += found[u]


def near_terms(neighbours, slot, parent, a_t, r_t, p_t):
    return pl.pallas_call(
        near_kernel,
        out_shape=[
            jax.ShapeDtypeStruct((4, CAP, 64, 128), BF16),
            jax.ShapeDtypeStruct((4 * BLOCKS, 32, 128), F32),
            jax.ShapeDtypeStruct((4,), jnp.int32),
            jax.ShapeDtypeStruct((4 * AREA,), jnp.int32),
            jax.ShapeDtypeStruct((4 * AREA,), jnp.int32),
        ],
        in_specs=[pl.BlockSpec(memory_space=SM)] * 3 + [pl.BlockSpec(memory_space=VM)] * 3,
        out_specs=[pl.BlockSpec(memory_space=VM)] * 2 + [pl.BlockSpec(memory_space=SM)] * 3,
        scratch_shapes=[
            VM((4 * E, 64, 128), BF16),
            VM((E, 64, 128), BF16),
            VM((E * 72, 128), F32),
            SM((NEAR + 8,), jnp.int32),
            SM((NEAR + 8,), jnp.int32),
            SM((NEAR + 8,), jnp.int32),
            SM((4 * AREA,), jnp.int32),
        ],
        compiler_params=pltpu.CompilerParams(vmem_limit_bytes=48 * MB),
        cost_estimate=pl.CostEstimate(flops=700_000_000, bytes_accessed=40_000_000, transcendentals=0),
        name="near_terms",
    )(neighbours, slot, parent, a_t, r_t, p_t)


def far_kernel(kinds, target, counts, far_blocks, far_sums, incoming, pairs, near, *refs):
    outs = refs[:-1]
    sums = refs[-1]
    sums[...] = near[0]
    j = target[0]
    start = j * AREA
    low = lax.broadcasted_iota(jnp.int32, (32, 128), 1) < 64

    def doubled(block):
        x = incoming[block]
        turned = jnp.concatenate([x[:, 64:], x[:, :64]], 1)
        return jnp.concatenate([jnp.where(low, x, turned), jnp.where(low, turned, x)], 0)

    def group(g, carry):
        at = g * GROUP
        found = [term_of(pairs[0, at + u], doubled(far_blocks[start + at + u])) for u in range(GROUP)]
        for u in range(GROUP):
            sums[far_sums[start + at + u]] += found[u]
        return carry

    lax.fori_loop(0, (counts[j] + GROUP - 1) // GROUP, group, 0)
    size = BLOCKS // len(kinds)
    for h, kind in enumerate(kinds):
        outs[h][...] = sums[h * size : (h + 1) * size].astype(kind)


def far_terms(kinds, target, lists, incoming, pairs, near, name):
    size = BLOCKS // len(kinds)
    return pl.pallas_call(
        functools.partial(far_kernel, kinds),
        grid_spec=pltpu.PrefetchScalarGridSpec(
            num_scalar_prefetch=4,
            grid=(1,),
            in_specs=[
                pl.BlockSpec((FAR, 32, 128), lambda i, target, *_: (0, 0, 0)),
                pl.BlockSpec((1, CAP, 64, 128), lambda i, target, *_: (target[0], 0, 0, 0)),
                pl.BlockSpec((1, BLOCKS, 32, 128), lambda i, target, *_: (target[0], 0, 0, 0)),
            ],
            out_specs=[pl.BlockSpec((size, 32, 128), lambda i, target, *_: (0, 0, 0))] * len(kinds),
            scratch_shapes=[VM((BLOCKS, 32, 128), F32)],
        ),
        out_shape=[jax.ShapeDtypeStruct((size, 32, 128), kind) for kind in kinds],
        compiler_params=pltpu.CompilerParams(vmem_limit_bytes=20 * MB),
        cost_estimate=pl.CostEstimate(flops=100_000_000, bytes_accessed=6_000_000, transcendentals=0),
        name=name,
    )(target, *lists, incoming, pairs, near)


def finish_kernel(own, low_a, low_b, high_a, high_b, out_ref):
    for h, (one, other) in enumerate(((low_a, low_b), (high_a, high_b))):
        total = own[h * HALF : (h + 1) * HALF] + one[...].astype(F32) + other[...].astype(F32)
        out_ref[h * HALF : (h + 1) * HALF, :32] = total[:, :, :64]
        out_ref[h * HALF : (h + 1) * HALF, 32:] = total[:, :, 64:]


def finish(*parts):
    return pl.pallas_call(
        finish_kernel,
        out_shape=jax.ShapeDtypeStruct((BLOCKS, 64, 64), F32),
        in_specs=[pl.BlockSpec(memory_space=VM)] * 5,
        out_specs=pl.BlockSpec(memory_space=VM),
        compiler_params=pltpu.CompilerParams(vmem_limit_bytes=24 * MB),
        name="finish",
    )(*parts)


def on_device(a_blocks, r_blocks, p_blocks, neighbours, send_rows, parent, slot):
    a_t = jnp.transpose(a_blocks, (1, 2, 3, 0)).reshape(4 * 4096, E)
    r_t = jnp.transpose(r_blocks, (1, 2, 0)).reshape(4096, E)
    p_t = jnp.transpose(p_blocks, (1, 2, 0)).reshape(4096, E)
    with jax.named_scope("exchange"):
        outgoing = send_blocks(jnp.transpose(send_rows, (2, 0, 1)).reshape(3, 64), p_t)
        incoming = lax.all_to_all(outgoing.reshape(64, 96, 128), "dev", 0, 0, tiled=True).reshape(FAR, 32, 128)
    with jax.named_scope("near"):
        pairs, near, *lists = near_terms(neighbours.T, slot.T, parent.reshape(1, E), a_t, r_t, p_t)
        near = near.reshape(4, BLOCKS, 32, 128)

    me = lax.axis_index("grp")

    def sums_of(ahead, kinds, name):
        target = ((me + ahead) % 4).astype(jnp.int32).reshape(1)
        return far_terms(kinds, target, lists, incoming, pairs, near, name)

    def to_next(x):
        return lax.ppermute(x, "grp", [(i, (i + 1) % 4) for i in range(4)])

    def to_last(x):
        return lax.ppermute(x, "grp", [(i, (i + 3) % 4) for i in range(4)])

    with jax.named_scope("far"):
        far_low, far_high = sums_of(2, (BF16, BF16), "far_two")
        passed_low, passed_high = to_next(far_low), to_last(far_high)
        next_low, next_high = sums_of(1, (F32, BF16), "far_next")
        from_last_high = to_next(next_high)
        last_low, last_high = sums_of(3, (BF16, F32), "far_last")
        from_next_low = to_last(last_low)
        from_last_low = to_next((next_low + passed_low.astype(F32)).astype(BF16))
        from_next_high = to_last((last_high + passed_high.astype(F32)).astype(BF16))
        (own,) = sums_of(0, (F32,), "far_own")
    with jax.named_scope("finish"):
        coarse = finish(own, from_last_low, from_next_low, from_last_high, from_next_high)
    return coarse.reshape(ROWS, SLOTS, 64, 64)


def solution(mesh):
    return jax.shard_map(
        on_device,
        mesh=mesh,
        in_specs=(
            P(("grp", "dev"), None, None, None),
            P(("grp", "dev"), None, None),
            P(("grp", "dev"), None, None),
            P(("grp", "dev"), None),
            P(("grp", "dev"), None, None),
            P(("grp", "dev")),
            P(("grp", "dev"), None),
        ),
        out_specs=P(("grp", "dev"), None, None, None),
        check_vma=False,
    )
```

time: 367 us -> 108 us (0.29)
  waiting for transfers between devices: 151 us -> 20.7 us
  other arithmetic: 87 us -> 3.87 us
  local copies, waits for them, and re-layouts: 87.6 us -> 20.8 us
  Pallas kernels: 0 us -> 40.4 us
  between operations: 13.5 us -> 0.12 us
  matrix products: 13 us -> 0 us
  starting transfers between devices: 13.2 us -> 21.1 us
    reduce_scatter x1 -> x0, waiting for transfers between devices: 131 us -> none  [on_device(): lax.psum_scatter(partial_sums.reshape(groups * CR_DEV, S, B, B), 'grp', s...]
    scatter-add x1 -> x0, other arithmetic: 78.2 us -> none  [on_device(): jax.ops.segment_sum(products.reshape(elements * stencil, B, B), segment_i...]
    pallas_call x0 -> x7, Pallas kernels: none -> 40.4 us  [the longest x1 25.6 us: near_terms(): pl.pallas_call(near_kernel, out_shape=[jax.ShapeDtypeStruct((4, CAP, 64,...]
    gather x2 -> x0, local copies, waits for them, and re-layouts: 25 us -> none  [the longest x1 22.3 us: on_device(): gathered = jnp.take(extended, full_index, axis=0)]
    reshape x1 -> x0, local copies, waits for them, and re-layouts: 17.7 us -> none  [on_device(): products.reshape(elements * stencil, B, B)]
    unnamed x16 -> x25, local copies, waits for them, and re-layouts: 37 us -> 20.8 us
    dot_general x1 -> x0, matrix products: 13 us -> none  [on_device(): jnp.einsum('eab,ekbc->ekac', r_blocks, applied, preferred_element_type=jn...]
    ppermute x0 -> x6, starting transfers between devices: none -> 8.16 us  [the longest x3 8.15 us: to_last(): return lax.ppermute(x, 'grp', [(i, (i + 3) % 4) for i in range(4)])]
  transfers between devices with their start and end apart: 2 -> 7, of which waited for: 2 -> 3; matrix products, arithmetic and copies ran while one was open for 6% -> 4% of each run, Pallas kernels for 0% -> 31%
where the time goes in v1:
time: 108 us; the launch traced here: 107 us
  Pallas kernels  40.4 us (37%)
  starting transfers between devices  21.1 us (20%)
  local copies, waits for them, and re-layouts  20.8 us (19%)
  waiting for transfers between devices  20.7 us (19%)
  other arithmetic  3.87 us (4%)
    pallas_call x1, Pallas kernels, near_terms(): pl.pallas_call(near_kernel, out_shape=[jax.ShapeDtypeStruct((4, CAP, 64,...  25.6 us
    unnamed x25, local copies, waits for them, and re-layouts  20.8 us
    all_to_all x1, starting transfers between devices, on_device(): lax.all_to_all(outgoing.reshape(64, 96, 128), 'dev', 0, 0, tiled=True)  13 us
    all_to_all x1, waiting for transfers between devices, on_device(): lax.all_to_all(outgoing.reshape(64, 96, 128), 'dev', 0, 0, tiled=True)  12.9 us
    pallas_call x4, Pallas kernels, far_terms(): pl.pallas_call(functools.partial(far_kernel, kinds), grid_spec=pltpu.Pref...  9.63 us
    ppermute x3, starting transfers between devices, to_last(): return lax.ppermute(x, 'grp', [(i, (i + 3) % 4) for i in range(4)])  8.15 us
    ppermute x3, waiting for transfers between devices, to_next(): return lax.ppermute(x, 'grp', [(i, (i + 1) % 4) for i in range(4)])  5.76 us
    pallas_call x1, Pallas kernels, send_blocks(): pl.pallas_call(send_kernel, out_shape=jax.ShapeDtypeStruct((FAR, 32, 128)...  2.74 us
  transfers between devices with their start and end apart: 7, of which 3 were waited for; matrix products, arithmetic and copies ran while one was open for 4% of the time, Pallas kernels for 31%

profile of v1, /device:TPU:1, one launch (start us, length us, event | category | flops | bytes accessed | tf_op | source)
XLA Modules:
  0.0 106.9 jit_solution(10731719034570309831)
XLA Ops:
  0.0 0.0 copy-start.9
  0.0 0.0 copy-start.10
  0.0 0.0 copy-start.11
  0.0 0.7 copy.10
  0.7 0.0 copy-start.6
  0.7 1.2 %copy-done.6 = bf16[128,64,64]{0,2,1:T(8,128)(2,1)S(1)} copy-done((bf16[128,64,64]{0,2,1:T(8,128)(2,1)S(1)}, bf16[128,64,64]{0,2,1:T(8,128)(2,1)}, u32[]{:S(2)}) %copy-start.6) | copy-done | bytes 1048600
  2.0 0.0 copy-start.7
  2.0 2.7 %send_blocks.1 = bf16[192,32,128]{2,1,0:T(8,128)(2,1)} custom-call(s32[3,64]{1,0:T(4,128)S(1)} %bitcast.36, bf16[4096,128]{1,0:T(8,128)(2,1)S(1)} %bitcast.33), custom_call_target="tpu_custom_call" | custom-call | tf_op jit(solution)/shard_map/exchange/send_blocks/pallas_call | solution.py:52
  4.7 13.0 %all-to-all-start = ((bf16[64,96,128]{2,1,0:T(8,128)(2,1)}), bf16[64,96,128]{2,1,0:T(8,128)(2,1)S(1)}, u32[]{:S(2)}, u32[]{:S(2)}) async-start(bf16[64,96,128]{2,1,0:T(8,128)(2,1)} %bitcast.13), calls=%async_computation | async-start | bytes 3145728 | tf_op jit(solution)/shard_map/exchange/all_to_all | solution.py:243
  17.7 0.0 copy-done.9
  17.7 0.0 copy-done.10
  17.7 0.0 copy-done.11
  17.7 0.0 copy-done.7
  17.7 0.0 copy-start.8
  17.8 1.2 %copy-done.8 = bf16[128,64,64]{0,2,1:T(8,128)(2,1)S(1)} copy-done((bf16[128,64,64]{0,2,1:T(8,128)(2,1)S(1)}, bf16[128,64,64]{0,2,1:T(8,128)(2,1)}, u32[]{:S(2)}) %copy-start.8) | copy-done | bytes 1048600
  19.0 25.6 %near_terms.1 = (bf16[4,96,64,128]{3,2,1,0:T(8,128)(2,1)}, f32[448,32,128]{2,1,0:T(8,128)}, s32[4]{0:T(128)S(1)}, s32[512]{0:T(512)S(1)}, s32[512]{0:T(512)S(1)}) custom-call(s32[3,128]{1,0:T(4,128)S(1)} %bitcast.37, s32[4,128]{1,0:T(4,128)S(1)} %bitcast.38, s32[1,128]{1,0:T(1,128)S(1)} %bitcast.39, bf16[16384,128]{1,0:T(8,128)(2,1)} %bitcast.40, ...), custom_call_target="tpu_custom_call" | custom-call | flops 700000000 | bytes 40000000 | tf_op jit(solution)/shard_map/near/near_terms/pallas_call | solution.py:145
  44.6 12.9 %all-to-all-done = bf16[64,96,128]{2,1,0:T(8,128)(2,1)S(1)} async-done(((bf16[64,96,128]{2,1,0:T(8,128)(2,1)}), bf16[64,96,128]{2,1,0:T(8,128)(2,1)S(1)}, u32[]{:S(2)}, u32[]{:S(2)}) %all-to-all-start) | async-done | bytes 1572896 | tf_op jit(solution)/shard_map/exchange/all_to_all | solution.py:243
  57.5 0.0 copy-start
  57.5 3.1 %copy-done = f32[448,32,128]{2,1,0:T(8,128)S(1)} copy-done((f32[448,32,128]{2,1,0:T(8,128)S(1)}, f32[448,32,128]{2,1,0:T(8,128)}, u32[]{:S(2)}) %copy-start) | copy-done | bytes 7340056
  60.6 0.0 copy-start.3
  60.6 2.8 %copy-done.3 = bf16[4,96,64,128]{3,2,1,0:T(8,128)(2,1)S(1)} copy-done((bf16[4,96,64,128]{3,2,1,0:T(8,128)(2,1)S(1)}, bf16[4,96,64,128]{3,2,1,0:T(8,128)(2,1)}, u32[]{:S(2)}) %copy-start.3) | copy-done | bytes 6291480
  63.4 2.0 %far_two.1 = (bf16[56,32,128]{2,1,0:T(8,128)(2,1)S(1)}, bf16[56,32,128]{2,1,0:T(8,128)(2,1)S(1)}) custom-call(s32[1]{0:T(128)} %bitcast.17.target, s32[4]{0:T(128)S(1)} %get-tuple-element.16.counts, s32[512]{0:T(512)S(1)} %get-tuple-element.17.far_blocks, s32[512]{0:T(512)S(1)} %get-tuple-element.18.far_sums, bf16[192,32,128]{2,1,0:T(8,128)(2,1)S(1)} %bitcast.29, ...), custom_call_target="tpu_custom_call" | custom-call | flops 100000000 | bytes 6000000 | tf_op jit(solution)/shard_map/far/far_two/pallas_call | solution.py:199
  65.4 2.8 %collective-permute-start.4 = (bf16[56,32,128]{2,1,0:T(8,128)(2,1)S(1)}, bf16[56,32,128]{2,1,0:T(8,128)(2,1)}, u32[]{:S(2)}, u32[]{:S(2)}) collective-permute-start(bf16[56,32,128]{2,1,0:T(8,128)(2,1)S(1)} %get-tuple-element.26), channel_id=1, source_target_pairs={{0,192},{64,0},{128,64},{192,128},{1,193},{65,1},{129,65},{193,129... | collective-permute-start | bytes 1376264 | tf_op jit(solution)/shard_map/far/ppermute | solution.py:258
  68.2 0.0 collective-permute-start
  68.2 0.0 copy-start.1
  68.2 3.1 %copy-done.1 = f32[448,32,128]{2,1,0:T(8,128)S(1)} copy-done((f32[448,32,128]{2,1,0:T(8,128)S(1)}, f32[448,32,128]{2,1,0:T(8,128)}, u32[]{:S(2)}) %copy-start.1) | copy-done | bytes 7340056
  71.3 0.0 copy-start.4
  71.3 2.8 %copy-done.4 = bf16[4,96,64,128]{3,2,1,0:T(8,128)(2,1)S(1)} copy-done((bf16[4,96,64,128]{3,2,1,0:T(8,128)(2,1)S(1)}, bf16[4,96,64,128]{3,2,1,0:T(8,128)(2,1)}, u32[]{:S(2)}) %copy-start.4) | copy-done | bytes 6291480
  74.1 2.8 %far_last.1 = (bf16[56,32,128]{2,1,0:T(8,128)(2,1)}, f32[56,32,128]{2,1,0:T(8,128)S(1)}) custom-call(s32[1]{0:T(128)} %bitcast.18.target, s32[4]{0:T(128)S(1)} %get-tuple-element.16.counts, s32[512]{0:T(512)S(1)} %get-tuple-element.17.far_blocks, s32[512]{0:T(512)S(1)} %get-tuple-element.18.far_sums, bf16[192,32,128]{2,1,0:T(8,128)(2,1)S(1)} %bitcast.30, ...), custom_call_target="tpu_custom_call" | custom-call | flops 100000000 | bytes 6000000 | tf_op jit(solution)/shard_map/far/far_last/pallas_call | solution.py:199
  76.9 2.7 %collective-permute-start.2 = (bf16[56,32,128]{2,1,0:T(8,128)(2,1)}, bf16[56,32,128]{2,1,0:T(8,128)(2,1)S(1)}, u32[]{:S(2)}, u32[]{:S(2)}) collective-permute-start(bf16[56,32,128]{2,1,0:T(8,128)(2,1)} %get-tuple-element.23), channel_id=1, source_target_pairs={{0,192},{64,0},{128,64},{192,128},{1,193},{65,1},{129,65},{193,129... | collective-permute-start | bytes 1376264 | tf_op jit(solution)/shard_map/far/ppermute | solution.py:258
  79.5 2.8 %far_next.1 = (f32[56,32,128]{2,1,0:T(8,128)S(1)}, bf16[56,32,128]{2,1,0:T(8,128)(2,1)}) custom-call(s32[1]{0:T(128)} %bitcast.16.target, s32[4]{0:T(128)S(1)} %get-tuple-element.16.counts, s32[512]{0:T(512)S(1)} %get-tuple-element.17.far_blocks, s32[512]{0:T(512)S(1)} %get-tuple-element.18.far_sums, bf16[192,32,128]{2,1,0:T(8,128)(2,1)S(1)} %bitcast.31, ...), custom_call_target="tpu_custom_call" | custom-call | flops 100000000 | bytes 6000000 | tf_op jit(solution)/shard_map/far/far_next/pallas_call | solution.py:199
  82.3 0.0 collective-permute-start.3
  82.3 0.0 collective-permute-done.4
  82.3 1.9 %add_convert_fusion = bf16[56,32,128]{2,1,0:T(8,128)(2,1)} fusion(f32[56,32,128]{2,1,0:T(8,128)S(1)} %get-tuple-element.25, bf16[56,32,128]{2,1,0:T(8,128)(2,1)} %collective-permute-done.4), kind=kLoop, calls=%fused_computation | loop fusion | flops 688128 | bytes 1835008 | tf_op jit(solution)/shard_map/far/convert_element_type | solution.py:268
  84.2 2.7 %collective-permute-start.5 = (bf16[56,32,128]{2,1,0:T(8,128)(2,1)}, bf16[56,32,128]{2,1,0:T(8,128)(2,1)S(1)}, u32[]{:S(2)}, u32[]{:S(2)}) collective-permute-start(bf16[56,32,128]{2,1,0:T(8,128)(2,1)} %add_convert_fusion), channel_id=1, source_target_pairs={{0,192},{64,0},{128,64},{192,128},{1,193},{65,1},{129,65},{193,129... | collective-permute-start | bytes 1376264 | tf_op jit(solution)/shard_map/far/ppermute | solution.py:258
  86.9 0.0 collective-permute-done
  86.9 1.9 %add_convert_fusion.1 = bf16[56,32,128]{2,1,0:T(8,128)(2,1)} fusion(f32[56,32,128]{2,1,0:T(8,128)S(1)} %get-tuple-element.21, bf16[56,32,128]{2,1,0:T(8,128)(2,1)} %collective-permute-done), kind=kLoop, calls=%fused_computation.1 | loop fusion | flops 688128 | bytes 1835008 | tf_op jit(solution)/shard_map/far/convert_element_type | solution.py:267
  88.8 0.0 collective-permute-start.1
  88.8 0.0 copy-start.2
  88.8 3.1 %copy-done.2 = f32[448,32,128]{2,1,0:T(8,128)S(1)} copy-done((f32[448,32,128]{2,1,0:T(8,128)S(1)}, f32[448,32,128]{2,1,0:T(8,128)}, u32[]{:S(2)}) %copy-start.2) | copy-done | bytes 7340056
  91.9 0.0 copy-start.5
  91.9 2.8 %copy-done.5 = bf16[4,96,64,128]{3,2,1,0:T(8,128)(2,1)S(1)} copy-done((bf16[4,96,64,128]{3,2,1,0:T(8,128)(2,1)S(1)}, bf16[4,96,64,128]{3,2,1,0:T(8,128)(2,1)}, u32[]{:S(2)}) %copy-start.5) | copy-done | bytes 6291480
  94.7 2.1 %far_own.1.own = f32[112,32,128]{2,1,0:T(8,128)S(1)} custom-call(s32[1]{0:T(128)} %bitcast.target, s32[4]{0:T(128)S(1)} %get-tuple-element.16.counts, s32[512]{0:T(512)S(1)} %get-tuple-element.17.far_blocks, s32[512]{0:T(512)S(1)} %get-tuple-element.18.far_sums, bf16[192,32,128]{2,1,0:T(8,128)(2,1)S(1)} %bitcast.32, bf16[4,96,64,128]{3,2,1,0:T(8,128)(2,1)S(1)} %copy-done.5, ...), custom_call_target="tpu_custom_call" | custom-call | flops 100000000 | bytes 6000000 | tf_op jit(solution)/shard_map/far/far_own/pallas_call | solution.py:199
  96.8 0.0 collective-permute-done.2.low_b
  96.8 0.0 collective-permute-done.3.high_a
  96.8 2.0 %collective-permute-done.5.high_b = bf16[56,32,128]{2,1,0:T(8,128)(2,1)S(1)} collective-permute-done((bf16[56,32,128]{2,1,0:T(8,128)(2,1)}, bf16[56,32,128]{2,1,0:T(8,128)(2,1)S(1)}, u32[]{:S(2)}, u32[]{:S(2)}) %collective-permute-start.5) | collective-permute-done | bytes 458784 | tf_op jit(solution)/shard_map/far/ppermute | solution.py:258
  98.8 5.8 %collective-permute-done.1.low_a = bf16[56,32,128]{2,1,0:T(8,128)(2,1)S(1)} collective-permute-done((bf16[56,32,128]{2,1,0:T(8,128)(2,1)}, bf16[56,32,128]{2,1,0:T(8,128)(2,1)S(1)}, u32[]{:S(2)}, u32[]{:S(2)}) %collective-permute-start.1) | collective-permute-done | bytes 458784 | tf_op jit(solution)/shard_map/far/ppermute | solution.py:255
  104.6 2.4 %finish.1 = f32[112,64,64]{2,1,0:T(8,128)} custom-call(f32[112,32,128]{2,1,0:T(8,128)S(1)} %far_own.1.own, bf16[56,32,128]{2,1,0:T(8,128)(2,1)S(1)} %collective-permute-done.1.low_a, bf16[56,32,128]{2,1,0:T(8,128)(2,1)S(1)} %collective-permute-done.2.low_b, bf16[56,32,128]{2,1,0:T(8,128)(2,1)S(1)} %collective-permute-done.3.high_a, ...), custom_call_target="tpu_custom_call" | custom-call | tf_op jit(solution)/shard_map/finish/finish/pallas_call | solution.py:227
Async XLA Ops:
  0.0 17.7 %copy-start.9 = (s32[128,3]{0,1:T(4,128)S(1)}, s32[128,3]{0,1:T(4,128)}, u32[]{:S(2)}) copy-start(s32[128,3]{0,1:T(4,128)} %param.10) | copy-start | bytes 4612
  0.0 17.7 %copy-start.10 = (s32[128,4]{0,1:T(4,128)S(1)}, s32[128,4]{0,1:T(4,128)}, u32[]{:S(2)}) copy-start(s32[128,4]{0,1:T(4,128)} %param.13) | copy-start | bytes 6148
  0.0 17.7 %copy-start.11 = (s32[128]{0:T(128)S(1)}, s32[128]{0:T(128)}, u32[]{:S(2)}) copy-start(s32[128]{0:T(128)} %param.12) | copy-start | bytes 1540
  0.7 1.2 %copy-start.6 = (bf16[128,64,64]{0,2,1:T(8,128)(2,1)S(1)}, bf16[128,64,64]{0,2,1:T(8,128)(2,1)}, u32[]{:S(2)}) copy-start(bf16[128,64,64]{0,2,1:T(8,128)(2,1)} %param.9) | copy-start | bytes 3145732
  2.0 15.8 %copy-start.7 = (bf16[128,64,64]{0,2,1:T(8,128)(2,1)S(1)}, bf16[128,64,64]{0,2,1:T(8,128)(2,1)}, u32[]{:S(2)}) copy-start(bf16[128,64,64]{0,2,1:T(8,128)(2,1)} %param.9) | copy-start | bytes 3145732
  4.7 52.8 %all-to-all-start = ((bf16[64,96,128]{2,1,0:T(8,128)(2,1)}), bf16[64,96,128]{2,1,0:T(8,128)(2,1)S(1)}, u32[]{:S(2)}, u32[]{:S(2)}) async-start(bf16[64,96,128]{2,1,0:T(8,128)(2,1)} %bitcast.13), calls=%async_computation | async-start | bytes 3145728 | tf_op jit(solution)/shard_map/exchange/all_to_all | solution.py:243
  17.7 1.2 %copy-start.8 = (bf16[128,64,64]{0,2,1:T(8,128)(2,1)S(1)}, bf16[128,64,64]{0,2,1:T(8,128)(2,1)}, u32[]{:S(2)}) copy-start(bf16[128,64,64]{0,2,1:T(8,128)(2,1)} %param.8) | copy-start | bytes 3145732
  57.5 3.1 %copy-start = (f32[448,32,128]{2,1,0:T(8,128)S(1)}, f32[448,32,128]{2,1,0:T(8,128)}, u32[]{:S(2)}) copy-start(f32[448,32,128]{2,1,0:T(8,128)} %get-tuple-element.20) | copy-start | bytes 22020100
  60.6 2.8 %copy-start.3 = (bf16[4,96,64,128]{3,2,1,0:T(8,128)(2,1)S(1)}, bf16[4,96,64,128]{3,2,1,0:T(8,128)(2,1)}, u32[]{:S(2)}) copy-start(bf16[4,96,64,128]{3,2,1,0:T(8,128)(2,1)} %get-tuple-element.19.pairs) | copy-start | bytes 18874372
  65.4 16.9 %collective-permute-start.4 = (bf16[56,32,128]{2,1,0:T(8,128)(2,1)S(1)}, bf16[56,32,128]{2,1,0:T(8,128)(2,1)}, u32[]{:S(2)}, u32[]{:S(2)}) collective-permute-start(bf16[56,32,128]{2,1,0:T(8,128)(2,1)S(1)} %get-tuple-element.26), channel_id=1, source_target_pairs={{0,192},{64,0},{128,64},{192,128},{1,193},{65,1},{129,65},{193,129... | collective-permute-start | bytes 1376264 | tf_op jit(solution)/shard_map/far/ppermute | solution.py:258
  68.2 18.7 %collective-permute-start = (bf16[56,32,128]{2,1,0:T(8,128)(2,1)S(1)}, bf16[56,32,128]{2,1,0:T(8,128)(2,1)}, u32[]{:S(2)}, u32[]{:S(2)}) collective-permute-start(bf16[56,32,128]{2,1,0:T(8,128)(2,1)S(1)} %get-tuple-element.22), channel_id=1, source_target_pairs={{0,64},{64,128},{128,192},{192,0},{1,65},{65,129},{129,193},{193,1... | collective-permute-start | bytes 1376264 | tf_op jit(solution)/shard_map/far/ppermute | solution.py:255
  68.2 3.1 %copy-start.1 = (f32[448,32,128]{2,1,0:T(8,128)S(1)}, f32[448,32,128]{2,1,0:T(8,128)}, u32[]{:S(2)}) copy-start(f32[448,32,128]{2,1,0:T(8,128)} %get-tuple-element.20) | copy-start | bytes 22020100
  71.3 2.8 %copy-start.4 = (bf16[4,96,64,128]{3,2,1,0:T(8,128)(2,1)S(1)}, bf16[4,96,64,128]{3,2,1,0:T(8,128)(2,1)}, u32[]{:S(2)}) copy-start(bf16[4,96,64,128]{3,2,1,0:T(8,128)(2,1)} %get-tuple-element.19.pairs) | copy-start | bytes 18874372
  76.9 19.9 %collective-permute-start.2 = (bf16[56,32,128]{2,1,0:T(8,128)(2,1)}, bf16[56,32,128]{2,1,0:T(8,128)(2,1)S(1)}, u32[]{:S(2)}, u32[]{:S(2)}) collective-permute-start(bf16[56,32,128]{2,1,0:T(8,128)(2,1)} %get-tuple-element.23), channel_id=1, source_target_pairs={{0,192},{64,0},{128,64},{192,128},{1,193},{65,1},{129,65},{193,129... | collective-permute-start | bytes 1376264 | tf_op jit(solution)/shard_map/far/ppermute | solution.py:258
  82.3 14.5 %collective-permute-start.3 = (bf16[56,32,128]{2,1,0:T(8,128)(2,1)}, bf16[56,32,128]{2,1,0:T(8,128)(2,1)S(1)}, u32[]{:S(2)}, u32[]{:S(2)}) collective-permute-start(bf16[56,32,128]{2,1,0:T(8,128)(2,1)} %get-tuple-element.24), channel_id=1, source_target_pairs={{0,64},{64,128},{128,192},{192,0},{1,65},{65,129},{129,193},{193,1... | collective-permute-start | bytes 1376264 | tf_op jit(solution)/shard_map/far/ppermute | solution.py:255
  84.2 14.6 %collective-permute-start.5 = (bf16[56,32,128]{2,1,0:T(8,128)(2,1)}, bf16[56,32,128]{2,1,0:T(8,128)(2,1)S(1)}, u32[]{:S(2)}, u32[]{:S(2)}) collective-permute-start(bf16[56,32,128]{2,1,0:T(8,128)(2,1)} %add_convert_fusion), channel_id=1, source_target_pairs={{0,192},{64,0},{128,64},{192,128},{1,193},{65,1},{129,65},{193,129... | collective-permute-start | bytes 1376264 | tf_op jit(solution)/shard_map/far/ppermute | solution.py:258
  88.8 15.7 %collective-permute-start.1 = (bf16[56,32,128]{2,1,0:T(8,128)(2,1)}, bf16[56,32,128]{2,1,0:T(8,128)(2,1)S(1)}, u32[]{:S(2)}, u32[]{:S(2)}) collective-permute-start(bf16[56,32,128]{2,1,0:T(8,128)(2,1)} %add_convert_fusion.1), channel_id=1, source_target_pairs={{0,64},{64,128},{128,192},{192,0},{1,65},{65,129},{129,193},{193,1... | collective-permute-start | bytes 1376264 | tf_op jit(solution)/shard_map/far/ppermute | solution.py:255
  88.8 3.1 %copy-start.2 = (f32[448,32,128]{2,1,0:T(8,128)S(1)}, f32[448,32,128]{2,1,0:T(8,128)}, u32[]{:S(2)}) copy-start(f32[448,32,128]{2,1,0:T(8,128)} %get-tuple-element.20) | copy-start | bytes 22020100
  91.9 2.8 %copy-start.5 = (bf16[4,96,64,128]{3,2,1,0:T(8,128)(2,1)S(1)}, bf16[4,96,64,128]{3,2,1,0:T(8,128)(2,1)}, u32[]{:S(2)}) copy-start(bf16[4,96,64,128]{3,2,1,0:T(8,128)(2,1)} %get-tuple-element.19.pairs) | copy-start | bytes 18874372

commit v2 on v1

v2 whole, which is shorter than its diff:
```python
import functools

import jax
import jax.numpy as jnp
from jax import lax
from jax.experimental import pallas as pl
from jax.experimental.pallas import tpu as pltpu
from jax.sharding import PartitionSpec as P

MB = 1 << 20
F32 = jnp.float32
BF16 = jnp.bfloat16
VM = pltpu.VMEM
SM = pltpu.SMEM
HBM = pltpu.HBM

E = 128
SPAN = 32
ROWS = 16
SLOTS = 7
BLOCKS = ROWS * SLOTS
HALF = BLOCKS // 2
FAR = 192
CAP = 3 * SPAN
GROUP = 32
GROUPS = CAP // GROUP
AREA = CAP + GROUP
SUMS = 4 * AREA
COUNTS = 8 * AREA
AHEAD = (2, 1, 3, 0)


def rows_at(index, size):
    return pl.ds(pl.multiple_of(index * size, size), size)


def transpose_slabs(slab_of, steps, stride, wide, first=0):
    @pl.loop(0, steps, unroll=8)
    def _(i):
        wide[pl.ds(first + i, E, stride=stride), :] = slab_of(i).astype(F32).T


def send_kernel(rows, p_ref, out_ref, rows_here, blocks, packed, wide, arrived):
    rows_copy = pltpu.make_async_copy(rows, rows_here, arrived.at[4])
    rows_copy.start()
    copies = [
        pltpu.make_async_copy(p_ref.at[:, pl.ds(c * 8, 8)], blocks.at[c], arrived.at[c]) for c in range(4)
    ]
    for copy in copies:
        copy.start()
    for c in range(4):
        copies[c].wait()
        transpose_slabs(lambda i: blocks[c, :, i].reshape(128, E), 8, 40, wide, c * 8)
    packed[...] = wide[...].reshape(E, 40, 128)[:, :32].astype(BF16)
    rows_copy.wait()

    @pl.loop(0, 64, unroll=4)
    def _(peer):
        for s in range(3):
            out_ref[peer * 3 + s] = packed[rows_here[s, 0, peer]]


def send_blocks(rows, p_t):
    return pl.pallas_call(
        send_kernel,
        out_shape=jax.ShapeDtypeStruct((FAR, 32, 128), BF16),
        in_specs=[pl.BlockSpec(memory_space=HBM)] * 2,
        out_specs=pl.BlockSpec(memory_space=VM),
        scratch_shapes=[
            SM((3, 1, 64), jnp.int32),
            VM((4, 2, 8, 64, E), BF16),
            VM((E, 32, 128), BF16),
            VM((E * 40, 128), F32),
            pltpu.SemaphoreType.DMA((5,)),
        ],
        compiler_params=pltpu.CompilerParams(vmem_limit_bytes=63 * MB),
        name="send_blocks",
    )(rows, p_t)


def term_of(pair, doubled):
    applied = jnp.dot(pair[:, :64], doubled, preferred_element_type=F32).astype(BF16)
    term = jnp.dot(pair[:, 64:], applied, preferred_element_type=F32)
    low = lax.broadcasted_iota(jnp.int32, (32, 128), 1) < 64
    return jnp.where(low, term[:32], term[32:])


def near_kernel(me, neighbours, slot, parent, a_ref, r_ref, p_ref, *refs):
    far_pairs_out, sums_out, plan, pairs, doubled, wide, far_pairs, sums = refs[:8]
    near_pairs, near_blocks, near_sums, far_list, written = refs[8:]
    copies = []

    def two(i):
        block = p_ref[rows_at(i, 64), :]
        return jnp.concatenate([block, block], 0)

    transpose_slabs(two, 64, 72, wide)
    doubled[...] = wide[...].reshape(E, 72, 128)[:, :64].astype(BF16)

    @pl.loop(0, 4)
    def _(k):
        transpose_slabs(
            lambda i: jnp.concatenate([a_ref[rows_at(k * 64 + i, 64), :], r_ref[rows_at(i, 64), :]], 0), 64, 72, wide
        )
        pairs[rows_at(k, E)] = wide[...].reshape(E, 72, 128)[:, :64].astype(BF16)

    pairs[4 * E] = jnp.zeros((64, 128), BF16)

    for part, ahead in enumerate(AHEAD):
        first = lax.rem(me[0] + ahead, 4) * SPAN
        start = part * AREA

        def element(i, carry):
            near, far = carry
            e = first + i
            base = lax.rem(parent[0, e], ROWS) * SLOTS
            near_pairs[near] = e
            near_blocks[near] = e
            near_sums[near] = base + slot[0, e]
            near = near + 1
            for k in range(1, 4):
                code = neighbours[k - 1, e]
                block_sum = base + slot[k, e]
                near_pairs[near] = k * E + e
                near_blocks[near] = code
                near_sums[near] = block_sum
                far_list[far] = k * E + e
                plan[far] = code - E
                plan[SUMS + far] = block_sum
                here = (code < E).astype(jnp.int32)
                near = near + here
                far = far + (1 - here)
            return near, far

        near, far = lax.fori_loop(0, SPAN, element, (0, start))
        many = far - start
        plan[COUNTS + part] = many

        def keep(i, carry):
            far_pairs[part, i] = pairs[far_list[start + i]]
            return carry

        lax.fori_loop(0, many, keep, 0)

        def pad_far(i, carry):
            far_pairs[part, i] = jnp.zeros((64, 128), BF16)
            plan[start + i] = 0
            plan[SUMS + start + i] = 0
            return carry

        lax.fori_loop(many, (many + GROUP - 1) // GROUP * GROUP, pad_far, 0)

        def pad_near(i, carry):
            near_pairs[i] = 4 * E
            near_blocks[i] = 0
            near_sums[i] = 0
            return carry

        copies.append(pltpu.make_async_copy(far_pairs.at[part], far_pairs_out.at[part], written.at[part]))
        copies[-1].start()
        groups = (near + GROUP - 1) // GROUP
        lax.fori_loop(near, groups * GROUP, pad_near, 0)
        sums[part] = jnp.zeros((BLOCKS, 32, 128), F32)

        def group(g, carry):
            at = g * GROUP
            found = [term_of(pairs[near_pairs[at + u]], doubled[near_blocks[at + u]]) for u in range(GROUP)]
            for u in range(GROUP):
                sums[part, near_sums[at + u]] += found[u]
            return carry

        lax.fori_loop(0, groups, group, 0)
        copies.append(pltpu.make_async_copy(sums.at[part], sums_out.at[part], written.at[4 + part]))
        copies[-1].start()

    for copy in copies:
        copy.wait()


def near_terms(me, neighbours, slot, parent, a_t, r_t, p_t):
    return pl.pallas_call(
        near_kernel,
        out_shape=[
            jax.ShapeDtypeStruct((4, CAP, 64, 128), BF16),
            jax.ShapeDtypeStruct((4, BLOCKS, 32, 128), F32),
        ]
        + [jax.ShapeDtypeStruct((COUNTS + 8,), jnp.int32)],
        in_specs=[pl.BlockSpec(memory_space=SM)] * 4 + [pl.BlockSpec(memory_space=VM)] * 3,
        out_specs=[pl.BlockSpec(memory_space=HBM)] * 2 + [pl.BlockSpec(memory_space=SM)],
        scratch_shapes=[
            VM((4 * E + 1, 64, 128), BF16),
            VM((E, 64, 128), BF16),
            VM((E * 72, 128), F32),
            VM((4, CAP, 64, 128), BF16),
            VM((4, BLOCKS, 32, 128), F32),
            SM((4 * SPAN + GROUP,), jnp.int32),
            SM((4 * SPAN + GROUP,), jnp.int32),
            SM((4 * SPAN + GROUP,), jnp.int32),
            SM((4 * AREA,), jnp.int32),
            pltpu.SemaphoreType.DMA((8,)),
        ],
        compiler_params=pltpu.CompilerParams(vmem_limit_bytes=55 * MB),
        cost_estimate=pl.CostEstimate(flops=700_000_000, bytes_accessed=40_000_000, transcendentals=0),
        name="near_terms",
    )(me, neighbours, slot, parent, a_t, r_t, p_t)


def far_kernel(parts, kinds, plan, incoming, *refs):
    pairs_in, near_in, *outs = refs[:-4]
    pairs, near, sums, arrived = refs[-4:]
    low = lax.broadcasted_iota(jnp.int32, (32, 128), 1) < 64

    def pairs_copy(n, g):
        some = pl.ds(g * GROUP, GROUP)
        return pltpu.make_async_copy(pairs_in.at[parts[n], some], pairs.at[n, some], arrived.at[n, g])

    def near_copy(n):
        return pltpu.make_async_copy(near_in.at[parts[n]], near.at[n], arrived.at[n, GROUPS])

    def doubled(block):
        x = incoming[block]
        turned = jnp.concatenate([x[:, 64:], x[:, :64]], 1)
        return jnp.concatenate([jnp.where(low, x, turned), jnp.where(low, turned, x)], 0)

    for n, part in enumerate(parts):
        for g in range(GROUPS):

            @pl.when(plan[COUNTS + part] > g * GROUP)
            def _(n=n, g=g):
                pairs_copy(n, g).start()

        near_copy(n).start()

    for n, part in enumerate(parts):
        sums[...] = jnp.zeros_like(sums)
        start = part * AREA
        groups = (plan[COUNTS + part] + GROUP - 1) // GROUP

        def group(g, carry):
            at = g * GROUP
            pairs_copy(n, g).wait()
            found = [term_of(pairs[n, at + u], doubled(plan[start + at + u])) for u in range(GROUP)]
            for u in range(GROUP):
                sums[plan[SUMS + start + at + u]] += found[u]
            return carry

        lax.fori_loop(0, groups, group, 0)
        near_copy(n).wait()
        size = BLOCKS // len(kinds[n])
        for h, kind in enumerate(kinds[n]):
            some = pl.ds(h * size, size)
            outs[2 * n + h][...] = (near[n, some] + sums[some]).astype(kind)


def far_terms(parts, kinds, plan, incoming, pairs, near, name):
    shapes = [(BLOCKS // len(some), kind) for some in kinds for kind in some]
    return pl.pallas_call(
        functools.partial(far_kernel, parts, kinds),
        in_specs=[pl.BlockSpec(memory_space=SM), pl.BlockSpec(memory_space=VM)]
        + [pl.BlockSpec(memory_space=HBM)] * 2,
        out_specs=[pl.BlockSpec(memory_space=VM)] * len(shapes),
        scratch_shapes=[
            VM((len(parts), CAP, 64, 128), BF16),
            VM((len(parts), BLOCKS, 32, 128), F32),
            VM((BLOCKS, 32, 128), F32),
            pltpu.SemaphoreType.DMA((len(parts), GROUPS + 1)),
        ],
        out_shape=[jax.ShapeDtypeStruct((size, 32, 128), kind) for size, kind in shapes],
        compiler_params=pltpu.CompilerParams(vmem_limit_bytes=48 * MB),
        cost_estimate=pl.CostEstimate(flops=100_000_000, bytes_accessed=6_000_000, transcendentals=0),
        name=name,
    )(plan, incoming, pairs, near)


def add_kernel(here_a, passed_a, here_b, passed_b, out_a, out_b):
    out_a[...] = (here_a[...] + passed_a[...].astype(F32)).astype(BF16)
    out_b[...] = (here_b[...] + passed_b[...].astype(F32)).astype(BF16)


def add_passed(*parts):
    return pl.pallas_call(
        add_kernel,
        out_shape=[jax.ShapeDtypeStruct((HALF, 32, 128), BF16)] * 2,
        in_specs=[pl.BlockSpec(memory_space=VM)] * 4,
        out_specs=[pl.BlockSpec(memory_space=VM)] * 2,
        compiler_params=pltpu.CompilerParams(vmem_limit_bytes=16 * MB),
        name="add_passed",
    )(*parts)


def finish_kernel(own, low_a, low_b, high_a, high_b, out_ref):
    for h, (one, other) in enumerate(((low_a, low_b), (high_a, high_b))):
        total = own[h * HALF : (h + 1) * HALF] + one[...].astype(F32) + other[...].astype(F32)
        out_ref[h * HALF : (h + 1) * HALF, :32] = total[:, :, :64]
        out_ref[h * HALF : (h + 1) * HALF, 32:] = total[:, :, 64:]


def finish(*parts):
    return pl.pallas_call(
        finish_kernel,
        out_shape=jax.ShapeDtypeStruct((BLOCKS, 64, 64), F32),
        in_specs=[pl.BlockSpec(memory_space=VM)] * 5,
        out_specs=pl.BlockSpec(memory_space=VM),
        compiler_params=pltpu.CompilerParams(vmem_limit_bytes=24 * MB),
        name="finish",
    )(*parts)


def on_device(a_blocks, r_blocks, p_blocks, neighbours, send_rows, parent, slot):
    a_t = jnp.transpose(a_blocks, (1, 2, 3, 0)).reshape(4 * 4096, E)
    r_t = jnp.transpose(r_blocks, (1, 2, 0)).reshape(4096, E)
    p_t = jnp.transpose(p_blocks, (1, 2, 0))
    me = lax.axis_index("grp").astype(jnp.int32).reshape(1)
    with jax.named_scope("exchange"):
        outgoing = send_blocks(jnp.transpose(send_rows, (2, 0, 1)), p_t.reshape(2, 32, 64, E))
        incoming = lax.all_to_all(outgoing.reshape(64, 96, 128), "dev", 0, 0, tiled=True).reshape(FAR, 32, 128)
    with jax.named_scope("near"):
        pairs, near, plan = near_terms(
            me, neighbours.T, slot.T, parent.reshape(1, E), a_t, r_t, p_t.reshape(4096, E)
        )

    def to_next(x):
        return lax.ppermute(x, "grp", [(i, (i + 1) % 4) for i in range(4)])

    def to_last(x):
        return lax.ppermute(x, "grp", [(i, (i + 3) % 4) for i in range(4)])

    with jax.named_scope("far"):
        far_low, far_high = far_terms((0,), ((BF16, BF16),), plan, incoming, pairs, near, "far_two")
        passed_low, passed_high = to_next(far_low), to_last(far_high)
        next_low, next_high, last_low, last_high = far_terms(
            (1, 2), ((F32, BF16), (BF16, F32)), plan, incoming, pairs, near, "far_one"
        )
        from_last_high, from_next_low = to_next(next_high), to_last(last_low)
        both_low, both_high = add_passed(next_low, passed_low, last_high, passed_high)
        from_last_low, from_next_high = to_next(both_low), to_last(both_high)
        (own,) = far_terms((3,), ((F32,),), plan, incoming, pairs, near, "far_own")
    with jax.named_scope("finish"):
        coarse = finish(own, from_last_low, from_next_low, from_last_high, from_next_high)
    return coarse.reshape(ROWS, SLOTS, 64, 64)


def solution(mesh):
    return jax.shard_map(
        on_device,
        mesh=mesh,
        in_specs=(
            P(("grp", "dev"), None, None, None),
            P(("grp", "dev"), None, None),
            P(("grp", "dev"), None, None),
            P(("grp", "dev"), None),
            P(("grp", "dev"), None, None),
            P(("grp", "dev")),
            P(("grp", "dev"), None),
        ),
        out_specs=P(("grp", "dev"), None, None, None),
        check_vma=False,
    )
```

time: 108 us -> 95.5 us (0.88)
  local copies, waits for them, and re-layouts: 20.8 us -> 0.7 us
  waiting for transfers between devices: 20.7 us -> 33.1 us
  other arithmetic: 3.87 us -> 0 us
    unnamed x25 -> x2, local copies, waits for them, and re-layouts: 20.8 us -> 0.7 us
    ppermute x3, waiting for transfers between devices: 5.76 us -> 14.6 us  [to_next(): return lax.ppermute(x, 'grp', [(i, (i + 1) % 4) for i in range(4)])]
    convert_element_type x2 -> x0, other arithmetic: 3.87 us -> none  [the longest x1 1.95 us: on_device(): from_next_high = to_last((last_high + passed_high.astype(F32)).astype(BF16))]
    ppermute x3, starting transfers between devices: 8.15 us -> 4.73 us  [to_last(): return lax.ppermute(x, 'grp', [(i, (i + 3) % 4) for i in range(4)])]
    ppermute x3, starting transfers between devices: 0.01 us -> 2.46 us  [to_next(): return lax.ppermute(x, 'grp', [(i, (i + 1) % 4) for i in range(4)])]
    all_to_all x1, waiting for transfers between devices: 12.9 us -> 15.1 us  [on_device(): lax.all_to_all(outgoing.reshape(64, 96, 128), 'dev', 0, 0, tiled=True)]
    ppermute x3, waiting for transfers between devices: 2 us -> 3.48 us  [to_last(): return lax.ppermute(x, 'grp', [(i, (i + 3) % 4) for i in range(4)])]
    pallas_call x4, Pallas kernels: 9.63 us -> 10.8 us  [the longest x3 10.7 us: far_terms(): pl.pallas_call(functools.partial(far_kernel, parts, kinds), in_specs=[pl....]
  transfers between devices with their start and end apart: 7 -> 7, of which waited for: 3 -> 5; matrix products, arithmetic and copies ran while one was open for 4% -> 0% of each run, Pallas kernels for 31% -> 34%
where the time goes in v2:
time: 95.5 us; the launch traced here: 95.2 us
  Pallas kernels  41.1 us (43%)
  waiting for transfers between devices  33.1 us (35%)
  starting transfers between devices  20.2 us (21%)
    pallas_call x1, Pallas kernels, near_terms(): pl.pallas_call(near_kernel, out_shape=[jax.ShapeDtypeStruct((4, CAP, 64,...  24.7 us
    all_to_all x1, waiting for transfers between devices, on_device(): lax.all_to_all(outgoing.reshape(64, 96, 128), 'dev', 0, 0, tiled=True)  15.1 us
    ppermute x3, waiting for transfers between devices, to_next(): return lax.ppermute(x, 'grp', [(i, (i + 1) % 4) for i in range(4)])  14.6 us
    all_to_all x1, starting transfers between devices, on_device(): lax.all_to_all(outgoing.reshape(64, 96, 128), 'dev', 0, 0, tiled=True)  13 us
    pallas_call x3, Pallas kernels, far_terms(): pl.pallas_call(functools.partial(far_kernel, parts, kinds), in_specs=[pl....  10.7 us
    ppermute x3, starting transfers between devices, to_last(): return lax.ppermute(x, 'grp', [(i, (i + 3) % 4) for i in range(4)])  4.73 us
    ppermute x3, waiting for transfers between devices, to_last(): return lax.ppermute(x, 'grp', [(i, (i + 3) % 4) for i in range(4)])  3.48 us
    pallas_call x1, Pallas kernels, send_blocks(): pl.pallas_call(send_kernel, out_shape=jax.ShapeDtypeStruct((FAR, 32, 128)...  3.16 us
  transfers between devices with their start and end apart: 7, of which 5 were waited for; matrix products, arithmetic and copies ran while one was open for 0% of the time, Pallas kernels for 34%

profile of v2, /device:TPU:1, one launch (start us, length us, event | category | flops | bytes accessed | tf_op | source)
XLA Modules:
  0.0 95.2 jit_solution(430970283268726790)
XLA Ops:
  0.0 3.2 %send_blocks.1 = bf16[192,32,128]{2,1,0:T(8,128)(2,1)} custom-call(s32[3,1,64]{2,1,0:T(1,128)} %bitcast.29, bf16[2,32,64,128]{3,2,1,0:T(8,128)(2,1)} %bitcast.24), custom_call_target="tpu_custom_call" | custom-call | tf_op jit(solution)/shard_map/exchange/send_blocks/pallas_call | solution.py:64
  3.2 13.0 %all-to-all-start = ((bf16[64,96,128]{2,1,0:T(8,128)(2,1)}), bf16[64,96,128]{2,1,0:T(8,128)(2,1)S(1)}, u32[]{:S(2)}, u32[]{:S(2)}) async-start(bf16[64,96,128]{2,1,0:T(8,128)(2,1)} %bitcast.22), calls=%async_computation | async-start | bytes 3145728 | tf_op jit(solution)/shard_map/exchange/all_to_all | solution.py:316
  16.2 24.7 %near_terms.1 = (bf16[4,96,64,128]{3,2,1,0:T(8,128)(2,1)}, f32[4,112,32,128]{3,2,1,0:T(8,128)}, s32[1032]{0:T(1024)}) custom-call(s32[1]{0:T(128)} %bitcast.me, s32[3,128]{1,0:T(4,128)} %bitcast.27, s32[4,128]{1,0:T(4,128)} %bitcast.28, s32[1,128]{1,0:T(1,128)} %bitcast.30, bf16[16384,128]{1,0:T(8,128)(2,1)} %bitcast.23, bf16[4096,128]{1,0:T(8,128)(2,1)} %bitcast.26, ...), custom_call_target="tpu_custom_call" | custom-call | flops 700000000 | bytes 40000000 | tf_op jit(solution)/shard_map/near/near_terms/pallas_call | solution.py:181
  40.9 15.1 %all-to-all-done = bf16[64,96,128]{2,1,0:T(8,128)(2,1)S(1)} async-done(((bf16[64,96,128]{2,1,0:T(8,128)(2,1)}), bf16[64,96,128]{2,1,0:T(8,128)(2,1)S(1)}, u32[]{:S(2)}, u32[]{:S(2)}) %all-to-all-start) | async-done | bytes 1572896 | tf_op jit(solution)/shard_map/exchange/all_to_all | solution.py:316
  56.0 0.0 copy-start
  56.0 0.7 copy-done
  56.7 3.1 %far_two.1 = (bf16[56,32,128]{2,1,0:T(8,128)(2,1)S(1)}, bf16[56,32,128]{2,1,0:T(8,128)(2,1)S(1)}) custom-call(s32[1032]{0:T(1024)S(1)} %copy-done, bf16[192,32,128]{2,1,0:T(8,128)(2,1)S(1)} %bitcast.19, bf16[4,96,64,128]{3,2,1,0:T(8,128)(2,1)} %get-tuple-element.17.refs_0_, f32[4,112,32,128]{3,2,1,0:T(8,128)} %get-tuple-element.18.refs_1_), custom_call_target="tpu_custom_call" | custom-call | flops 100000000 | bytes 6000000 | tf_op jit(solution)/shard_map/far/far_two/pallas_call | solution.py:257
  59.7 1.4 %collective-permute-start = (bf16[56,32,128]{2,1,0:T(8,128)(2,1)S(1)}, bf16[56,32,128]{2,1,0:T(8,128)(2,1)S(1)}, u32[]{:S(2)}, u32[]{:S(2)}) collective-permute-start(bf16[56,32,128]{2,1,0:T(8,128)(2,1)S(1)} %get-tuple-element.20), channel_id=1, source_target_pairs={{0,64},{64,128},{128,192},{192,0},{1,65},{65,129},{129,193},{193,1... | collective-permute-start | bytes 1376264 | tf_op jit(solution)/shard_map/far/ppermute | solution.py:323
  61.1 1.5 %collective-permute-start.1 = (bf16[56,32,128]{2,1,0:T(8,128)(2,1)S(1)}, bf16[56,32,128]{2,1,0:T(8,128)(2,1)S(1)}, u32[]{:S(2)}, u32[]{:S(2)}) collective-permute-start(bf16[56,32,128]{2,1,0:T(8,128)(2,1)S(1)} %get-tuple-element.22), channel_id=1, source_target_pairs={{0,192},{64,0},{128,64},{192,128},{1,193},{65,1},{129,65},{193,129... | collective-permute-start | bytes 1376264 | tf_op jit(solution)/shard_map/far/ppermute | solution.py:326
  62.6 4.6 %far_one.1 = (f32[56,32,128]{2,1,0:T(8,128)S(1)}, bf16[56,32,128]{2,1,0:T(8,128)(2,1)S(1)}, bf16[56,32,128]{2,1,0:T(8,128)(2,1)S(1)}, f32[56,32,128]{2,1,0:T(8,128)S(1)}) custom-call(s32[1032]{0:T(1024)S(1)} %copy-done, bf16[192,32,128]{2,1,0:T(8,128)(2,1)S(1)} %bitcast.20, bf16[4,96,64,128]{3,2,1,0:T(8,128)(2,1)} %get-tuple-element.17.refs_0_, ...), custom_call_target="tpu_custom_call" | custom-call | flops 100000000 | bytes 6000000 | tf_op jit(solution)/shard_map/far/far_one/pallas_call | solution.py:257
  67.2 1.5 %collective-permute-start.3 = (bf16[56,32,128]{2,1,0:T(8,128)(2,1)S(1)}, bf16[56,32,128]{2,1,0:T(8,128)(2,1)S(1)}, u32[]{:S(2)}, u32[]{:S(2)}) collective-permute-start(bf16[56,32,128]{2,1,0:T(8,128)(2,1)S(1)} %get-tuple-element.24), channel_id=1, source_target_pairs={{0,192},{64,0},{128,64},{192,128},{1,193},{65,1},{129,65},{193,129... | collective-permute-start | bytes 1376264 | tf_op jit(solution)/shard_map/far/ppermute | solution.py:326
  68.7 0.1 collective-permute-start.4
  68.7 4.4 %collective-permute-done.passed_a = bf16[56,32,128]{2,1,0:T(8,128)(2,1)S(1)} collective-permute-done((bf16[56,32,128]{2,1,0:T(8,128)(2,1)S(1)}, bf16[56,32,128]{2,1,0:T(8,128)(2,1)S(1)}, u32[]{:S(2)}, u32[]{:S(2)}) %collective-permute-start) | collective-permute-done | bytes 458784 | tf_op jit(solution)/shard_map/far/ppermute | solution.py:323
  73.1 0.0 collective-permute-done.1.passed_b
  73.1 0.2 add_passed.1
  73.3 1.0 %collective-permute-start.2 = (bf16[56,32,128]{2,1,0:T(8,128)(2,1)S(1)}, bf16[56,32,128]{2,1,0:T(8,128)(2,1)S(1)}, u32[]{:S(2)}, u32[]{:S(2)}) collective-permute-start(bf16[56,32,128]{2,1,0:T(8,128)(2,1)S(1)} %get-tuple-element.23), channel_id=1, source_target_pairs={{0,64},{64,128},{128,192},{192,0},{1,65},{65,129},{129,193},{193,1... | collective-permute-start | bytes 1376264 | tf_op jit(solution)/shard_map/far/ppermute | solution.py:323
  74.3 1.8 %collective-permute-start.5 = (bf16[56,32,128]{2,1,0:T(8,128)(2,1)S(1)}, bf16[56,32,128]{2,1,0:T(8,128)(2,1)S(1)}, u32[]{:S(2)}, u32[]{:S(2)}) collective-permute-start(bf16[56,32,128]{2,1,0:T(8,128)(2,1)S(1)} %get-tuple-element.26), channel_id=1, source_target_pairs={{0,192},{64,0},{128,64},{192,128},{1,193},{65,1},{129,65},{193,129... | collective-permute-start | bytes 1376264 | tf_op jit(solution)/shard_map/far/ppermute | solution.py:326
  76.0 3.1 %far_own.1.own = f32[112,32,128]{2,1,0:T(8,128)S(1)} custom-call(s32[1032]{0:T(1024)S(1)} %copy-done, bf16[192,32,128]{2,1,0:T(8,128)(2,1)S(1)} %bitcast.21, bf16[4,96,64,128]{3,2,1,0:T(8,128)(2,1)} %get-tuple-element.17.refs_0_, f32[4,112,32,128]{3,2,1,0:T(8,128)} %get-tuple-element.18.refs_1_), custom_call_target="tpu_custom_call" | custom-call | flops 100000000 | bytes 6000000 | tf_op jit(solution)/shard_map/far/far_own/pallas_call | solution.py:257
  79.1 3.5 %collective-permute-done.3.low_b = bf16[56,32,128]{2,1,0:T(8,128)(2,1)S(1)} collective-permute-done((bf16[56,32,128]{2,1,0:T(8,128)(2,1)S(1)}, bf16[56,32,128]{2,1,0:T(8,128)(2,1)S(1)}, u32[]{:S(2)}, u32[]{:S(2)}) %collective-permute-start.3) | collective-permute-done | bytes 458784 | tf_op jit(solution)/shard_map/far/ppermute | solution.py:326
  82.6 0.4 collective-permute-done.4.high_a
  83.0 9.8 %collective-permute-done.2.low_a = bf16[56,32,128]{2,1,0:T(8,128)(2,1)S(1)} collective-permute-done((bf16[56,32,128]{2,1,0:T(8,128)(2,1)S(1)}, bf16[56,32,128]{2,1,0:T(8,128)(2,1)S(1)}, u32[]{:S(2)}, u32[]{:S(2)}) %collective-permute-start.2) | collective-permute-done | bytes 458784 | tf_op jit(solution)/shard_map/far/ppermute | solution.py:323
  92.8 0.0 collective-permute-done.5.high_b
  92.8 2.4 %finish.1 = f32[112,64,64]{2,1,0:T(8,128)} custom-call(f32[112,32,128]{2,1,0:T(8,128)S(1)} %far_own.1.own, bf16[56,32,128]{2,1,0:T(8,128)(2,1)S(1)} %collective-permute-done.2.low_a, bf16[56,32,128]{2,1,0:T(8,128)(2,1)S(1)} %collective-permute-done.3.low_b, bf16[56,32,128]{2,1,0:T(8,128)(2,1)S(1)} %collective-permute-done.4.high_a, ...), custom_call_target="tpu_custom_call" | custom-call | tf_op jit(solution)/shard_map/finish/finish/pallas_call | solution.py:299
Async XLA Ops:
  3.2 52.8 %all-to-all-start = ((bf16[64,96,128]{2,1,0:T(8,128)(2,1)}), bf16[64,96,128]{2,1,0:T(8,128)(2,1)S(1)}, u32[]{:S(2)}, u32[]{:S(2)}) async-start(bf16[64,96,128]{2,1,0:T(8,128)(2,1)} %bitcast.22), calls=%async_computation | async-start | bytes 3145728 | tf_op jit(solution)/shard_map/exchange/all_to_all | solution.py:316
  56.0 0.7 copy-start
  59.7 13.4 %collective-permute-start = (bf16[56,32,128]{2,1,0:T(8,128)(2,1)S(1)}, bf16[56,32,128]{2,1,0:T(8,128)(2,1)S(1)}, u32[]{:S(2)}, u32[]{:S(2)}) collective-permute-start(bf16[56,32,128]{2,1,0:T(8,128)(2,1)S(1)} %get-tuple-element.20), channel_id=1, source_target_pairs={{0,64},{64,128},{128,192},{192,0},{1,65},{65,129},{129,193},{193,1... | collective-permute-start | bytes 1376264 | tf_op jit(solution)/shard_map/far/ppermute | solution.py:323
  61.1 12.0 %collective-permute-start.1 = (bf16[56,32,128]{2,1,0:T(8,128)(2,1)S(1)}, bf16[56,32,128]{2,1,0:T(8,128)(2,1)S(1)}, u32[]{:S(2)}, u32[]{:S(2)}) collective-permute-start(bf16[56,32,128]{2,1,0:T(8,128)(2,1)S(1)} %get-tuple-element.22), channel_id=1, source_target_pairs={{0,192},{64,0},{128,64},{192,128},{1,193},{65,1},{129,65},{193,129... | collective-permute-start | bytes 1376264 | tf_op jit(solution)/shard_map/far/ppermute | solution.py:326
  67.2 15.4 %collective-permute-start.3 = (bf16[56,32,128]{2,1,0:T(8,128)(2,1)S(1)}, bf16[56,32,128]{2,1,0:T(8,128)(2,1)S(1)}, u32[]{:S(2)}, u32[]{:S(2)}) collective-permute-start(bf16[56,32,128]{2,1,0:T(8,128)(2,1)S(1)} %get-tuple-element.24), channel_id=1, source_target_pairs={{0,192},{64,0},{128,64},{192,128},{1,193},{65,1},{129,65},{193,129... | collective-permute-start | bytes 1376264 | tf_op jit(solution)/shard_map/far/ppermute | solution.py:326
  68.7 14.3 %collective-permute-start.4 = (bf16[56,32,128]{2,1,0:T(8,128)(2,1)S(1)}, bf16[56,32,128]{2,1,0:T(8,128)(2,1)S(1)}, u32[]{:S(2)}, u32[]{:S(2)}) collective-permute-start(bf16[56,32,128]{2,1,0:T(8,128)(2,1)S(1)} %get-tuple-element.25), channel_id=1, source_target_pairs={{0,64},{64,128},{128,192},{192,0},{1,65},{65,129},{129,193},{193,1... | collective-permute-start | bytes 1376264 | tf_op jit(solution)/shard_map/far/ppermute | solution.py:323
  73.3 19.5 %collective-permute-start.2 = (bf16[56,32,128]{2,1,0:T(8,128)(2,1)S(1)}, bf16[56,32,128]{2,1,0:T(8,128)(2,1)S(1)}, u32[]{:S(2)}, u32[]{:S(2)}) collective-permute-start(bf16[56,32,128]{2,1,0:T(8,128)(2,1)S(1)} %get-tuple-element.23), channel_id=1, source_target_pairs={{0,64},{64,128},{128,192},{192,0},{1,65},{65,129},{129,193},{193,1... | collective-permute-start | bytes 1376264 | tf_op jit(solution)/shard_map/far/ppermute | solution.py:323
  74.3 18.5 %collective-permute-start.5 = (bf16[56,32,128]{2,1,0:T(8,128)(2,1)S(1)}, bf16[56,32,128]{2,1,0:T(8,128)(2,1)S(1)}, u32[]{:S(2)}, u32[]{:S(2)}) collective-permute-start(bf16[56,32,128]{2,1,0:T(8,128)(2,1)S(1)} %get-tuple-element.26), channel_id=1, source_target_pairs={{0,192},{64,0},{128,64},{192,128},{1,193},{65,1},{129,65},{193,129... | collective-permute-start | bytes 1376264 | tf_op jit(solution)/shard_map/far/ppermute | solution.py:326

commit v3 on v2

--- a/solution.py
+++ b/solution.py
@@ -24,9 +24,12 @@
 CAP = 3 * SPAN
 GROUP = 32
 GROUPS = CAP // GROUP
+CHUNKS = 4
 AREA = CAP + GROUP
 SUMS = 4 * AREA
 COUNTS = 8 * AREA
+PLAN = COUNTS + 1024
+ROOM = 3 * MB
 AHEAD = (2, 1, 3, 0)
 
 
@@ -40,7 +43,7 @@
         wide[pl.ds(first + i, E, stride=stride), :] = slab_of(i).astype(F32).T
 
 
-def send_kernel(rows, p_ref, out_ref, rows_here, blocks, packed, wide, arrived):
+def send_kernel(rows, p_ref, out_ref, rows_here, blocks, packed, wide, outgoing, arrived, written):
     rows_copy = pltpu.make_async_copy(rows, rows_here, arrived.at[4])
     rows_copy.start()
     copies = [
@@ -54,10 +57,21 @@
     packed[...] = wide[...].reshape(E, 40, 128)[:, :32].astype(BF16)
     rows_copy.wait()
 
-    @pl.loop(0, 64, unroll=4)
-    def _(peer):
-        for s in range(3):
-            out_ref[peer * 3 + s] = packed[rows_here[s, 0, peer]]
+    copies = []
+    for c in range(CHUNKS):
+        size = FAR // CHUNKS
+
+        @pl.loop(0, 64 // CHUNKS, unroll=4)
+        def _(n):
+            peer = c * (64 // CHUNKS) + n
+            for s in range(3):
+                outgoing[peer * 3 + s] = packed[rows_here[s, 0, peer]]
+
+        some = pl.ds(c * size, size)
+        copies.append(pltpu.make_async_copy(outgoing.at[some], out_ref.at[some], written.at[c]))
+        copies[-1].start()
+    for copy in copies:
+        copy.wait()
 
 
 def send_blocks(rows, p_t):
@@ -65,13 +79,15 @@
         send_kernel,
         out_shape=jax.ShapeDtypeStruct((FAR, 32, 128), BF16),
         in_specs=[pl.BlockSpec(memory_space=HBM)] * 2,
-        out_specs=pl.BlockSpec(memory_space=VM),
+        out_specs=pl.BlockSpec(memory_space=HBM),
         scratch_shapes=[
             SM((3, 1, 64), jnp.int32),
             VM((4, 2, 8, 64, E), BF16),
             VM((E, 32, 128), BF16),
             VM((E * 40, 128), F32),
+            VM((FAR, 32, 128), BF16),
             pltpu.SemaphoreType.DMA((5,)),
+            pltpu.SemaphoreType.DMA((CHUNKS,)),
         ],
         compiler_params=pltpu.CompilerParams(vmem_limit_bytes=63 * MB),
         name="send_blocks",
@@ -86,8 +102,8 @@
 
 
 def near_kernel(me, neighbours, slot, parent, a_ref, r_ref, p_ref, *refs):
-    far_pairs_out, sums_out, plan, pairs, doubled, wide, far_pairs, sums = refs[:8]
-    near_pairs, near_blocks, near_sums, far_list, written = refs[8:]
+    far_pairs_out, sums_out, plan_out, pairs, doubled, wide, far_pairs, sums = refs[:8]
+    plan, near_pairs, near_blocks, near_sums, far_list, written = refs[8:]
     copies = []
 
     def two(i):
@@ -173,6 +189,8 @@
         copies.append(pltpu.make_async_copy(sums.at[part], sums_out.at[part], written.at[4 + part]))
         copies[-1].start()
 
+    copies.append(pltpu.make_async_copy(plan, plan_out.at[pl.ds(0, PLAN)], written.at[8]))
+    copies[-1].start()
     for copy in copies:
         copy.wait()
 
@@ -184,20 +202,21 @@
             jax.ShapeDtypeStruct((4, CAP, 64, 128), BF16),
             jax.ShapeDtypeStruct((4, BLOCKS, 32, 128), F32),
         ]
-        + [jax.ShapeDtypeStruct((COUNTS + 8,), jnp.int32)],
+        + [jax.ShapeDtypeStruct((ROOM,), jnp.int32)],
         in_specs=[pl.BlockSpec(memory_space=SM)] * 4 + [pl.BlockSpec(memory_space=VM)] * 3,
-        out_specs=[pl.BlockSpec(memory_space=HBM)] * 2 + [pl.BlockSpec(memory_space=SM)],
+        out_specs=[pl.BlockSpec(memory_space=HBM)] * 3,
         scratch_shapes=[
             VM((4 * E + 1, 64, 128), BF16),
             VM((E, 64, 128), BF16),
             VM((E * 72, 128), F32),
             VM((4, CAP, 64, 128), BF16),
             VM((4, BLOCKS, 32, 128), F32),
+            SM((PLAN,), jnp.int32),
             SM((4 * SPAN + GROUP,), jnp.int32),
             SM((4 * SPAN + GROUP,), jnp.int32),
             SM((4 * SPAN + GROUP,), jnp.int32),
             SM((4 * AREA,), jnp.int32),
-            pltpu.SemaphoreType.DMA((8,)),
+            pltpu.SemaphoreType.DMA((9,)),
         ],
         compiler_params=pltpu.CompilerParams(vmem_limit_bytes=55 * MB),
         cost_estimate=pl.CostEstimate(flops=700_000_000, bytes_accessed=40_000_000, transcendentals=0),
@@ -205,9 +224,11 @@
     )(me, neighbours, slot, parent, a_t, r_t, p_t)
 
 
-def far_kernel(parts, kinds, plan, incoming, *refs):
-    pairs_in, near_in, *outs = refs[:-4]
-    pairs, near, sums, arrived = refs[-4:]
+def far_kernel(parts, kinds, plan_in, incoming, *refs):
+    pairs_in, near_in, *outs = refs[:-6]
+    plan, pairs, near, sums, arrived, plan_arrived = refs[-6:]
+    plan_copy = pltpu.make_async_copy(plan_in.at[pl.ds(0, PLAN)], plan, plan_arrived)
+    plan_copy.start()
     low = lax.broadcasted_iota(jnp.int32, (32, 128), 1) < 64
 
     def pairs_copy(n, g):
@@ -222,14 +243,17 @@
         turned = jnp.concatenate([x[:, 64:], x[:, :64]], 1)
         return jnp.concatenate([jnp.where(low, x, turned), jnp.where(low, turned, x)], 0)
 
+    for n in range(len(parts)):
+        pairs_copy(n, 0).start()
+        near_copy(n).start()
+    plan_copy.wait()
     for n, part in enumerate(parts):
-        for g in range(GROUPS):
+        for g in range(1, GROUPS):
 
             @pl.when(plan[COUNTS + part] > g * GROUP)
             def _(n=n, g=g):
                 pairs_copy(n, g).start()
 
-        near_copy(n).start()
 
     for n, part in enumerate(parts):
         sums[...] = jnp.zeros_like(sums)
@@ -245,6 +269,11 @@
             return carry
 
         lax.fori_loop(0, groups, group, 0)
+
+        @pl.when(groups == 0)
+        def _(n=n):
+            pairs_copy(n, 0).wait()
+
         near_copy(n).wait()
         size = BLOCKS // len(kinds[n])
         for h, kind in enumerate(kinds[n]):
@@ -256,14 +285,16 @@
     shapes = [(BLOCKS // len(some), kind) for some in kinds for kind in some]
     return pl.pallas_call(
         functools.partial(far_kernel, parts, kinds),
-        in_specs=[pl.BlockSpec(memory_space=SM), pl.BlockSpec(memory_space=VM)]
+        in_specs=[pl.BlockSpec(memory_space=HBM), pl.BlockSpec(memory_space=VM)]
         + [pl.BlockSpec(memory_space=HBM)] * 2,
         out_specs=[pl.BlockSpec(memory_space=VM)] * len(shapes),
         scratch_shapes=[
+            SM((PLAN,), jnp.int32),
             VM((len(parts), CAP, 64, 128), BF16),
             VM((len(parts), BLOCKS, 32, 128), F32),
             VM((BLOCKS, 32, 128), F32),
             pltpu.SemaphoreType.DMA((len(parts), GROUPS + 1)),
+            pltpu.SemaphoreType.DMA,
         ],
         out_shape=[jax.ShapeDtypeStruct((size, 32, 128), kind) for size, kind in shapes],
         compiler_params=pltpu.CompilerParams(vmem_limit_bytes=48 * MB),
@@ -288,11 +319,20 @@
     )(*parts)
 
 
-def finish_kernel(own, low_a, low_b, high_a, high_b, out_ref):
-    for h, (one, other) in enumerate(((low_a, low_b), (high_a, high_b))):
-        total = own[h * HALF : (h + 1) * HALF] + one[...].astype(F32) + other[...].astype(F32)
-        out_ref[h * HALF : (h + 1) * HALF, :32] = total[:, :, :64]
-        out_ref[h * HALF : (h + 1) * HALF, 32:] = total[:, :, 64:]
+def finish_kernel(own, low_a, low_b, high_a, high_b, out_ref, totals, written):
+    copies = []
+    size = BLOCKS // CHUNKS
+    for c in range(CHUNKS):
+        one, other = ((low_a, low_b), (high_a, high_b))[c * 2 // CHUNKS]
+        some = pl.ds(c * size, size)
+        here = pl.ds(c * size % HALF, size)
+        total = own[some] + one[here].astype(F32) + other[here].astype(F32)
+        totals[some, :32] = total[:, :, :64]
+        totals[some, 32:] = total[:, :, 64:]
+        copies.append(pltpu.make_async_copy(totals.at[some], out_ref.at[some], written.at[c]))
+        copies[-1].start()
+    for copy in copies:
+        copy.wait()
 
 
 def finish(*parts):
@@ -300,7 +340,8 @@
         finish_kernel,
         out_shape=jax.ShapeDtypeStruct((BLOCKS, 64, 64), F32),
         in_specs=[pl.BlockSpec(memory_space=VM)] * 5,
-        out_specs=pl.BlockSpec(memory_space=VM),
+        out_specs=pl.BlockSpec(memory_space=HBM),
+        scratch_shapes=[VM((BLOCKS, 64, 64), F32), pltpu.SemaphoreType.DMA((CHUNKS,))],
         compiler_params=pltpu.CompilerParams(vmem_limit_bytes=24 * MB),
         name="finish",
     )(*parts)

time: 95.5 us -> 93.7 us (0.981)
  Pallas kernels: 41.1 us -> 40.1 us
  transfers between devices with their start and end apart: 7 -> 7, of which waited for: 5 -> 4; matrix products, arithmetic and copies ran while one was open for 0% -> 0% of each run, Pallas kernels for 34% -> 35%
where the time goes in v3:
time: 93.7 us; the launch traced here: 93.4 us
  Pallas kernels  40.1 us (43%)
  waiting for transfers between devices  33 us (35%)
  starting transfers between devices  20.2 us (22%)
    pallas_call x1, Pallas kernels, near_terms(): pl.pallas_call(near_kernel, out_shape=[jax.ShapeDtypeStruct((4, CAP, 64,...  24.1 us
    all_to_all x1, waiting for transfers between devices, on_device(): lax.all_to_all(outgoing.reshape(64, 96, 128), 'dev', 0, 0, tiled=True)  15.7 us
    ppermute x3, waiting for transfers between devices, to_next(): return lax.ppermute(x, 'grp', [(i, (i + 1) % 4) for i in range(4)])  13.8 us
    all_to_all x1, starting transfers between devices, on_device(): lax.all_to_all(outgoing.reshape(64, 96, 128), 'dev', 0, 0, tiled=True)  13 us
    pallas_call x3, Pallas kernels, far_terms(): pl.pallas_call(functools.partial(far_kernel, parts, kinds), in_specs=[pl....  10.9 us
    ppermute x3, starting transfers between devices, to_last(): return lax.ppermute(x, 'grp', [(i, (i + 3) % 4) for i in range(4)])  4.75 us
    ppermute x3, waiting for transfers between devices, to_last(): return lax.ppermute(x, 'grp', [(i, (i + 3) % 4) for i in range(4)])  3.6 us
    pallas_call x1, Pallas kernels, send_blocks(): pl.pallas_call(send_kernel, out_shape=jax.ShapeDtypeStruct((FAR, 32, 128)...  2.92 us
  transfers between devices with their start and end apart: 7, of which 4 were waited for; matrix products, arithmetic and copies ran while one was open for 0% of the time, Pallas kernels for 35%

profile of v3, /device:TPU:1, one launch (start us, length us, event | category | flops | bytes accessed | tf_op | source)
XLA Modules:
  0.0 93.4 jit_solution(14590914130550732584)
XLA Ops:
  0.0 2.9 %send_blocks.1 = bf16[192,32,128]{2,1,0:T(8,128)(2,1)} custom-call(s32[3,1,64]{2,1,0:T(1,128)} %bitcast.29, bf16[2,32,64,128]{3,2,1,0:T(8,128)(2,1)} %bitcast.24), custom_call_target="tpu_custom_call" | custom-call | tf_op jit(solution)/shard_map/exchange/send_blocks/pallas_call | solution.py:78
  2.9 13.0 %all-to-all-start = ((bf16[64,96,128]{2,1,0:T(8,128)(2,1)}), bf16[64,96,128]{2,1,0:T(8,128)(2,1)S(1)}, u32[]{:S(2)}, u32[]{:S(2)}) async-start(bf16[64,96,128]{2,1,0:T(8,128)(2,1)} %bitcast.22), calls=%async_computation | async-start | bytes 3145728 | tf_op jit(solution)/shard_map/exchange/all_to_all | solution.py:357
  15.9 24.1 %near_terms.1 = (bf16[4,96,64,128]{3,2,1,0:T(8,128)(2,1)}, f32[4,112,32,128]{3,2,1,0:T(8,128)}, s32[3145728]{0:T(1024)}) custom-call(s32[1]{0:T(128)} %bitcast.me, s32[3,128]{1,0:T(4,128)} %bitcast.27, s32[4,128]{1,0:T(4,128)} %bitcast.28, s32[1,128]{1,0:T(1,128)} %bitcast.30, bf16[16384,128]{1,0:T(8,128)(2,1)} %bitcast.23, bf16[4096,128]{1,0:T(8,128)(2,1)} %bitcast.26, ...), custom_call_target="tpu_custom_call" | custom-call | flops 700000000 | bytes 40000000 | tf_op jit(solution)/shard_map/near/near_terms/pallas_call | solution.py:199
  40.1 15.7 %all-to-all-done = bf16[64,96,128]{2,1,0:T(8,128)(2,1)S(1)} async-done(((bf16[64,96,128]{2,1,0:T(8,128)(2,1)}), bf16[64,96,128]{2,1,0:T(8,128)(2,1)S(1)}, u32[]{:S(2)}, u32[]{:S(2)}) %all-to-all-start) | async-done | bytes 1572896 | tf_op jit(solution)/shard_map/exchange/all_to_all | solution.py:357
  55.7 3.0 %far_two.1 = (bf16[56,32,128]{2,1,0:T(8,128)(2,1)S(1)}, bf16[56,32,128]{2,1,0:T(8,128)(2,1)S(1)}) custom-call(s32[3145728]{0:T(1024)} %get-tuple-element.16.plan_in, bf16[192,32,128]{2,1,0:T(8,128)(2,1)S(1)} %bitcast.19, bf16[4,96,64,128]{3,2,1,0:T(8,128)(2,1)} %get-tuple-element.17.refs_0_, f32[4,112,32,128]{3,2,1,0:T(8,128)} %get-tuple-element.18.refs_1_), custom_call_target="tpu_custom_call" | custom-call | flops 100000000 | bytes 6000000 | tf_op jit(solution)/shard_map/far/far_two/pallas_call | solution.py:286
  58.7 1.4 %collective-permute-start = (bf16[56,32,128]{2,1,0:T(8,128)(2,1)S(1)}, bf16[56,32,128]{2,1,0:T(8,128)(2,1)S(1)}, u32[]{:S(2)}, u32[]{:S(2)}) collective-permute-start(bf16[56,32,128]{2,1,0:T(8,128)(2,1)S(1)} %get-tuple-element.20), channel_id=1, source_target_pairs={{0,64},{64,128},{128,192},{192,0},{1,65},{65,129},{129,193},{193,1... | collective-permute-start | bytes 1376264 | tf_op jit(solution)/shard_map/far/ppermute | solution.py:364
  60.1 1.5 %collective-permute-start.1 = (bf16[56,32,128]{2,1,0:T(8,128)(2,1)S(1)}, bf16[56,32,128]{2,1,0:T(8,128)(2,1)S(1)}, u32[]{:S(2)}, u32[]{:S(2)}) collective-permute-start(bf16[56,32,128]{2,1,0:T(8,128)(2,1)S(1)} %get-tuple-element.22), channel_id=1, source_target_pairs={{0,192},{64,0},{128,64},{192,128},{1,193},{65,1},{129,65},{193,129... | collective-permute-start | bytes 1376264 | tf_op jit(solution)/shard_map/far/ppermute | solution.py:367
  61.6 5.0 %far_one.1 = (f32[56,32,128]{2,1,0:T(8,128)S(1)}, bf16[56,32,128]{2,1,0:T(8,128)(2,1)S(1)}, bf16[56,32,128]{2,1,0:T(8,128)(2,1)S(1)}, f32[56,32,128]{2,1,0:T(8,128)S(1)}) custom-call(s32[3145728]{0:T(1024)} %get-tuple-element.16.plan_in, bf16[192,32,128]{2,1,0:T(8,128)(2,1)S(1)} %bitcast.20, bf16[4,96,64,128]{3,2,1,0:T(8,128)(2,1)} %get-tuple-element.17.refs_0_, ...), custom_call_target="tpu_custom_call" | custom-call | flops 100000000 | bytes 6000000 | tf_op jit(solution)/shard_map/far/far_one/pallas_call | solution.py:286
  66.6 1.5 %collective-permute-start.3 = (bf16[56,32,128]{2,1,0:T(8,128)(2,1)S(1)}, bf16[56,32,128]{2,1,0:T(8,128)(2,1)S(1)}, u32[]{:S(2)}, u32[]{:S(2)}) collective-permute-start(bf16[56,32,128]{2,1,0:T(8,128)(2,1)S(1)} %get-tuple-element.24), channel_id=1, source_target_pairs={{0,192},{64,0},{128,64},{192,128},{1,193},{65,1},{129,65},{193,129... | collective-permute-start | bytes 1376264 | tf_op jit(solution)/shard_map/far/ppermute | solution.py:367
  68.0 0.1 collective-permute-start.4
  68.1 4.0 %collective-permute-done.passed_a = bf16[56,32,128]{2,1,0:T(8,128)(2,1)S(1)} collective-permute-done((bf16[56,32,128]{2,1,0:T(8,128)(2,1)S(1)}, bf16[56,32,128]{2,1,0:T(8,128)(2,1)S(1)}, u32[]{:S(2)}, u32[]{:S(2)}) %collective-permute-start) | collective-permute-done | bytes 458784 | tf_op jit(solution)/shard_map/far/ppermute | solution.py:364
  72.1 0.0 collective-permute-done.1.passed_b
  72.1 0.2 add_passed.1
  72.2 1.0 %collective-permute-start.2 = (bf16[56,32,128]{2,1,0:T(8,128)(2,1)S(1)}, bf16[56,32,128]{2,1,0:T(8,128)(2,1)S(1)}, u32[]{:S(2)}, u32[]{:S(2)}) collective-permute-start(bf16[56,32,128]{2,1,0:T(8,128)(2,1)S(1)} %get-tuple-element.23), channel_id=1, source_target_pairs={{0,64},{64,128},{128,192},{192,0},{1,65},{65,129},{129,193},{193,1... | collective-permute-start | bytes 1376264 | tf_op jit(solution)/shard_map/far/ppermute | solution.py:364
  73.2 1.8 %collective-permute-start.5 = (bf16[56,32,128]{2,1,0:T(8,128)(2,1)S(1)}, bf16[56,32,128]{2,1,0:T(8,128)(2,1)S(1)}, u32[]{:S(2)}, u32[]{:S(2)}) collective-permute-start(bf16[56,32,128]{2,1,0:T(8,128)(2,1)S(1)} %get-tuple-element.26), channel_id=1, source_target_pairs={{0,192},{64,0},{128,64},{192,128},{1,193},{65,1},{129,65},{193,129... | collective-permute-start | bytes 1376264 | tf_op jit(solution)/shard_map/far/ppermute | solution.py:367
  75.0 3.0 %far_own.1.own = f32[112,32,128]{2,1,0:T(8,128)S(1)} custom-call(s32[3145728]{0:T(1024)} %get-tuple-element.16.plan_in, bf16[192,32,128]{2,1,0:T(8,128)(2,1)S(1)} %bitcast.21, bf16[4,96,64,128]{3,2,1,0:T(8,128)(2,1)} %get-tuple-element.17.refs_0_, f32[4,112,32,128]{3,2,1,0:T(8,128)} %get-tuple-element.18.refs_1_), custom_call_target="tpu_custom_call" | custom-call | flops 100000000 | bytes 6000000 | tf_op jit(solution)/shard_map/far/far_own/pallas_call | solution.py:286
  78.0 3.6 %collective-permute-done.3.low_b = bf16[56,32,128]{2,1,0:T(8,128)(2,1)S(1)} collective-permute-done((bf16[56,32,128]{2,1,0:T(8,128)(2,1)S(1)}, bf16[56,32,128]{2,1,0:T(8,128)(2,1)S(1)}, u32[]{:S(2)}, u32[]{:S(2)}) %collective-permute-start.3) | collective-permute-done | bytes 458784 | tf_op jit(solution)/shard_map/far/ppermute | solution.py:367
  81.5 0.0 collective-permute-done.4.high_a
  81.5 9.8 %collective-permute-done.2.low_a = bf16[56,32,128]{2,1,0:T(8,128)(2,1)S(1)} collective-permute-done((bf16[56,32,128]{2,1,0:T(8,128)(2,1)S(1)}, bf16[56,32,128]{2,1,0:T(8,128)(2,1)S(1)}, u32[]{:S(2)}, u32[]{:S(2)}) %collective-permute-start.2) | collective-permute-done | bytes 458784 | tf_op jit(solution)/shard_map/far/ppermute | solution.py:364
  91.3 0.0 collective-permute-done.5.high_b
  91.4 2.1 %finish.1 = f32[112,64,64]{2,1,0:T(8,128)} custom-call(f32[112,32,128]{2,1,0:T(8,128)S(1)} %far_own.1.own, bf16[56,32,128]{2,1,0:T(8,128)(2,1)S(1)} %collective-permute-done.2.low_a, bf16[56,32,128]{2,1,0:T(8,128)(2,1)S(1)} %collective-permute-done.3.low_b, bf16[56,32,128]{2,1,0:T(8,128)(2,1)S(1)} %collective-permute-done.4.high_a, ...), custom_call_target="tpu_custom_call" | custom-call | tf_op jit(solution)/shard_map/finish/finish/pallas_call | solution.py:339
Async XLA Ops:
  2.9 52.8 %all-to-all-start = ((bf16[64,96,128]{2,1,0:T(8,128)(2,1)}), bf16[64,96,128]{2,1,0:T(8,128)(2,1)S(1)}, u32[]{:S(2)}, u32[]{:S(2)}) async-start(bf16[64,96,128]{2,1,0:T(8,128)(2,1)} %bitcast.22), calls=%async_computation | async-start | bytes 3145728 | tf_op jit(solution)/shard_map/exchange/all_to_all | solution.py:357
  58.7 13.4 %collective-permute-start = (bf16[56,32,128]{2,1,0:T(8,128)(2,1)S(1)}, bf16[56,32,128]{2,1,0:T(8,128)(2,1)S(1)}, u32[]{:S(2)}, u32[]{:S(2)}) collective-permute-start(bf16[56,32,128]{2,1,0:T(8,128)(2,1)S(1)} %get-tuple-element.20), channel_id=1, source_target_pairs={{0,64},{64,128},{128,192},{192,0},{1,65},{65,129},{129,193},{193,1... | collective-permute-start | bytes 1376264 | tf_op jit(solution)/shard_map/far/ppermute | solution.py:364
  60.1 12.0 %collective-permute-start.1 = (bf16[56,32,128]{2,1,0:T(8,128)(2,1)S(1)}, bf16[56,32,128]{2,1,0:T(8,128)(2,1)S(1)}, u32[]{:S(2)}, u32[]{:S(2)}) collective-permute-start(bf16[56,32,128]{2,1,0:T(8,128)(2,1)S(1)} %get-tuple-element.22), channel_id=1, source_target_pairs={{0,192},{64,0},{128,64},{192,128},{1,193},{65,1},{129,65},{193,129... | collective-permute-start | bytes 1376264 | tf_op jit(solution)/shard_map/far/ppermute | solution.py:367
  66.6 15.0 %collective-permute-start.3 = (bf16[56,32,128]{2,1,0:T(8,128)(2,1)S(1)}, bf16[56,32,128]{2,1,0:T(8,128)(2,1)S(1)}, u32[]{:S(2)}, u32[]{:S(2)}) collective-permute-start(bf16[56,32,128]{2,1,0:T(8,128)(2,1)S(1)} %get-tuple-element.24), channel_id=1, source_target_pairs={{0,192},{64,0},{128,64},{192,128},{1,193},{65,1},{129,65},{193,129... | collective-permute-start | bytes 1376264 | tf_op jit(solution)/shard_map/far/ppermute | solution.py:367
  68.0 13.5 %collective-permute-start.4 = (bf16[56,32,128]{2,1,0:T(8,128)(2,1)S(1)}, bf16[56,32,128]{2,1,0:T(8,128)(2,1)S(1)}, u32[]{:S(2)}, u32[]{:S(2)}) collective-permute-start(bf16[56,32,128]{2,1,0:T(8,128)(2,1)S(1)} %get-tuple-element.25), channel_id=1, source_target_pairs={{0,64},{64,128},{128,192},{192,0},{1,65},{65,129},{129,193},{193,1... | collective-permute-start | bytes 1376264 | tf_op jit(solution)/shard_map/far/ppermute | solution.py:364
  72.2 19.1 %collective-permute-start.2 = (bf16[56,32,128]{2,1,0:T(8,128)(2,1)S(1)}, bf16[56,32,128]{2,1,0:T(8,128)(2,1)S(1)}, u32[]{:S(2)}, u32[]{:S(2)}) collective-permute-start(bf16[56,32,128]{2,1,0:T(8,128)(2,1)S(1)} %get-tuple-element.23), channel_id=1, source_target_pairs={{0,64},{64,128},{128,192},{192,0},{1,65},{65,129},{129,193},{193,1... | collective-permute-start | bytes 1376264 | tf_op jit(solution)/shard_map/far/ppermute | solution.py:364
  73.2 18.1 %collective-permute-start.5 = (bf16[56,32,128]{2,1,0:T(8,128)(2,1)S(1)}, bf16[56,32,128]{2,1,0:T(8,128)(2,1)S(1)}, u32[]{:S(2)}, u32[]{:S(2)}) collective-permute-start(bf16[56,32,128]{2,1,0:T(8,128)(2,1)S(1)} %get-tuple-element.26), channel_id=1, source_target_pairs={{0,192},{64,0},{128,64},{192,128},{1,193},{65,1},{129,65},{193,129... | collective-permute-start | bytes 1376264 | tf_op jit(solution)/shard_map/far/ppermute | solution.py:367

commit v4 on v3

--- a/solution.py
+++ b/solution.py
@@ -24,6 +24,7 @@
 CAP = 3 * SPAN
 GROUP = 32
 GROUPS = CAP // GROUP
+FIRST = 40
 CHUNKS = 4
 AREA = CAP + GROUP
 SUMS = 4 * AREA
@@ -43,7 +44,7 @@
         wide[pl.ds(first + i, E, stride=stride), :] = slab_of(i).astype(F32).T
 
 
-def send_kernel(rows, p_ref, out_ref, rows_here, blocks, packed, wide, outgoing, arrived, written):
+def send_kernel(rows, p_ref, out_ref, rows_here, blocks, wide, outgoing, arrived, written):
     rows_copy = pltpu.make_async_copy(rows, rows_here, arrived.at[4])
     rows_copy.start()
     copies = [
@@ -54,7 +55,6 @@
     for c in range(4):
         copies[c].wait()
         transpose_slabs(lambda i: blocks[c, :, i].reshape(128, E), 8, 40, wide, c * 8)
-    packed[...] = wide[...].reshape(E, 40, 128)[:, :32].astype(BF16)
     rows_copy.wait()
 
     copies = []
@@ -65,7 +65,8 @@
         def _(n):
             peer = c * (64 // CHUNKS) + n
             for s in range(3):
-                outgoing[peer * 3 + s] = packed[rows_here[s, 0, peer]]
+                row = pl.multiple_of(rows_here[s, 0, peer] * 40, 8)
+                outgoing[peer * 3 + s] = wide[pl.ds(row, 32), :].astype(BF16)
 
         some = pl.ds(c * size, size)
         copies.append(pltpu.make_async_copy(outgoing.at[some], out_ref.at[some], written.at[c]))
@@ -83,7 +84,6 @@
         scratch_shapes=[
             SM((3, 1, 64), jnp.int32),
             VM((4, 2, 8, 64, E), BF16),
-            VM((E, 32, 128), BF16),
             VM((E * 40, 128), F32),
             VM((FAR, 32, 128), BF16),
             pltpu.SemaphoreType.DMA((5,)),
@@ -102,8 +102,8 @@
 
 
 def near_kernel(me, neighbours, slot, parent, a_ref, r_ref, p_ref, *refs):
-    far_pairs_out, sums_out, plan_out, pairs, doubled, wide, far_pairs, sums = refs[:8]
-    plan, near_pairs, near_blocks, near_sums, far_list, written = refs[8:]
+    far_pairs_out, sums_out, early_low, early_high, plan_out, pairs, doubled, wide, far_pairs, sums, early = refs[:11]
+    plan, near_pairs, near_blocks, near_sums, far_list, written = refs[11:]
     copies = []
 
     def two(i):
@@ -186,8 +186,14 @@
             return carry
 
         lax.fori_loop(0, groups, group, 0)
-        copies.append(pltpu.make_async_copy(sums.at[part], sums_out.at[part], written.at[4 + part]))
-        copies[-1].start()
+        if part == 0:
+            early[...] = sums[0].astype(BF16)
+            for h, out in enumerate((early_low, early_high)):
+                copies.append(pltpu.make_async_copy(early.at[pl.ds(h * HALF, HALF)], out, written.at[9 + h]))
+                copies[-1].start()
+        else:
+            copies.append(pltpu.make_async_copy(sums.at[part], sums_out.at[part], written.at[4 + part]))
+            copies[-1].start()
 
     copies.append(pltpu.make_async_copy(plan, plan_out.at[pl.ds(0, PLAN)], written.at[8]))
     copies[-1].start()
@@ -201,22 +207,25 @@
         out_shape=[
             jax.ShapeDtypeStruct((4, CAP, 64, 128), BF16),
             jax.ShapeDtypeStruct((4, BLOCKS, 32, 128), F32),
+            jax.ShapeDtypeStruct((HALF, 32, 128), BF16),
+            jax.ShapeDtypeStruct((HALF, 32, 128), BF16),
         ]
         + [jax.ShapeDtypeStruct((ROOM,), jnp.int32)],
         in_specs=[pl.BlockSpec(memory_space=SM)] * 4 + [pl.BlockSpec(memory_space=VM)] * 3,
-        out_specs=[pl.BlockSpec(memory_space=HBM)] * 3,
+        out_specs=[pl.BlockSpec(memory_space=HBM)] * 5,
         scratch_shapes=[
             VM((4 * E + 1, 64, 128), BF16),
             VM((E, 64, 128), BF16),
             VM((E * 72, 128), F32),
             VM((4, CAP, 64, 128), BF16),
             VM((4, BLOCKS, 32, 128), F32),
+            VM((BLOCKS, 32, 128), BF16),
             SM((PLAN,), jnp.int32),
             SM((4 * SPAN + GROUP,), jnp.int32),
             SM((4 * SPAN + GROUP,), jnp.int32),
             SM((4 * SPAN + GROUP,), jnp.int32),
             SM((4 * AREA,), jnp.int32),
-            pltpu.SemaphoreType.DMA((9,)),
+            pltpu.SemaphoreType.DMA((11,)),
         ],
         compiler_params=pltpu.CompilerParams(vmem_limit_bytes=55 * MB),
         cost_estimate=pl.CostEstimate(flops=700_000_000, bytes_accessed=40_000_000, transcendentals=0),
@@ -245,7 +254,8 @@
 
     for n in range(len(parts)):
         pairs_copy(n, 0).start()
-        near_copy(n).start()
+        if parts[n]:
+            near_copy(n).start()
     plan_copy.wait()
     for n, part in enumerate(parts):
         for g in range(1, GROUPS):
@@ -274,11 +284,13 @@
         def _(n=n):
             pairs_copy(n, 0).wait()
 
-        near_copy(n).wait()
+        if part:
+            near_copy(n).wait()
         size = BLOCKS // len(kinds[n])
         for h, kind in enumerate(kinds[n]):
             some = pl.ds(h * size, size)
-            outs[2 * n + h][...] = (near[n, some] + sums[some]).astype(kind)
+            total = near[n, some] + sums[some] if part else sums[some]
+            outs[2 * n + h][...] = total.astype(kind)
 
 
 def far_terms(parts, kinds, plan, incoming, pairs, near, name):
@@ -303,47 +315,53 @@
     )(plan, incoming, pairs, near)
 
 
-def add_kernel(here_a, passed_a, here_b, passed_b, out_a, out_b):
-    out_a[...] = (here_a[...] + passed_a[...].astype(F32)).astype(BF16)
-    out_b[...] = (here_b[...] + passed_b[...].astype(F32)).astype(BF16)
+def add_kernel(here_a, early_a, passed_a, here_b, early_b, passed_b, *outs):
+    sides = (here_a, early_a, passed_a), (here_b, early_b, passed_b)
+    for n, (here, early, passed) in enumerate(sides):
+        total = (here[...] + early[...].astype(F32) + passed[...].astype(F32)).astype(BF16)
+        outs[2 * n][...] = total[:FIRST]
+        outs[2 * n + 1][...] = total[FIRST:]
 
 
 def add_passed(*parts):
     return pl.pallas_call(
         add_kernel,
-        out_shape=[jax.ShapeDtypeStruct((HALF, 32, 128), BF16)] * 2,
-        in_specs=[pl.BlockSpec(memory_space=VM)] * 4,
-        out_specs=[pl.BlockSpec(memory_space=VM)] * 2,
+        out_shape=[jax.ShapeDtypeStruct((size, 32, 128), BF16) for size in (FIRST, HALF - FIRST)] * 2,
+        in_specs=[pl.BlockSpec(memory_space=VM)] * 6,
+        out_specs=[pl.BlockSpec(memory_space=VM)] * 4,
         compiler_params=pltpu.CompilerParams(vmem_limit_bytes=16 * MB),
         name="add_passed",
     )(*parts)
 
 
-def finish_kernel(own, low_a, low_b, high_a, high_b, out_ref, totals, written):
+def finish_kernel(first, size, own, low_a, low_b, high_a, high_b, *refs):
+    out_ref, totals, written = refs[-3:]
     copies = []
-    size = BLOCKS // CHUNKS
-    for c in range(CHUNKS):
-        one, other = ((low_a, low_b), (high_a, high_b))[c * 2 // CHUNKS]
-        some = pl.ds(c * size, size)
-        here = pl.ds(c * size % HALF, size)
-        total = own[some] + one[here].astype(F32) + other[here].astype(F32)
-        totals[some, :32] = total[:, :, :64]
-        totals[some, 32:] = total[:, :, 64:]
-        copies.append(pltpu.make_async_copy(totals.at[some], out_ref.at[some], written.at[c]))
-        copies[-1].start()
+    step = size // 2
+    for h, (one, other) in enumerate(((low_a, low_b), (high_a, high_b))):
+        for c in range(2):
+            at = first + c * step
+            some = pl.ds(h * HALF + at, step)
+            mine = pl.ds(h * size + c * step, step)
+            total = own[some] + one[pl.ds(at, step)].astype(F32) + other[pl.ds(c * step, step)].astype(F32)
+            totals[mine, :32] = total[:, :, :64]
+            totals[mine, 32:] = total[:, :, 64:]
+            copies.append(pltpu.make_async_copy(totals.at[mine], out_ref.at[some], written.at[2 * h + c]))
+            copies[-1].start()
     for copy in copies:
         copy.wait()
 
 
-def finish(*parts):
+def finish(first, size, *parts):
     return pl.pallas_call(
-        finish_kernel,
+        functools.partial(finish_kernel, first, size),
         out_shape=jax.ShapeDtypeStruct((BLOCKS, 64, 64), F32),
-        in_specs=[pl.BlockSpec(memory_space=VM)] * 5,
+        in_specs=[pl.BlockSpec(memory_space=VM)] * 5 + [pl.BlockSpec(memory_space=HBM)] * (len(parts) - 5),
         out_specs=pl.BlockSpec(memory_space=HBM),
-        scratch_shapes=[VM((BLOCKS, 64, 64), F32), pltpu.SemaphoreType.DMA((CHUNKS,))],
+        input_output_aliases={5: 0} if first else {},
+        scratch_shapes=[VM((2 * size, 64, 64), F32), pltpu.SemaphoreType.DMA((4,))],
         compiler_params=pltpu.CompilerParams(vmem_limit_bytes=24 * MB),
-        name="finish",
+        name=f"finish_{first}",
     )(*parts)
 
 
@@ -356,7 +374,7 @@
         outgoing = send_blocks(jnp.transpose(send_rows, (2, 0, 1)), p_t.reshape(2, 32, 64, E))
         incoming = lax.all_to_all(outgoing.reshape(64, 96, 128), "dev", 0, 0, tiled=True).reshape(FAR, 32, 128)
     with jax.named_scope("near"):
-        pairs, near, plan = near_terms(
+        pairs, near, early_low, early_high, plan = near_terms(
             me, neighbours.T, slot.T, parent.reshape(1, E), a_t, r_t, p_t.reshape(4096, E)
         )
 
@@ -366,6 +384,9 @@
     def to_last(x):
         return lax.ppermute(x, "grp", [(i, (i + 3) % 4) for i in range(4)])
 
+    with jax.named_scope("early"):
+        early_low, early_high = to_next(early_low), to_last(early_high)
+        incoming, early_low, early_high = lax.optimization_barrier((incoming, early_low, early_high))
     with jax.named_scope("far"):
         far_low, far_high = far_terms((0,), ((BF16, BF16),), plan, incoming, pairs, near, "far_two")
         passed_low, passed_high = to_next(far_low), to_last(far_high)
@@ -373,11 +394,15 @@
             (1, 2), ((F32, BF16), (BF16, F32)), plan, incoming, pairs, near, "far_one"
         )
         from_last_high, from_next_low = to_next(next_high), to_last(last_low)
-        both_low, both_high = add_passed(next_low, passed_low, last_high, passed_high)
-        from_last_low, from_next_high = to_next(both_low), to_last(both_high)
+        low, low_rest, high, high_rest = add_passed(
+            next_low, early_low, passed_low, last_high, early_high, passed_high
+        )
+        from_last_low, from_next_high = to_next(low), to_last(high)
+        low_rest, high_rest = to_next(low_rest), to_last(high_rest)
         (own,) = far_terms((3,), ((F32,),), plan, incoming, pairs, near, "far_own")
     with jax.named_scope("finish"):
-        coarse = finish(own, from_last_low, from_next_low, from_last_high, from_next_high)
+        coarse = finish(0, FIRST, own, from_next_low, from_last_low, from_last_high, from_next_high)
+        coarse = finish(FIRST, HALF - FIRST, own, from_next_low, low_rest, from_last_high, high_rest, coarse)
     return coarse.reshape(ROWS, SLOTS, 64, 64)
 
 

time: 93.7 us -> 92.5 us (0.987)
  waiting for transfers between devices: 33 us -> 25.4 us
  starting transfers between devices: 20.2 us -> 26 us
    all_to_all x1, waiting for transfers between devices: 15.7 us -> 2.35 us  [on_device(): lax.all_to_all(outgoing.reshape(64, 96, 128), 'dev', 0, 0, tiled=True)]
    ppermute x3 -> x5, starting transfers between devices: 4.75 us -> 9.19 us  [to_last(): return lax.ppermute(x, 'grp', [(i, (i + 3) % 4) for i in range(4)])]
    ppermute x3 -> x5, waiting for transfers between devices: 3.6 us -> 6.5 us  [to_last(): return lax.ppermute(x, 'grp', [(i, (i + 3) % 4) for i in range(4)])]
    ppermute x3 -> x5, waiting for transfers between devices: 13.8 us -> 16.5 us  [to_next(): return lax.ppermute(x, 'grp', [(i, (i + 1) % 4) for i in range(4)])]
    ppermute x3 -> x5, starting transfers between devices: 2.45 us -> 3.83 us  [to_next(): return lax.ppermute(x, 'grp', [(i, (i + 1) % 4) for i in range(4)])]
    pallas_call x2 -> x3, Pallas kernels: 2.2 us -> 3.04 us  [the longest x2 2.77 us: finish(): pl.pallas_call(functools.partial(finish_kernel, first, size), out_shape=j...]
  transfers between devices with their start and end apart: 7 -> 11, of which waited for: 4 -> 6; matrix products, arithmetic and copies ran while one was open for 0% -> 0% of each run, Pallas kernels for 35% -> 37%
where the time goes in v4:
time: 92.5 us; the launch traced here: 92.2 us
  Pallas kernels  40.6 us (44%)
  starting transfers between devices  26 us (28%)
  waiting for transfers between devices  25.4 us (27%)
    pallas_call x1, Pallas kernels, near_terms(): pl.pallas_call(near_kernel, out_shape=[jax.ShapeDtypeStruct((4, CAP, 64,...  24.2 us
    ppermute x5, waiting for transfers between devices, to_next(): return lax.ppermute(x, 'grp', [(i, (i + 1) % 4) for i in range(4)])  16.5 us
    all_to_all x1, starting transfers between devices, on_device(): lax.all_to_all(outgoing.reshape(64, 96, 128), 'dev', 0, 0, tiled=True)  13 us
    pallas_call x3, Pallas kernels, far_terms(): pl.pallas_call(functools.partial(far_kernel, parts, kinds), in_specs=[pl....  10.6 us
    ppermute x5, starting transfers between devices, to_last(): return lax.ppermute(x, 'grp', [(i, (i + 3) % 4) for i in range(4)])  9.19 us
    ppermute x5, waiting for transfers between devices, to_last(): return lax.ppermute(x, 'grp', [(i, (i + 3) % 4) for i in range(4)])  6.5 us
    ppermute x5, starting transfers between devices, to_next(): return lax.ppermute(x, 'grp', [(i, (i + 1) % 4) for i in range(4)])  3.83 us
    pallas_call x1, Pallas kernels, send_blocks(): pl.pallas_call(send_kernel, out_shape=jax.ShapeDtypeStruct((FAR, 32, 128)...  2.82 us
  transfers between devices with their start and end apart: 11, of which 6 were waited for; matrix products, arithmetic and copies ran while one was open for 0% of the time, Pallas kernels for 37%

profile of v4, /device:TPU:1, one launch (start us, length us, event | category | flops | bytes accessed | tf_op | source)
XLA Modules:
  0.0 92.2 jit_solution(790741131601649811)
XLA Ops:
  0.0 2.8 %send_blocks.1 = bf16[192,32,128]{2,1,0:T(8,128)(2,1)} custom-call(s32[3,1,64]{2,1,0:T(1,128)} %bitcast.29, bf16[2,32,64,128]{3,2,1,0:T(8,128)(2,1)} %bitcast.24), custom_call_target="tpu_custom_call" | custom-call | tf_op jit(solution)/shard_map/exchange/send_blocks/pallas_call | solution.py:79
  2.8 13.0 %all-to-all-start = ((bf16[64,96,128]{2,1,0:T(8,128)(2,1)}), bf16[64,96,128]{2,1,0:T(8,128)(2,1)S(1)}, u32[]{:S(2)}, u32[]{:S(2)}) async-start(bf16[64,96,128]{2,1,0:T(8,128)(2,1)} %bitcast.22), calls=%async_computation | async-start | bytes 3145728 | tf_op jit(solution)/shard_map/exchange/all_to_all | solution.py:375
  15.8 24.2 %near_terms.1 = (bf16[4,96,64,128]{3,2,1,0:T(8,128)(2,1)}, f32[4,112,32,128]{3,2,1,0:T(8,128)}, bf16[56,32,128]{2,1,0:T(8,128)(2,1)}, bf16[56,32,128]{2,1,0:T(8,128)(2,1)}, s32[3145728]{0:T(1024)}) custom-call(s32[1]{0:T(128)} %bitcast.me, s32[3,128]{1,0:T(4,128)} %bitcast.27, s32[4,128]{1,0:T(4,128)} %bitcast.28, s32[1,128]{1,0:T(1,128)} %bitcast.30, ...), custom_call_target="tpu_custom_call" | custom-call | flops 700000000 | bytes 40000000 | tf_op jit(solution)/shard_map/near/near_terms/pallas_call | solution.py:205
  40.0 1.4 %collective-permute-start = (bf16[56,32,128]{2,1,0:T(8,128)(2,1)}, bf16[56,32,128]{2,1,0:T(8,128)(2,1)S(1)}, u32[]{:S(2)}, u32[]{:S(2)}) collective-permute-start(bf16[56,32,128]{2,1,0:T(8,128)(2,1)} %get-tuple-element.24), channel_id=1, source_target_pairs={{0,64},{64,128},{128,192},{192,0},{1,65},{65,129},{129,193},{193,1... | collective-permute-start | bytes 1376264 | tf_op jit(solution)/shard_map/early/ppermute | solution.py:382
  41.4 1.5 %collective-permute-start.1 = (bf16[56,32,128]{2,1,0:T(8,128)(2,1)}, bf16[56,32,128]{2,1,0:T(8,128)(2,1)S(1)}, u32[]{:S(2)}, u32[]{:S(2)}) collective-permute-start(bf16[56,32,128]{2,1,0:T(8,128)(2,1)} %get-tuple-element.25), channel_id=1, source_target_pairs={{0,192},{64,0},{128,64},{192,128},{1,193},{65,1},{129,65},{193,129... | collective-permute-start | bytes 1376264 | tf_op jit(solution)/shard_map/early/ppermute | solution.py:385
  42.9 10.4 %collective-permute-done.early_a = bf16[56,32,128]{2,1,0:T(8,128)(2,1)S(1)} collective-permute-done((bf16[56,32,128]{2,1,0:T(8,128)(2,1)}, bf16[56,32,128]{2,1,0:T(8,128)(2,1)S(1)}, u32[]{:S(2)}, u32[]{:S(2)}) %collective-permute-start) | collective-permute-done | bytes 458784 | tf_op jit(solution)/shard_map/early/ppermute | solution.py:382
  53.3 0.0 collective-permute-done.1.early_b
  53.3 2.4 %all-to-all-done = bf16[64,96,128]{2,1,0:T(8,128)(2,1)S(1)} async-done(((bf16[64,96,128]{2,1,0:T(8,128)(2,1)}), bf16[64,96,128]{2,1,0:T(8,128)(2,1)S(1)}, u32[]{:S(2)}, u32[]{:S(2)}) %all-to-all-start) | async-done | bytes 1572896 | tf_op jit(solution)/shard_map/exchange/all_to_all | solution.py:375
  55.6 2.6 %far_two.1 = (bf16[56,32,128]{2,1,0:T(8,128)(2,1)S(1)}, bf16[56,32,128]{2,1,0:T(8,128)(2,1)S(1)}) custom-call(s32[3145728]{0:T(1024)} %get-tuple-element.23.plan_in, bf16[192,32,128]{2,1,0:T(8,128)(2,1)S(1)} %bitcast.19, bf16[4,96,64,128]{3,2,1,0:T(8,128)(2,1)} %get-tuple-element.27.refs_0_, f32[4,112,32,128]{3,2,1,0:T(8,128)} %get-tuple-element.28.refs_1_), custom_call_target="tpu_custom_call" | custom-call | flops 100000000 | bytes 6000000 | tf_op jit(solution)/shard_map/far/far_two/pallas_call | solution.py:298
  58.3 1.4 %collective-permute-start.3 = (bf16[56,32,128]{2,1,0:T(8,128)(2,1)S(1)}, bf16[56,32,128]{2,1,0:T(8,128)(2,1)S(1)}, u32[]{:S(2)}, u32[]{:S(2)}) collective-permute-start(bf16[56,32,128]{2,1,0:T(8,128)(2,1)S(1)} %get-tuple-element.32), channel_id=1, source_target_pairs={{0,64},{64,128},{128,192},{192,0},{1,65},{65,129},{129,193},{193,1... | collective-permute-start | bytes 1376264 | tf_op jit(solution)/shard_map/far/ppermute | solution.py:382
  59.6 1.5 %collective-permute-start.4 = (bf16[56,32,128]{2,1,0:T(8,128)(2,1)S(1)}, bf16[56,32,128]{2,1,0:T(8,128)(2,1)S(1)}, u32[]{:S(2)}, u32[]{:S(2)}) collective-permute-start(bf16[56,32,128]{2,1,0:T(8,128)(2,1)S(1)} %get-tuple-element.35), channel_id=1, source_target_pairs={{0,192},{64,0},{128,64},{192,128},{1,193},{65,1},{129,65},{193,129... | collective-permute-start | bytes 1376264 | tf_op jit(solution)/shard_map/far/ppermute | solution.py:385
  61.2 5.0 %far_one.1 = (f32[56,32,128]{2,1,0:T(8,128)S(1)}, bf16[56,32,128]{2,1,0:T(8,128)(2,1)S(1)}, bf16[56,32,128]{2,1,0:T(8,128)(2,1)S(1)}, f32[56,32,128]{2,1,0:T(8,128)S(1)}) custom-call(s32[3145728]{0:T(1024)} %get-tuple-element.23.plan_in, bf16[192,32,128]{2,1,0:T(8,128)(2,1)S(1)} %bitcast.20, bf16[4,96,64,128]{3,2,1,0:T(8,128)(2,1)} %get-tuple-element.27.refs_0_, ...), custom_call_target="tpu_custom_call" | custom-call | flops 100000000 | bytes 6000000 | tf_op jit(solution)/shard_map/far/far_one/pallas_call | solution.py:298
  66.1 1.5 %collective-permute-start.2 = (bf16[56,32,128]{2,1,0:T(8,128)(2,1)S(1)}, bf16[56,32,128]{2,1,0:T(8,128)(2,1)S(1)}, u32[]{:S(2)}, u32[]{:S(2)}) collective-permute-start(bf16[56,32,128]{2,1,0:T(8,128)(2,1)S(1)} %get-tuple-element.29), channel_id=1, source_target_pairs={{0,192},{64,0},{128,64},{192,128},{1,193},{65,1},{129,65},{193,129... | collective-permute-start | bytes 1376264 | tf_op jit(solution)/shard_map/far/ppermute | solution.py:385
  67.6 0.1 collective-permute-start.6
  67.7 4.0 %collective-permute-done.3.passed_a = bf16[56,32,128]{2,1,0:T(8,128)(2,1)S(1)} collective-permute-done((bf16[56,32,128]{2,1,0:T(8,128)(2,1)S(1)}, bf16[56,32,128]{2,1,0:T(8,128)(2,1)S(1)}, u32[]{:S(2)}, u32[]{:S(2)}) %collective-permute-start.3) | collective-permute-done | bytes 458784 | tf_op jit(solution)/shard_map/far/ppermute | solution.py:382
  71.7 0.0 collective-permute-done.4.passed_b
  71.7 0.3 add_passed.1
  71.9 1.0 %collective-permute-start.8 = (bf16[40,32,128]{2,1,0:T(8,128)(2,1)S(1)}, bf16[40,32,128]{2,1,0:T(8,128)(2,1)S(1)}, u32[]{:S(2)}, u32[]{:S(2)}) collective-permute-start(bf16[40,32,128]{2,1,0:T(8,128)(2,1)S(1)} %get-tuple-element.39), channel_id=1, source_target_pairs={{0,64},{64,128},{128,192},{192,0},{1,65},{65,129},{129,193},{193,1... | collective-permute-start | bytes 983048 | tf_op jit(solution)/shard_map/far/ppermute | solution.py:382
  72.9 1.8 %collective-permute-start.9 = (bf16[40,32,128]{2,1,0:T(8,128)(2,1)S(1)}, bf16[40,32,128]{2,1,0:T(8,128)(2,1)S(1)}, u32[]{:S(2)}, u32[]{:S(2)}) collective-permute-start(bf16[40,32,128]{2,1,0:T(8,128)(2,1)S(1)} %get-tuple-element.40), channel_id=1, source_target_pairs={{0,192},{64,0},{128,64},{192,128},{1,193},{65,1},{129,65},{193,129... | collective-permute-start | bytes 983048 | tf_op jit(solution)/shard_map/far/ppermute | solution.py:385
  74.7 0.0 collective-permute-start.5
  74.7 6.4 %collective-permute-done.2.low_a = bf16[56,32,128]{2,1,0:T(8,128)(2,1)S(1)} collective-permute-done((bf16[56,32,128]{2,1,0:T(8,128)(2,1)S(1)}, bf16[56,32,128]{2,1,0:T(8,128)(2,1)S(1)}, u32[]{:S(2)}, u32[]{:S(2)}) %collective-permute-start.2) | collective-permute-done | bytes 458784 | tf_op jit(solution)/shard_map/far/ppermute | solution.py:385
  81.1 2.9 %collective-permute-start.7 = (bf16[16,32,128]{2,1,0:T(8,128)(2,1)S(1)}, bf16[16,32,128]{2,1,0:T(8,128)(2,1)S(1)}, u32[]{:S(2)}, u32[]{:S(2)}) collective-permute-start(bf16[16,32,128]{2,1,0:T(8,128)(2,1)S(1)} %get-tuple-element.38), channel_id=1, source_target_pairs={{0,192},{64,0},{128,64},{192,128},{1,193},{65,1},{129,65},{193,129... | collective-permute-start | bytes 393224 | tf_op jit(solution)/shard_map/far/ppermute | solution.py:385
  84.0 3.0 %far_own.1.own = f32[112,32,128]{2,1,0:T(8,128)S(1)} custom-call(s32[3145728]{0:T(1024)} %get-tuple-element.23.plan_in, bf16[192,32,128]{2,1,0:T(8,128)(2,1)S(1)} %bitcast.21, bf16[4,96,64,128]{3,2,1,0:T(8,128)(2,1)} %get-tuple-element.27.refs_0_, f32[4,112,32,128]{3,2,1,0:T(8,128)} %get-tuple-element.28.refs_1_), custom_call_target="tpu_custom_call" | custom-call | flops 100000000 | bytes 6000000 | tf_op jit(solution)/shard_map/far/far_own/pallas_call | solution.py:298
  87.0 0.0 collective-permute-done.6.high_a
  87.0 1.1 %collective-permute-done.8.low_b = bf16[40,32,128]{2,1,0:T(8,128)(2,1)S(1)} collective-permute-done((bf16[40,32,128]{2,1,0:T(8,128)(2,1)S(1)}, bf16[40,32,128]{2,1,0:T(8,128)(2,1)S(1)}, u32[]{:S(2)}, u32[]{:S(2)}) %collective-permute-start.8) | collective-permute-done | bytes 327712 | tf_op jit(solution)/shard_map/far/ppermute | solution.py:382
  88.1 0.0 collective-permute-done.9.high_b
  88.1 1.7 %finish_0.1.refs_0_ = f32[112,64,64]{2,1,0:T(8,128)} custom-call(f32[112,32,128]{2,1,0:T(8,128)S(1)} %far_own.1.own, bf16[56,32,128]{2,1,0:T(8,128)(2,1)S(1)} %collective-permute-done.2.low_a, bf16[40,32,128]{2,1,0:T(8,128)(2,1)S(1)} %collective-permute-done.8.low_b, bf16[56,32,128]{2,1,0:T(8,128)(2,1)S(1)} %collective-permute-done.6.high_a, ...), custom_call_target="tpu_custom_call" | custom-call | tf_op jit(solution)/shard_map/finish/finish_0/pallas_call | solution.py:356
  89.8 1.1 %collective-permute-done.5.low_b = bf16[16,32,128]{2,1,0:T(8,128)(2,1)S(1)} collective-permute-done((bf16[16,32,128]{2,1,0:T(8,128)(2,1)S(1)}, bf16[16,32,128]{2,1,0:T(8,128)(2,1)S(1)}, u32[]{:S(2)}, u32[]{:S(2)}) %collective-permute-start.5) | collective-permute-done | bytes 131104 | tf_op jit(solution)/shard_map/far/ppermute | solution.py:382
  90.9 0.0 collective-permute-done.7.high_b
  90.9 1.1 %finish_40.1 = f32[112,64,64]{2,1,0:T(8,128)} custom-call(f32[112,32,128]{2,1,0:T(8,128)S(1)} %far_own.1.own, bf16[56,32,128]{2,1,0:T(8,128)(2,1)S(1)} %collective-permute-done.2.low_a, bf16[16,32,128]{2,1,0:T(8,128)(2,1)S(1)} %collective-permute-done.5.low_b, ...), custom_call_target="tpu_custom_call", output_to_operand_aliasing={{}: (5, {})} | custom-call | tf_op jit(solution)/shard_map/finish/finish_40/pallas_call | solution.py:356
Async XLA Ops:
  2.8 52.8 %all-to-all-start = ((bf16[64,96,128]{2,1,0:T(8,128)(2,1)}), bf16[64,96,128]{2,1,0:T(8,128)(2,1)S(1)}, u32[]{:S(2)}, u32[]{:S(2)}) async-start(bf16[64,96,128]{2,1,0:T(8,128)(2,1)} %bitcast.22), calls=%async_computation | async-start | bytes 3145728 | tf_op jit(solution)/shard_map/exchange/all_to_all | solution.py:375
  40.0 13.3 %collective-permute-start = (bf16[56,32,128]{2,1,0:T(8,128)(2,1)}, bf16[56,32,128]{2,1,0:T(8,128)(2,1)S(1)}, u32[]{:S(2)}, u32[]{:S(2)}) collective-permute-start(bf16[56,32,128]{2,1,0:T(8,128)(2,1)} %get-tuple-element.24), channel_id=1, source_target_pairs={{0,64},{64,128},{128,192},{192,0},{1,65},{65,129},{129,193},{193,1... | collective-permute-start | bytes 1376264 | tf_op jit(solution)/shard_map/early/ppermute | solution.py:382
  41.4 11.9 %collective-permute-start.1 = (bf16[56,32,128]{2,1,0:T(8,128)(2,1)}, bf16[56,32,128]{2,1,0:T(8,128)(2,1)S(1)}, u32[]{:S(2)}, u32[]{:S(2)}) collective-permute-start(bf16[56,32,128]{2,1,0:T(8,128)(2,1)} %get-tuple-element.25), channel_id=1, source_target_pairs={{0,192},{64,0},{128,64},{192,128},{1,193},{65,1},{129,65},{193,129... | collective-permute-start | bytes 1376264 | tf_op jit(solution)/shard_map/early/ppermute | solution.py:385
  58.3 13.4 %collective-permute-start.3 = (bf16[56,32,128]{2,1,0:T(8,128)(2,1)S(1)}, bf16[56,32,128]{2,1,0:T(8,128)(2,1)S(1)}, u32[]{:S(2)}, u32[]{:S(2)}) collective-permute-start(bf16[56,32,128]{2,1,0:T(8,128)(2,1)S(1)} %get-tuple-element.32), channel_id=1, source_target_pairs={{0,64},{64,128},{128,192},{192,0},{1,65},{65,129},{129,193},{193,1... | collective-permute-start | bytes 1376264 | tf_op jit(solution)/shard_map/far/ppermute | solution.py:382
  59.6 12.0 %collective-permute-start.4 = (bf16[56,32,128]{2,1,0:T(8,128)(2,1)S(1)}, bf16[56,32,128]{2,1,0:T(8,128)(2,1)S(1)}, u32[]{:S(2)}, u32[]{:S(2)}) collective-permute-start(bf16[56,32,128]{2,1,0:T(8,128)(2,1)S(1)} %get-tuple-element.35), channel_id=1, source_target_pairs={{0,192},{64,0},{128,64},{192,128},{1,193},{65,1},{129,65},{193,129... | collective-permute-start | bytes 1376264 | tf_op jit(solution)/shard_map/far/ppermute | solution.py:385
  66.1 15.0 %collective-permute-start.2 = (bf16[56,32,128]{2,1,0:T(8,128)(2,1)S(1)}, bf16[56,32,128]{2,1,0:T(8,128)(2,1)S(1)}, u32[]{:S(2)}, u32[]{:S(2)}) collective-permute-start(bf16[56,32,128]{2,1,0:T(8,128)(2,1)S(1)} %get-tuple-element.29), channel_id=1, source_target_pairs={{0,192},{64,0},{128,64},{192,128},{1,193},{65,1},{129,65},{193,129... | collective-permute-start | bytes 1376264 | tf_op jit(solution)/shard_map/far/ppermute | solution.py:385
  67.6 19.4 %collective-permute-start.6 = (bf16[56,32,128]{2,1,0:T(8,128)(2,1)S(1)}, bf16[56,32,128]{2,1,0:T(8,128)(2,1)S(1)}, u32[]{:S(2)}, u32[]{:S(2)}) collective-permute-start(bf16[56,32,128]{2,1,0:T(8,128)(2,1)S(1)} %get-tuple-element.37), channel_id=1, source_target_pairs={{0,64},{64,128},{128,192},{192,0},{1,65},{65,129},{129,193},{193,1... | collective-permute-start | bytes 1376264 | tf_op jit(solution)/shard_map/far/ppermute | solution.py:382
  71.9 16.2 %collective-permute-start.8 = (bf16[40,32,128]{2,1,0:T(8,128)(2,1)S(1)}, bf16[40,32,128]{2,1,0:T(8,128)(2,1)S(1)}, u32[]{:S(2)}, u32[]{:S(2)}) collective-permute-start(bf16[40,32,128]{2,1,0:T(8,128)(2,1)S(1)} %get-tuple-element.39), channel_id=1, source_target_pairs={{0,64},{64,128},{128,192},{192,0},{1,65},{65,129},{129,193},{193,1... | collective-permute-start | bytes 983048 | tf_op jit(solution)/shard_map/far/ppermute | solution.py:382
  72.9 15.2 %collective-permute-start.9 = (bf16[40,32,128]{2,1,0:T(8,128)(2,1)S(1)}, bf16[40,32,128]{2,1,0:T(8,128)(2,1)S(1)}, u32[]{:S(2)}, u32[]{:S(2)}) collective-permute-start(bf16[40,32,128]{2,1,0:T(8,128)(2,1)S(1)} %get-tuple-element.40), channel_id=1, source_target_pairs={{0,192},{64,0},{128,64},{192,128},{1,193},{65,1},{129,65},{193,129... | collective-permute-start | bytes 983048 | tf_op jit(solution)/shard_map/far/ppermute | solution.py:385
  74.7 16.2 %collective-permute-start.5 = (bf16[16,32,128]{2,1,0:T(8,128)(2,1)S(1)}, bf16[16,32,128]{2,1,0:T(8,128)(2,1)S(1)}, u32[]{:S(2)}, u32[]{:S(2)}) collective-permute-start(bf16[16,32,128]{2,1,0:T(8,128)(2,1)S(1)} %get-tuple-element.36), channel_id=1, source_target_pairs={{0,64},{64,128},{128,192},{192,0},{1,65},{65,129},{129,193},{193,1... | collective-permute-start | bytes 393224 | tf_op jit(solution)/shard_map/far/ppermute | solution.py:382
  81.1 9.8 %collective-permute-start.7 = (bf16[16,32,128]{2,1,0:T(8,128)(2,1)S(1)}, bf16[16,32,128]{2,1,0:T(8,128)(2,1)S(1)}, u32[]{:S(2)}, u32[]{:S(2)}) collective-permute-start(bf16[16,32,128]{2,1,0:T(8,128)(2,1)S(1)} %get-tuple-element.38), channel_id=1, source_target_pairs={{0,192},{64,0},{128,64},{192,128},{1,193},{65,1},{129,65},{193,129... | collective-permute-start | bytes 393224 | tf_op jit(solution)/shard_map/far/ppermute | solution.py:385

commit v5 on v4

--- a/solution.py
+++ b/solution.py
@@ -24,12 +24,14 @@
 CAP = 3 * SPAN
 GROUP = 32
 GROUPS = CAP // GROUP
+CHUNKS = 4
+SURE = 2
 FIRST = 40
-CHUNKS = 4
 AREA = CAP + GROUP
 SUMS = 4 * AREA
 COUNTS = 8 * AREA
 PLAN = COUNTS + 1024
+NEAR_AREA = 4 * SPAN + GROUP
 ROOM = 3 * MB
 AHEAD = (2, 1, 3, 0)
 
@@ -101,30 +103,18 @@
     return jnp.where(low, term[:32], term[32:])
 
 
-def near_kernel(me, neighbours, slot, parent, a_ref, r_ref, p_ref, *refs):
-    far_pairs_out, sums_out, early_low, early_high, plan_out, pairs, doubled, wide, far_pairs, sums, early = refs[:11]
-    plan, near_pairs, near_blocks, near_sums, far_list, written = refs[11:]
+def near_kernel(me, neighbours, slot, parent, a_in, r_in, p_in, *refs):
+    far_pairs_out, sums_out, early_low, early_high, plan_out, a_ref, r_ref, p_ref, pairs, doubled = refs[:10]
+    wide, far_pairs, sums, early, plan, near_pairs, near_blocks, near_sums, far_list, arrived, written = refs[10:]
+    incoming = [pltpu.make_async_copy(p_in, p_ref, arrived.at[5]), pltpu.make_async_copy(r_in, r_ref, arrived.at[4])]
+    incoming += [pltpu.make_async_copy(a_in.at[k], a_ref.at[k], arrived.at[k]) for k in range(4)]
+    for copy in incoming:
+        copy.start()
     copies = []
 
-    def two(i):
-        block = p_ref[rows_at(i, 64), :]
-        return jnp.concatenate([block, block], 0)
-
-    transpose_slabs(two, 64, 72, wide)
-    doubled[...] = wide[...].reshape(E, 72, 128)[:, :64].astype(BF16)
-
-    @pl.loop(0, 4)
-    def _(k):
-        transpose_slabs(
-            lambda i: jnp.concatenate([a_ref[rows_at(k * 64 + i, 64), :], r_ref[rows_at(i, 64), :]], 0), 64, 72, wide
-        )
-        pairs[rows_at(k, E)] = wide[...].reshape(E, 72, 128)[:, :64].astype(BF16)
-
-    pairs[4 * E] = jnp.zeros((64, 128), BF16)
-
+    near_counts, far_counts = [], []
     for part, ahead in enumerate(AHEAD):
         first = lax.rem(me[0] + ahead, 4) * SPAN
-        start = part * AREA
 
         def element(i, carry):
             near, far = carry
@@ -148,9 +138,47 @@
                 far = far + (1 - here)
             return near, far
 
-        near, far = lax.fori_loop(0, SPAN, element, (0, start))
-        many = far - start
-        plan[COUNTS + part] = many
+        near, far = lax.fori_loop(0, SPAN, element, (part * NEAR_AREA, part * AREA), unroll=2)
+        near_counts.append(near - part * NEAR_AREA)
+        far_counts.append(far - part * AREA)
+        plan[COUNTS + part] = far_counts[-1]
+
+        def pad_far(i, carry):
+            plan[part * AREA + i] = 0
+            plan[SUMS + part * AREA + i] = 0
+            return carry
+
+        lax.fori_loop(far_counts[-1], (far_counts[-1] + GROUP - 1) // GROUP * GROUP, pad_far, 0)
+
+        def pad_near(i, carry):
+            near_pairs[part * NEAR_AREA + i] = 4 * E
+            near_blocks[part * NEAR_AREA + i] = 0
+            near_sums[part * NEAR_AREA + i] = 0
+            return carry
+
+        lax.fori_loop(near_counts[-1], (near_counts[-1] + GROUP - 1) // GROUP * GROUP, pad_near, 0)
+
+    copies.append(pltpu.make_async_copy(plan, plan_out.at[pl.ds(0, PLAN)], written.at[8]))
+    copies[-1].start()
+
+    def two(i):
+        block = p_ref[rows_at(i, 64), :]
+        return jnp.concatenate([block, block], 0)
+
+    incoming[0].wait()
+    transpose_slabs(two, 64, 72, wide)
+    doubled[...] = wide[...].reshape(E, 72, 128)[:, :64].astype(BF16)
+    incoming[1].wait()
+    for k in range(4):
+        incoming[2 + k].wait()
+        transpose_slabs(
+            lambda i: jnp.concatenate([a_ref[k, rows_at(i, 64), :], r_ref[rows_at(i, 64), :]], 0), 64, 72, wide
+        )
+        pairs[rows_at(k, E)] = wide[...].reshape(E, 72, 128)[:, :64].astype(BF16)
+    pairs[4 * E] = jnp.zeros((64, 128), BF16)
+
+    for part in range(4):
+        start, many = part * AREA, far_counts[part]
 
         def keep(i, carry):
             far_pairs[part, i] = pairs[far_list[start + i]]
@@ -158,34 +186,23 @@
 
         lax.fori_loop(0, many, keep, 0)
 
-        def pad_far(i, carry):
+        def clear(i, carry):
             far_pairs[part, i] = jnp.zeros((64, 128), BF16)
-            plan[start + i] = 0
-            plan[SUMS + start + i] = 0
-            return carry
-
-        lax.fori_loop(many, (many + GROUP - 1) // GROUP * GROUP, pad_far, 0)
-
-        def pad_near(i, carry):
-            near_pairs[i] = 4 * E
-            near_blocks[i] = 0
-            near_sums[i] = 0
-            return carry
-
+            return carry
+
+        lax.fori_loop(many, (many + GROUP - 1) // GROUP * GROUP, clear, 0)
         copies.append(pltpu.make_async_copy(far_pairs.at[part], far_pairs_out.at[part], written.at[part]))
         copies[-1].start()
-        groups = (near + GROUP - 1) // GROUP
-        lax.fori_loop(near, groups * GROUP, pad_near, 0)
         sums[part] = jnp.zeros((BLOCKS, 32, 128), F32)
 
         def group(g, carry):
-            at = g * GROUP
+            at = part * NEAR_AREA + g * GROUP
             found = [term_of(pairs[near_pairs[at + u]], doubled[near_blocks[at + u]]) for u in range(GROUP)]
             for u in range(GROUP):
                 sums[part, near_sums[at + u]] += found[u]
             return carry
 
-        lax.fori_loop(0, groups, group, 0)
+        lax.fori_loop(0, (near_counts[part] + GROUP - 1) // GROUP, group, 0)
         if part == 0:
             early[...] = sums[0].astype(BF16)
             for h, out in enumerate((early_low, early_high)):
@@ -195,8 +212,6 @@
             copies.append(pltpu.make_async_copy(sums.at[part], sums_out.at[part], written.at[4 + part]))
             copies[-1].start()
 
-    copies.append(pltpu.make_async_copy(plan, plan_out.at[pl.ds(0, PLAN)], written.at[8]))
-    copies[-1].start()
     for copy in copies:
         copy.wait()
 
@@ -211,9 +226,12 @@
             jax.ShapeDtypeStruct((HALF, 32, 128), BF16),
         ]
         + [jax.ShapeDtypeStruct((ROOM,), jnp.int32)],
-        in_specs=[pl.BlockSpec(memory_space=SM)] * 4 + [pl.BlockSpec(memory_space=VM)] * 3,
+        in_specs=[pl.BlockSpec(memory_space=SM)] * 4 + [pl.BlockSpec(memory_space=HBM)] * 3,
         out_specs=[pl.BlockSpec(memory_space=HBM)] * 5,
         scratch_shapes=[
+            VM((4, 4096, E), BF16),
+            VM((4096, E), BF16),
+            VM((4096, E), BF16),
             VM((4 * E + 1, 64, 128), BF16),
             VM((E, 64, 128), BF16),
             VM((E * 72, 128), F32),
@@ -221,10 +239,11 @@
             VM((4, BLOCKS, 32, 128), F32),
             VM((BLOCKS, 32, 128), BF16),
             SM((PLAN,), jnp.int32),
-            SM((4 * SPAN + GROUP,), jnp.int32),
-            SM((4 * SPAN + GROUP,), jnp.int32),
-            SM((4 * SPAN + GROUP,), jnp.int32),
+            SM((4 * NEAR_AREA,), jnp.int32),
+            SM((4 * NEAR_AREA,), jnp.int32),
+            SM((4 * NEAR_AREA,), jnp.int32),
             SM((4 * AREA,), jnp.int32),
+            pltpu.SemaphoreType.DMA((6,)),
             pltpu.SemaphoreType.DMA((11,)),
         ],
         compiler_params=pltpu.CompilerParams(vmem_limit_bytes=55 * MB),
@@ -253,12 +272,13 @@
         return jnp.concatenate([jnp.where(low, x, turned), jnp.where(low, turned, x)], 0)
 
     for n in range(len(parts)):
-        pairs_copy(n, 0).start()
+        for g in range(SURE):
+            pairs_copy(n, g).start()
         if parts[n]:
             near_copy(n).start()
     plan_copy.wait()
     for n, part in enumerate(parts):
-        for g in range(1, GROUPS):
+        for g in range(SURE, GROUPS):
 
             @pl.when(plan[COUNTS + part] > g * GROUP)
             def _(n=n, g=g):
@@ -280,9 +300,11 @@
 
         lax.fori_loop(0, groups, group, 0)
 
-        @pl.when(groups == 0)
-        def _(n=n):
-            pairs_copy(n, 0).wait()
+        for g in range(SURE):
+
+            @pl.when(groups <= g)
+            def _(n=n, g=g):
+                pairs_copy(n, g).wait()
 
         if part:
             near_copy(n).wait()
@@ -366,7 +388,7 @@
 
 
 def on_device(a_blocks, r_blocks, p_blocks, neighbours, send_rows, parent, slot):
-    a_t = jnp.transpose(a_blocks, (1, 2, 3, 0)).reshape(4 * 4096, E)
+    a_t = jnp.transpose(a_blocks, (1, 2, 3, 0)).reshape(4, 4096, E)
     r_t = jnp.transpose(r_blocks, (1, 2, 0)).reshape(4096, E)
     p_t = jnp.transpose(p_blocks, (1, 2, 0))
     me = lax.axis_index("grp").astype(jnp.int32).reshape(1)
@@ -386,7 +408,6 @@
 
     with jax.named_scope("early"):
         early_low, early_high = to_next(early_low), to_last(early_high)
-        incoming, early_low, early_high = lax.optimization_barrier((incoming, early_low, early_high))
     with jax.named_scope("far"):
         far_low, far_high = far_terms((0,), ((BF16, BF16),), plan, incoming, pairs, near, "far_two")
         passed_low, passed_high = to_next(far_low), to_last(far_high)

time: 92.5 us -> 92.6 us (level)
  waiting for transfers between devices: 25.4 us -> 28.3 us
  Pallas kernels: 40.6 us -> 37.8 us
    all_to_all x1, waiting for transfers between devices: 2.35 us -> 14 us  [on_device(): lax.all_to_all(outgoing.reshape(64, 96, 128), 'dev', 0, 0, tiled=True)]
    ppermute x5, waiting for transfers between devices: 16.5 us -> 7.89 us  [to_next(): return lax.ppermute(x, 'grp', [(i, (i + 1) % 4) for i in range(4)])]
    pallas_call x3, Pallas kernels: 10.6 us -> 9.02 us  [far_terms(): pl.pallas_call(functools.partial(far_kernel, parts, kinds), in_specs=[pl....]
    pallas_call x1, Pallas kernels: 24.2 us -> 22.9 us  [near_terms(): pl.pallas_call(near_kernel, out_shape=[jax.ShapeDtypeStruct((4, CAP, 64,...]
  transfers between devices with their start and end apart: 11 -> 11, of which waited for: 6 -> 5; matrix products, arithmetic and copies ran while one was open for 0% -> 0% of each run, Pallas kernels for 37% -> 37%
where the time goes in v5:
time: 92.6 us; the launch traced here: 92.3 us
  Pallas kernels  37.8 us (41%)
  waiting for transfers between devices  28.3 us (31%)
  starting transfers between devices  26 us (28%)
    pallas_call x1, Pallas kernels, near_terms(): pl.pallas_call(near_kernel, out_shape=[jax.ShapeDtypeStruct((4, CAP, 64,...  22.9 us
    all_to_all x1, waiting for transfers between devices, on_device(): lax.all_to_all(outgoing.reshape(64, 96, 128), 'dev', 0, 0, tiled=True)  14 us
    all_to_all x1, starting transfers between devices, on_device(): lax.all_to_all(outgoing.reshape(64, 96, 128), 'dev', 0, 0, tiled=True)  13 us
    ppermute x5, starting transfers between devices, to_last(): return lax.ppermute(x, 'grp', [(i, (i + 3) % 4) for i in range(4)])  9.13 us
    pallas_call x3, Pallas kernels, far_terms(): pl.pallas_call(functools.partial(far_kernel, parts, kinds), in_specs=[pl....  9.02 us
    ppermute x5, waiting for transfers between devices, to_next(): return lax.ppermute(x, 'grp', [(i, (i + 1) % 4) for i in range(4)])  7.89 us
    ppermute x5, waiting for transfers between devices, to_last(): return lax.ppermute(x, 'grp', [(i, (i + 3) % 4) for i in range(4)])  6.45 us
    ppermute x5, starting transfers between devices, to_next(): return lax.ppermute(x, 'grp', [(i, (i + 1) % 4) for i in range(4)])  3.83 us
  transfers between devices with their start and end apart: 11, of which 5 were waited for; matrix products, arithmetic and copies ran while one was open for 0% of the time, Pallas kernels for 37%

profile of v5, /device:TPU:1, one launch (start us, length us, event | category | flops | bytes accessed | tf_op | source)
XLA Modules:
  0.0 92.3 jit_solution(10791730484992769856)
XLA Ops:
  0.0 2.8 %send_blocks.1 = bf16[192,32,128]{2,1,0:T(8,128)(2,1)} custom-call(s32[3,1,64]{2,1,0:T(1,128)} %bitcast.29, bf16[2,32,64,128]{3,2,1,0:T(8,128)(2,1)} %bitcast.24), custom_call_target="tpu_custom_call" | custom-call | tf_op jit(solution)/shard_map/exchange/send_blocks/pallas_call | solution.py:81
  2.8 13.0 %all-to-all-start = ((bf16[64,96,128]{2,1,0:T(8,128)(2,1)}), bf16[64,96,128]{2,1,0:T(8,128)(2,1)S(1)}, u32[]{:S(2)}, u32[]{:S(2)}) async-start(bf16[64,96,128]{2,1,0:T(8,128)(2,1)} %bitcast.22), calls=%async_computation | async-start | bytes 3145728 | tf_op jit(solution)/shard_map/exchange/all_to_all | solution.py:397
  15.8 22.9 %near_terms.1 = (bf16[4,96,64,128]{3,2,1,0:T(8,128)(2,1)}, f32[4,112,32,128]{3,2,1,0:T(8,128)}, bf16[56,32,128]{2,1,0:T(8,128)(2,1)}, bf16[56,32,128]{2,1,0:T(8,128)(2,1)}, s32[3145728]{0:T(1024)}) custom-call(s32[1]{0:T(128)} %bitcast.me, s32[3,128]{1,0:T(4,128)} %bitcast.27, s32[4,128]{1,0:T(4,128)} %bitcast.28, s32[1,128]{1,0:T(1,128)} %bitcast.30, ...), custom_call_target="tpu_custom_call" | custom-call | flops 700000000 | bytes 40000000 | tf_op jit(solution)/shard_map/near/near_terms/pallas_call | solution.py:220
  38.8 1.3 %collective-permute-start.1 = (bf16[56,32,128]{2,1,0:T(8,128)(2,1)}, bf16[56,32,128]{2,1,0:T(8,128)(2,1)S(1)}, u32[]{:S(2)}, u32[]{:S(2)}) collective-permute-start(bf16[56,32,128]{2,1,0:T(8,128)(2,1)} %get-tuple-element.25), channel_id=1, source_target_pairs={{0,64},{64,128},{128,192},{192,0},{1,65},{65,129},{129,193},{193,1... | collective-permute-start | bytes 1376264 | tf_op jit(solution)/shard_map/early/ppermute | solution.py:404
  40.1 1.5 %collective-permute-start.3 = (bf16[56,32,128]{2,1,0:T(8,128)(2,1)}, bf16[56,32,128]{2,1,0:T(8,128)(2,1)S(1)}, u32[]{:S(2)}, u32[]{:S(2)}) collective-permute-start(bf16[56,32,128]{2,1,0:T(8,128)(2,1)} %get-tuple-element.28), channel_id=1, source_target_pairs={{0,192},{64,0},{128,64},{192,128},{1,193},{65,1},{129,65},{193,129... | collective-permute-start | bytes 1376264 | tf_op jit(solution)/shard_map/early/ppermute | solution.py:407
  41.6 14.0 %all-to-all-done = bf16[64,96,128]{2,1,0:T(8,128)(2,1)S(1)} async-done(((bf16[64,96,128]{2,1,0:T(8,128)(2,1)}), bf16[64,96,128]{2,1,0:T(8,128)(2,1)S(1)}, u32[]{:S(2)}, u32[]{:S(2)}) %all-to-all-start) | async-done | bytes 1572896 | tf_op jit(solution)/shard_map/exchange/all_to_all | solution.py:397
  55.6 2.4 %far_two.1 = (bf16[56,32,128]{2,1,0:T(8,128)(2,1)S(1)}, bf16[56,32,128]{2,1,0:T(8,128)(2,1)S(1)}) custom-call(s32[3145728]{0:T(1024)} %get-tuple-element.20.plan_in, bf16[192,32,128]{2,1,0:T(8,128)(2,1)S(1)} %bitcast.19, bf16[4,96,64,128]{3,2,1,0:T(8,128)(2,1)} %get-tuple-element.21.refs_0_, f32[4,112,32,128]{3,2,1,0:T(8,128)} %get-tuple-element.22.refs_1_), custom_call_target="tpu_custom_call" | custom-call | flops 100000000 | bytes 6000000 | tf_op jit(solution)/shard_map/far/far_two/pallas_call | solution.py:320
  58.0 1.4 %collective-permute-start.2 = (bf16[56,32,128]{2,1,0:T(8,128)(2,1)S(1)}, bf16[56,32,128]{2,1,0:T(8,128)(2,1)S(1)}, u32[]{:S(2)}, u32[]{:S(2)}) collective-permute-start(bf16[56,32,128]{2,1,0:T(8,128)(2,1)S(1)} %get-tuple-element.26), channel_id=1, source_target_pairs={{0,64},{64,128},{128,192},{192,0},{1,65},{65,129},{129,193},{193,1... | collective-permute-start | bytes 1376264 | tf_op jit(solution)/shard_map/far/ppermute | solution.py:404
  59.4 1.5 %collective-permute-start.4 = (bf16[56,32,128]{2,1,0:T(8,128)(2,1)S(1)}, bf16[56,32,128]{2,1,0:T(8,128)(2,1)S(1)}, u32[]{:S(2)}, u32[]{:S(2)}) collective-permute-start(bf16[56,32,128]{2,1,0:T(8,128)(2,1)S(1)} %get-tuple-element.29), channel_id=1, source_target_pairs={{0,192},{64,0},{128,64},{192,128},{1,193},{65,1},{129,65},{193,129... | collective-permute-start | bytes 1376264 | tf_op jit(solution)/shard_map/far/ppermute | solution.py:407
  60.9 4.1 %far_one.1 = (f32[56,32,128]{2,1,0:T(8,128)S(1)}, bf16[56,32,128]{2,1,0:T(8,128)(2,1)S(1)}, bf16[56,32,128]{2,1,0:T(8,128)(2,1)S(1)}, f32[56,32,128]{2,1,0:T(8,128)S(1)}) custom-call(s32[3145728]{0:T(1024)} %get-tuple-element.20.plan_in, bf16[192,32,128]{2,1,0:T(8,128)(2,1)S(1)} %bitcast.20, bf16[4,96,64,128]{3,2,1,0:T(8,128)(2,1)} %get-tuple-element.21.refs_0_, ...), custom_call_target="tpu_custom_call" | custom-call | flops 100000000 | bytes 6000000 | tf_op jit(solution)/shard_map/far/far_one/pallas_call | solution.py:320
  65.1 1.4 %collective-permute-start = (bf16[56,32,128]{2,1,0:T(8,128)(2,1)S(1)}, bf16[56,32,128]{2,1,0:T(8,128)(2,1)S(1)}, u32[]{:S(2)}, u32[]{:S(2)}) collective-permute-start(bf16[56,32,128]{2,1,0:T(8,128)(2,1)S(1)} %get-tuple-element.23), channel_id=1, source_target_pairs={{0,192},{64,0},{128,64},{192,128},{1,193},{65,1},{129,65},{193,129... | collective-permute-start | bytes 1376264 | tf_op jit(solution)/shard_map/far/ppermute | solution.py:407
  66.5 0.0 collective-permute-done.1.early_a
  66.5 0.1 collective-permute-start.6
  66.6 0.0 collective-permute-done.3.early_b
  66.6 4.8 %collective-permute-done.2.passed_a = bf16[56,32,128]{2,1,0:T(8,128)(2,1)S(1)} collective-permute-done((bf16[56,32,128]{2,1,0:T(8,128)(2,1)S(1)}, bf16[56,32,128]{2,1,0:T(8,128)(2,1)S(1)}, u32[]{:S(2)}, u32[]{:S(2)}) %collective-permute-start.2) | collective-permute-done | bytes 458784 | tf_op jit(solution)/shard_map/far/ppermute | solution.py:404
  71.4 0.0 collective-permute-done.4.passed_b
  71.4 0.3 add_passed.1
  71.7 1.0 %collective-permute-start.8 = (bf16[40,32,128]{2,1,0:T(8,128)(2,1)S(1)}, bf16[40,32,128]{2,1,0:T(8,128)(2,1)S(1)}, u32[]{:S(2)}, u32[]{:S(2)}) collective-permute-start(bf16[40,32,128]{2,1,0:T(8,128)(2,1)S(1)} %get-tuple-element.33), channel_id=1, source_target_pairs={{0,64},{64,128},{128,192},{192,0},{1,65},{65,129},{129,193},{193,1... | collective-permute-start | bytes 983048 | tf_op jit(solution)/shard_map/far/ppermute | solution.py:404
  72.7 1.7 %collective-permute-start.9 = (bf16[40,32,128]{2,1,0:T(8,128)(2,1)S(1)}, bf16[40,32,128]{2,1,0:T(8,128)(2,1)S(1)}, u32[]{:S(2)}, u32[]{:S(2)}) collective-permute-start(bf16[40,32,128]{2,1,0:T(8,128)(2,1)S(1)} %get-tuple-element.34), channel_id=1, source_target_pairs={{0,192},{64,0},{128,64},{192,128},{1,193},{65,1},{129,65},{193,129... | collective-permute-start | bytes 983048 | tf_op jit(solution)/shard_map/far/ppermute | solution.py:407
  74.4 0.0 collective-permute-start.5
  74.4 6.4 %collective-permute-done.low_a = bf16[56,32,128]{2,1,0:T(8,128)(2,1)S(1)} collective-permute-done((bf16[56,32,128]{2,1,0:T(8,128)(2,1)S(1)}, bf16[56,32,128]{2,1,0:T(8,128)(2,1)S(1)}, u32[]{:S(2)}, u32[]{:S(2)}) %collective-permute-start) | collective-permute-done | bytes 458784 | tf_op jit(solution)/shard_map/far/ppermute | solution.py:407
  80.9 2.9 %collective-permute-start.7 = (bf16[16,32,128]{2,1,0:T(8,128)(2,1)S(1)}, bf16[16,32,128]{2,1,0:T(8,128)(2,1)S(1)}, u32[]{:S(2)}, u32[]{:S(2)}) collective-permute-start(bf16[16,32,128]{2,1,0:T(8,128)(2,1)S(1)} %get-tuple-element.32), channel_id=1, source_target_pairs={{0,192},{64,0},{128,64},{192,128},{1,193},{65,1},{129,65},{193,129... | collective-permute-start | bytes 393224 | tf_op jit(solution)/shard_map/far/ppermute | solution.py:407
  83.8 2.5 %far_own.1.own = f32[112,32,128]{2,1,0:T(8,128)S(1)} custom-call(s32[3145728]{0:T(1024)} %get-tuple-element.20.plan_in, bf16[192,32,128]{2,1,0:T(8,128)(2,1)S(1)} %bitcast.21, bf16[4,96,64,128]{3,2,1,0:T(8,128)(2,1)} %get-tuple-element.21.refs_0_, f32[4,112,32,128]{3,2,1,0:T(8,128)} %get-tuple-element.22.refs_1_), custom_call_target="tpu_custom_call" | custom-call | flops 100000000 | bytes 6000000 | tf_op jit(solution)/shard_map/far/far_own/pallas_call | solution.py:320
  86.3 0.0 collective-permute-done.6.high_a
  86.3 2.0 %collective-permute-done.8.low_b = bf16[40,32,128]{2,1,0:T(8,128)(2,1)S(1)} collective-permute-done((bf16[40,32,128]{2,1,0:T(8,128)(2,1)S(1)}, bf16[40,32,128]{2,1,0:T(8,128)(2,1)S(1)}, u32[]{:S(2)}, u32[]{:S(2)}) %collective-permute-start.8) | collective-permute-done | bytes 327712 | tf_op jit(solution)/shard_map/far/ppermute | solution.py:404
  88.3 0.0 collective-permute-done.9.high_b
  88.3 1.7 %finish_0.1.refs_0_ = f32[112,64,64]{2,1,0:T(8,128)} custom-call(f32[112,32,128]{2,1,0:T(8,128)S(1)} %far_own.1.own, bf16[56,32,128]{2,1,0:T(8,128)(2,1)S(1)} %collective-permute-done.low_a, bf16[40,32,128]{2,1,0:T(8,128)(2,1)S(1)} %collective-permute-done.8.low_b, bf16[56,32,128]{2,1,0:T(8,128)(2,1)S(1)} %collective-permute-done.6.high_a, ...), custom_call_target="tpu_custom_call" | custom-call | tf_op jit(solution)/shard_map/finish/finish_0/pallas_call | solution.py:378
  89.9 1.1 %collective-permute-done.5.low_b = bf16[16,32,128]{2,1,0:T(8,128)(2,1)S(1)} collective-permute-done((bf16[16,32,128]{2,1,0:T(8,128)(2,1)S(1)}, bf16[16,32,128]{2,1,0:T(8,128)(2,1)S(1)}, u32[]{:S(2)}, u32[]{:S(2)}) %collective-permute-start.5) | collective-permute-done | bytes 131104 | tf_op jit(solution)/shard_map/far/ppermute | solution.py:404
  91.1 0.0 collective-permute-done.7.high_b
  91.1 1.1 %finish_40.1 = f32[112,64,64]{2,1,0:T(8,128)} custom-call(f32[112,32,128]{2,1,0:T(8,128)S(1)} %far_own.1.own, bf16[56,32,128]{2,1,0:T(8,128)(2,1)S(1)} %collective-permute-done.low_a, bf16[16,32,128]{2,1,0:T(8,128)(2,1)S(1)} %collective-permute-done.5.low_b, bf16[56,32,128]{2,1,0:T(8,128)(2,1)S(1)} %collective-permute-done.6.high_a, ...), custom_call_target="tpu_custom_call", output_to_operand_aliasing={{}: (5, {})} | custom-call | tf_op jit(solution)/shard_map/finish/finish_40/pallas_call | solution.py:378
Async XLA Ops:
  2.8 52.8 %all-to-all-start = ((bf16[64,96,128]{2,1,0:T(8,128)(2,1)}), bf16[64,96,128]{2,1,0:T(8,128)(2,1)S(1)}, u32[]{:S(2)}, u32[]{:S(2)}) async-start(bf16[64,96,128]{2,1,0:T(8,128)(2,1)} %bitcast.22), calls=%async_computation | async-start | bytes 3145728 | tf_op jit(solution)/shard_map/exchange/all_to_all | solution.py:397
  38.8 27.8 %collective-permute-start.1 = (bf16[56,32,128]{2,1,0:T(8,128)(2,1)}, bf16[56,32,128]{2,1,0:T(8,128)(2,1)S(1)}, u32[]{:S(2)}, u32[]{:S(2)}) collective-permute-start(bf16[56,32,128]{2,1,0:T(8,128)(2,1)} %get-tuple-element.25), channel_id=1, source_target_pairs={{0,64},{64,128},{128,192},{192,0},{1,65},{65,129},{129,193},{193,1... | collective-permute-start | bytes 1376264 | tf_op jit(solution)/shard_map/early/ppermute | solution.py:404
  40.1 26.5 %collective-permute-start.3 = (bf16[56,32,128]{2,1,0:T(8,128)(2,1)}, bf16[56,32,128]{2,1,0:T(8,128)(2,1)S(1)}, u32[]{:S(2)}, u32[]{:S(2)}) collective-permute-start(bf16[56,32,128]{2,1,0:T(8,128)(2,1)} %get-tuple-element.28), channel_id=1, source_target_pairs={{0,192},{64,0},{128,64},{192,128},{1,193},{65,1},{129,65},{193,129... | collective-permute-start | bytes 1376264 | tf_op jit(solution)/shard_map/early/ppermute | solution.py:407
  58.0 13.4 %collective-permute-start.2 = (bf16[56,32,128]{2,1,0:T(8,128)(2,1)S(1)}, bf16[56,32,128]{2,1,0:T(8,128)(2,1)S(1)}, u32[]{:S(2)}, u32[]{:S(2)}) collective-permute-start(bf16[56,32,128]{2,1,0:T(8,128)(2,1)S(1)} %get-tuple-element.26), channel_id=1, source_target_pairs={{0,64},{64,128},{128,192},{192,0},{1,65},{65,129},{129,193},{193,1... | collective-permute-start | bytes 1376264 | tf_op jit(solution)/shard_map/far/ppermute | solution.py:404
  59.4 12.0 %collective-permute-start.4 = (bf16[56,32,128]{2,1,0:T(8,128)(2,1)S(1)}, bf16[56,32,128]{2,1,0:T(8,128)(2,1)S(1)}, u32[]{:S(2)}, u32[]{:S(2)}) collective-permute-start(bf16[56,32,128]{2,1,0:T(8,128)(2,1)S(1)} %get-tuple-element.29), channel_id=1, source_target_pairs={{0,192},{64,0},{128,64},{192,128},{1,193},{65,1},{129,65},{193,129... | collective-permute-start | bytes 1376264 | tf_op jit(solution)/shard_map/far/ppermute | solution.py:407
  65.1 15.8 %collective-permute-start = (bf16[56,32,128]{2,1,0:T(8,128)(2,1)S(1)}, bf16[56,32,128]{2,1,0:T(8,128)(2,1)S(1)}, u32[]{:S(2)}, u32[]{:S(2)}) collective-permute-start(bf16[56,32,128]{2,1,0:T(8,128)(2,1)S(1)} %get-tuple-element.23), channel_id=1, source_target_pairs={{0,192},{64,0},{128,64},{192,128},{1,193},{65,1},{129,65},{193,129... | collective-permute-start | bytes 1376264 | tf_op jit(solution)/shard_map/far/ppermute | solution.py:407
  66.5 19.8 %collective-permute-start.6 = (bf16[56,32,128]{2,1,0:T(8,128)(2,1)S(1)}, bf16[56,32,128]{2,1,0:T(8,128)(2,1)S(1)}, u32[]{:S(2)}, u32[]{:S(2)}) collective-permute-start(bf16[56,32,128]{2,1,0:T(8,128)(2,1)S(1)} %get-tuple-element.31), channel_id=1, source_target_pairs={{0,64},{64,128},{128,192},{192,0},{1,65},{65,129},{129,193},{193,1... | collective-permute-start | bytes 1376264 | tf_op jit(solution)/shard_map/far/ppermute | solution.py:404
  71.7 16.6 %collective-permute-start.8 = (bf16[40,32,128]{2,1,0:T(8,128)(2,1)S(1)}, bf16[40,32,128]{2,1,0:T(8,128)(2,1)S(1)}, u32[]{:S(2)}, u32[]{:S(2)}) collective-permute-start(bf16[40,32,128]{2,1,0:T(8,128)(2,1)S(1)} %get-tuple-element.33), channel_id=1, source_target_pairs={{0,64},{64,128},{128,192},{192,0},{1,65},{65,129},{129,193},{193,1... | collective-permute-start | bytes 983048 | tf_op jit(solution)/shard_map/far/ppermute | solution.py:404
  72.7 15.6 %collective-permute-start.9 = (bf16[40,32,128]{2,1,0:T(8,128)(2,1)S(1)}, bf16[40,32,128]{2,1,0:T(8,128)(2,1)S(1)}, u32[]{:S(2)}, u32[]{:S(2)}) collective-permute-start(bf16[40,32,128]{2,1,0:T(8,128)(2,1)S(1)} %get-tuple-element.34), channel_id=1, source_target_pairs={{0,192},{64,0},{128,64},{192,128},{1,193},{65,1},{129,65},{193,129... | collective-permute-start | bytes 983048 | tf_op jit(solution)/shard_map/far/ppermute | solution.py:407
  74.4 16.6 %collective-permute-start.5 = (bf16[16,32,128]{2,1,0:T(8,128)(2,1)S(1)}, bf16[16,32,128]{2,1,0:T(8,128)(2,1)S(1)}, u32[]{:S(2)}, u32[]{:S(2)}) collective-permute-start(bf16[16,32,128]{2,1,0:T(8,128)(2,1)S(1)} %get-tuple-element.30), channel_id=1, source_target_pairs={{0,64},{64,128},{128,192},{192,0},{1,65},{65,129},{129,193},{193,1... | collective-permute-start | bytes 393224 | tf_op jit(solution)/shard_map/far/ppermute | solution.py:404
  80.9 10.2 %collective-permute-start.7 = (bf16[16,32,128]{2,1,0:T(8,128)(2,1)S(1)}, bf16[16,32,128]{2,1,0:T(8,128)(2,1)S(1)}, u32[]{:S(2)}, u32[]{:S(2)}) collective-permute-start(bf16[16,32,128]{2,1,0:T(8,128)(2,1)S(1)} %get-tuple-element.32), channel_id=1, source_target_pairs={{0,192},{64,0},{128,64},{192,128},{1,193},{65,1},{129,65},{193,129... | collective-permute-start | bytes 393224 | tf_op jit(solution)/shard_map/far/ppermute | solution.py:407

commit v6 on v5

--- a/solution.py
+++ b/solution.py
@@ -86,7 +86,7 @@
         scratch_shapes=[
             SM((3, 1, 64), jnp.int32),
             VM((4, 2, 8, 64, E), BF16),
-            VM((E * 40, 128), F32),
+            VM((E * 40 + 40, 128), F32),
             VM((FAR, 32, 128), BF16),
             pltpu.SemaphoreType.DMA((5,)),
             pltpu.SemaphoreType.DMA((CHUNKS,)),
@@ -167,14 +167,14 @@
 
     incoming[0].wait()
     transpose_slabs(two, 64, 72, wide)
-    doubled[...] = wide[...].reshape(E, 72, 128)[:, :64].astype(BF16)
+    doubled[...] = wide[: E * 72].reshape(E, 72, 128)[:, :64].astype(BF16)
     incoming[1].wait()
     for k in range(4):
         incoming[2 + k].wait()
         transpose_slabs(
             lambda i: jnp.concatenate([a_ref[k, rows_at(i, 64), :], r_ref[rows_at(i, 64), :]], 0), 64, 72, wide
         )
-        pairs[rows_at(k, E)] = wide[...].reshape(E, 72, 128)[:, :64].astype(BF16)
+        pairs[rows_at(k, E)] = wide[: E * 72].reshape(E, 72, 128)[:, :64].astype(BF16)
     pairs[4 * E] = jnp.zeros((64, 128), BF16)
 
     for part in range(4):
@@ -234,7 +234,7 @@
             VM((4096, E), BF16),
             VM((4 * E + 1, 64, 128), BF16),
             VM((E, 64, 128), BF16),
-            VM((E * 72, 128), F32),
+            VM((E * 72 + 72, 128), F32),
             VM((4, CAP, 64, 128), BF16),
             VM((4, BLOCKS, 32, 128), F32),
             VM((BLOCKS, 32, 128), BF16),

time: 92.6 us -> 92.6 us (level)
  no operation moved by 1% of the time
where the time goes in v6:
time: 92.6 us; the launch traced here: 92.4 us
  Pallas kernels  37.8 us (41%)
  waiting for transfers between devices  28.4 us (31%)
  starting transfers between devices  26 us (28%)
    pallas_call x1, Pallas kernels, near_terms(): pl.pallas_call(near_kernel, out_shape=[jax.ShapeDtypeStruct((4, CAP, 64,...  22.9 us
    all_to_all x1, waiting for transfers between devices, on_device(): lax.all_to_all(outgoing.reshape(64, 96, 128), 'dev', 0, 0, tiled=True)  14 us
    all_to_all x1, starting transfers between devices, on_device(): lax.all_to_all(outgoing.reshape(64, 96, 128), 'dev', 0, 0, tiled=True)  13 us
    ppermute x5, starting transfers between devices, to_last(): return lax.ppermute(x, 'grp', [(i, (i + 3) % 4) for i in range(4)])  9.16 us
    pallas_call x3, Pallas kernels, far_terms(): pl.pallas_call(functools.partial(far_kernel, parts, kinds), in_specs=[pl....  9.02 us
    ppermute x5, waiting for transfers between devices, to_next(): return lax.ppermute(x, 'grp', [(i, (i + 1) % 4) for i in range(4)])  7.91 us
    ppermute x5, waiting for transfers between devices, to_last(): return lax.ppermute(x, 'grp', [(i, (i + 3) % 4) for i in range(4)])  6.43 us
    ppermute x5, starting transfers between devices, to_next(): return lax.ppermute(x, 'grp', [(i, (i + 1) % 4) for i in range(4)])  3.82 us
  transfers between devices with their start and end apart: 11, of which 5 were waited for; matrix products, arithmetic and copies ran while one was open for 0% of the time, Pallas kernels for 37%

profile of v6, /device:TPU:1, one launch (start us, length us, event | category | flops | bytes accessed | tf_op | source)
XLA Modules:
  0.0 92.4 jit_solution(2794882770296591615)
XLA Ops:
  0.0 2.8 %send_blocks.1 = bf16[192,32,128]{2,1,0:T(8,128)(2,1)} custom-call(s32[3,1,64]{2,1,0:T(1,128)} %bitcast.29, bf16[2,32,64,128]{3,2,1,0:T(8,128)(2,1)} %bitcast.24), custom_call_target="tpu_custom_call" | custom-call | tf_op jit(solution)/shard_map/exchange/send_blocks/pallas_call | solution.py:81
  2.8 13.0 %all-to-all-start = ((bf16[64,96,128]{2,1,0:T(8,128)(2,1)}), bf16[64,96,128]{2,1,0:T(8,128)(2,1)S(1)}, u32[]{:S(2)}, u32[]{:S(2)}) async-start(bf16[64,96,128]{2,1,0:T(8,128)(2,1)} %bitcast.22), calls=%async_computation | async-start | bytes 3145728 | tf_op jit(solution)/shard_map/exchange/all_to_all | solution.py:397
  15.8 22.9 %near_terms.1 = (bf16[4,96,64,128]{3,2,1,0:T(8,128)(2,1)}, f32[4,112,32,128]{3,2,1,0:T(8,128)}, bf16[56,32,128]{2,1,0:T(8,128)(2,1)}, bf16[56,32,128]{2,1,0:T(8,128)(2,1)}, s32[3145728]{0:T(1024)}) custom-call(s32[1]{0:T(128)} %bitcast.me, s32[3,128]{1,0:T(4,128)} %bitcast.27, s32[4,128]{1,0:T(4,128)} %bitcast.28, s32[1,128]{1,0:T(1,128)} %bitcast.30, ...), custom_call_target="tpu_custom_call" | custom-call | flops 700000000 | bytes 40000000 | tf_op jit(solution)/shard_map/near/near_terms/pallas_call | solution.py:220
  38.8 1.4 %collective-permute-start.1 = (bf16[56,32,128]{2,1,0:T(8,128)(2,1)}, bf16[56,32,128]{2,1,0:T(8,128)(2,1)S(1)}, u32[]{:S(2)}, u32[]{:S(2)}) collective-permute-start(bf16[56,32,128]{2,1,0:T(8,128)(2,1)} %get-tuple-element.25), channel_id=1, source_target_pairs={{0,64},{64,128},{128,192},{192,0},{1,65},{65,129},{129,193},{193,1... | collective-permute-start | bytes 1376264 | tf_op jit(solution)/shard_map/early/ppermute | solution.py:404
  40.1 1.5 %collective-permute-start.3 = (bf16[56,32,128]{2,1,0:T(8,128)(2,1)}, bf16[56,32,128]{2,1,0:T(8,128)(2,1)S(1)}, u32[]{:S(2)}, u32[]{:S(2)}) collective-permute-start(bf16[56,32,128]{2,1,0:T(8,128)(2,1)} %get-tuple-element.28), channel_id=1, source_target_pairs={{0,192},{64,0},{128,64},{192,128},{1,193},{65,1},{129,65},{193,129... | collective-permute-start | bytes 1376264 | tf_op jit(solution)/shard_map/early/ppermute | solution.py:407
  41.6 14.0 %all-to-all-done = bf16[64,96,128]{2,1,0:T(8,128)(2,1)S(1)} async-done(((bf16[64,96,128]{2,1,0:T(8,128)(2,1)}), bf16[64,96,128]{2,1,0:T(8,128)(2,1)S(1)}, u32[]{:S(2)}, u32[]{:S(2)}) %all-to-all-start) | async-done | bytes 1572896 | tf_op jit(solution)/shard_map/exchange/all_to_all | solution.py:397
  55.6 2.4 %far_two.1 = (bf16[56,32,128]{2,1,0:T(8,128)(2,1)S(1)}, bf16[56,32,128]{2,1,0:T(8,128)(2,1)S(1)}) custom-call(s32[3145728]{0:T(1024)} %get-tuple-element.20.plan_in, bf16[192,32,128]{2,1,0:T(8,128)(2,1)S(1)} %bitcast.19, bf16[4,96,64,128]{3,2,1,0:T(8,128)(2,1)} %get-tuple-element.21.refs_0_, f32[4,112,32,128]{3,2,1,0:T(8,128)} %get-tuple-element.22.refs_1_), custom_call_target="tpu_custom_call" | custom-call | flops 100000000 | bytes 6000000 | tf_op jit(solution)/shard_map/far/far_two/pallas_call | solution.py:320
  58.0 1.4 %collective-permute-start.2 = (bf16[56,32,128]{2,1,0:T(8,128)(2,1)S(1)}, bf16[56,32,128]{2,1,0:T(8,128)(2,1)S(1)}, u32[]{:S(2)}, u32[]{:S(2)}) collective-permute-start(bf16[56,32,128]{2,1,0:T(8,128)(2,1)S(1)} %get-tuple-element.26), channel_id=1, source_target_pairs={{0,64},{64,128},{128,192},{192,0},{1,65},{65,129},{129,193},{193,1... | collective-permute-start | bytes 1376264 | tf_op jit(solution)/shard_map/far/ppermute | solution.py:404
  59.4 1.5 %collective-permute-start.4 = (bf16[56,32,128]{2,1,0:T(8,128)(2,1)S(1)}, bf16[56,32,128]{2,1,0:T(8,128)(2,1)S(1)}, u32[]{:S(2)}, u32[]{:S(2)}) collective-permute-start(bf16[56,32,128]{2,1,0:T(8,128)(2,1)S(1)} %get-tuple-element.29), channel_id=1, source_target_pairs={{0,192},{64,0},{128,64},{192,128},{1,193},{65,1},{129,65},{193,129... | collective-permute-start | bytes 1376264 | tf_op jit(solution)/shard_map/far/ppermute | solution.py:407
  60.9 4.1 %far_one.1 = (f32[56,32,128]{2,1,0:T(8,128)S(1)}, bf16[56,32,128]{2,1,0:T(8,128)(2,1)S(1)}, bf16[56,32,128]{2,1,0:T(8,128)(2,1)S(1)}, f32[56,32,128]{2,1,0:T(8,128)S(1)}) custom-call(s32[3145728]{0:T(1024)} %get-tuple-element.20.plan_in, bf16[192,32,128]{2,1,0:T(8,128)(2,1)S(1)} %bitcast.20, bf16[4,96,64,128]{3,2,1,0:T(8,128)(2,1)} %get-tuple-element.21.refs_0_, ...), custom_call_target="tpu_custom_call" | custom-call | flops 100000000 | bytes 6000000 | tf_op jit(solution)/shard_map/far/far_one/pallas_call | solution.py:320
  65.1 1.5 %collective-permute-start = (bf16[56,32,128]{2,1,0:T(8,128)(2,1)S(1)}, bf16[56,32,128]{2,1,0:T(8,128)(2,1)S(1)}, u32[]{:S(2)}, u32[]{:S(2)}) collective-permute-start(bf16[56,32,128]{2,1,0:T(8,128)(2,1)S(1)} %get-tuple-element.23), channel_id=1, source_target_pairs={{0,192},{64,0},{128,64},{192,128},{1,193},{65,1},{129,65},{193,129... | collective-permute-start | bytes 1376264 | tf_op jit(solution)/shard_map/far/ppermute | solution.py:407
  66.5 0.0 collective-permute-done.1.early_a
  66.5 0.1 collective-permute-start.6
  66.6 0.0 collective-permute-done.3.early_b
  66.6 4.8 %collective-permute-done.2.passed_a = bf16[56,32,128]{2,1,0:T(8,128)(2,1)S(1)} collective-permute-done((bf16[56,32,128]{2,1,0:T(8,128)(2,1)S(1)}, bf16[56,32,128]{2,1,0:T(8,128)(2,1)S(1)}, u32[]{:S(2)}, u32[]{:S(2)}) %collective-permute-start.2) | collective-permute-done | bytes 458784 | tf_op jit(solution)/shard_map/far/ppermute | solution.py:404
  71.4 0.0 collective-permute-done.4.passed_b
  71.4 0.3 add_passed.1
  71.7 1.0 %collective-permute-start.8 = (bf16[40,32,128]{2,1,0:T(8,128)(2,1)S(1)}, bf16[40,32,128]{2,1,0:T(8,128)(2,1)S(1)}, u32[]{:S(2)}, u32[]{:S(2)}) collective-permute-start(bf16[40,32,128]{2,1,0:T(8,128)(2,1)S(1)} %get-tuple-element.33), channel_id=1, source_target_pairs={{0,64},{64,128},{128,192},{192,0},{1,65},{65,129},{129,193},{193,1... | collective-permute-start | bytes 983048 | tf_op jit(solution)/shard_map/far/ppermute | solution.py:404
  72.7 1.7 %collective-permute-start.9 = (bf16[40,32,128]{2,1,0:T(8,128)(2,1)S(1)}, bf16[40,32,128]{2,1,0:T(8,128)(2,1)S(1)}, u32[]{:S(2)}, u32[]{:S(2)}) collective-permute-start(bf16[40,32,128]{2,1,0:T(8,128)(2,1)S(1)} %get-tuple-element.34), channel_id=1, source_target_pairs={{0,192},{64,0},{128,64},{192,128},{1,193},{65,1},{129,65},{193,129... | collective-permute-start | bytes 983048 | tf_op jit(solution)/shard_map/far/ppermute | solution.py:407
  74.5 0.0 collective-permute-start.5
  74.5 6.4 %collective-permute-done.low_a = bf16[56,32,128]{2,1,0:T(8,128)(2,1)S(1)} collective-permute-done((bf16[56,32,128]{2,1,0:T(8,128)(2,1)S(1)}, bf16[56,32,128]{2,1,0:T(8,128)(2,1)S(1)}, u32[]{:S(2)}, u32[]{:S(2)}) %collective-permute-start) | collective-permute-done | bytes 458784 | tf_op jit(solution)/shard_map/far/ppermute | solution.py:407
  80.9 2.9 %collective-permute-start.7 = (bf16[16,32,128]{2,1,0:T(8,128)(2,1)S(1)}, bf16[16,32,128]{2,1,0:T(8,128)(2,1)S(1)}, u32[]{:S(2)}, u32[]{:S(2)}) collective-permute-start(bf16[16,32,128]{2,1,0:T(8,128)(2,1)S(1)} %get-tuple-element.32), channel_id=1, source_target_pairs={{0,192},{64,0},{128,64},{192,128},{1,193},{65,1},{129,65},{193,129... | collective-permute-start | bytes 393224 | tf_op jit(solution)/shard_map/far/ppermute | solution.py:407
  83.8 2.5 %far_own.1.own = f32[112,32,128]{2,1,0:T(8,128)S(1)} custom-call(s32[3145728]{0:T(1024)} %get-tuple-element.20.plan_in, bf16[192,32,128]{2,1,0:T(8,128)(2,1)S(1)} %bitcast.21, bf16[4,96,64,128]{3,2,1,0:T(8,128)(2,1)} %get-tuple-element.21.refs_0_, f32[4,112,32,128]{3,2,1,0:T(8,128)} %get-tuple-element.22.refs_1_), custom_call_target="tpu_custom_call" | custom-call | flops 100000000 | bytes 6000000 | tf_op jit(solution)/shard_map/far/far_own/pallas_call | solution.py:320
  86.3 0.0 collective-permute-done.6.high_a
  86.3 2.0 %collective-permute-done.8.low_b = bf16[40,32,128]{2,1,0:T(8,128)(2,1)S(1)} collective-permute-done((bf16[40,32,128]{2,1,0:T(8,128)(2,1)S(1)}, bf16[40,32,128]{2,1,0:T(8,128)(2,1)S(1)}, u32[]{:S(2)}, u32[]{:S(2)}) %collective-permute-start.8) | collective-permute-done | bytes 327712 | tf_op jit(solution)/shard_map/far/ppermute | solution.py:404
  88.3 0.0 collective-permute-done.9.high_b
  88.3 1.7 %finish_0.1.refs_0_ = f32[112,64,64]{2,1,0:T(8,128)} custom-call(f32[112,32,128]{2,1,0:T(8,128)S(1)} %far_own.1.own, bf16[56,32,128]{2,1,0:T(8,128)(2,1)S(1)} %collective-permute-done.low_a, bf16[40,32,128]{2,1,0:T(8,128)(2,1)S(1)} %collective-permute-done.8.low_b, bf16[56,32,128]{2,1,0:T(8,128)(2,1)S(1)} %collective-permute-done.6.high_a, ...), custom_call_target="tpu_custom_call" | custom-call | tf_op jit(solution)/shard_map/finish/finish_0/pallas_call | solution.py:378
  90.0 1.1 %collective-permute-done.5.low_b = bf16[16,32,128]{2,1,0:T(8,128)(2,1)S(1)} collective-permute-done((bf16[16,32,128]{2,1,0:T(8,128)(2,1)S(1)}, bf16[16,32,128]{2,1,0:T(8,128)(2,1)S(1)}, u32[]{:S(2)}, u32[]{:S(2)}) %collective-permute-start.5) | collective-permute-done | bytes 131104 | tf_op jit(solution)/shard_map/far/ppermute | solution.py:404
  91.1 0.0 collective-permute-done.7.high_b
  91.1 1.1 %finish_40.1 = f32[112,64,64]{2,1,0:T(8,128)} custom-call(f32[112,32,128]{2,1,0:T(8,128)S(1)} %far_own.1.own, bf16[56,32,128]{2,1,0:T(8,128)(2,1)S(1)} %collective-permute-done.low_a, bf16[16,32,128]{2,1,0:T(8,128)(2,1)S(1)} %collective-permute-done.5.low_b, bf16[56,32,128]{2,1,0:T(8,128)(2,1)S(1)} %collective-permute-done.6.high_a, ...), custom_call_target="tpu_custom_call", output_to_operand_aliasing={{}: (5, {})} | custom-call | tf_op jit(solution)/shard_map/finish/finish_40/pallas_call | solution.py:378
Async XLA Ops:
  2.8 52.8 %all-to-all-start = ((bf16[64,96,128]{2,1,0:T(8,128)(2,1)}), bf16[64,96,128]{2,1,0:T(8,128)(2,1)S(1)}, u32[]{:S(2)}, u32[]{:S(2)}) async-start(bf16[64,96,128]{2,1,0:T(8,128)(2,1)} %bitcast.22), calls=%async_computation | async-start | bytes 3145728 | tf_op jit(solution)/shard_map/exchange/all_to_all | solution.py:397
  38.8 27.8 %collective-permute-start.1 = (bf16[56,32,128]{2,1,0:T(8,128)(2,1)}, bf16[56,32,128]{2,1,0:T(8,128)(2,1)S(1)}, u32[]{:S(2)}, u32[]{:S(2)}) collective-permute-start(bf16[56,32,128]{2,1,0:T(8,128)(2,1)} %get-tuple-element.25), channel_id=1, source_target_pairs={{0,64},{64,128},{128,192},{192,0},{1,65},{65,129},{129,193},{193,1... | collective-permute-start | bytes 1376264 | tf_op jit(solution)/shard_map/early/ppermute | solution.py:404
  40.1 26.5 %collective-permute-start.3 = (bf16[56,32,128]{2,1,0:T(8,128)(2,1)}, bf16[56,32,128]{2,1,0:T(8,128)(2,1)S(1)}, u32[]{:S(2)}, u32[]{:S(2)}) collective-permute-start(bf16[56,32,128]{2,1,0:T(8,128)(2,1)} %get-tuple-element.28), channel_id=1, source_target_pairs={{0,192},{64,0},{128,64},{192,128},{1,193},{65,1},{129,65},{193,129... | collective-permute-start | bytes 1376264 | tf_op jit(solution)/shard_map/early/ppermute | solution.py:407
  58.0 13.4 %collective-permute-start.2 = (bf16[56,32,128]{2,1,0:T(8,128)(2,1)S(1)}, bf16[56,32,128]{2,1,0:T(8,128)(2,1)S(1)}, u32[]{:S(2)}, u32[]{:S(2)}) collective-permute-start(bf16[56,32,128]{2,1,0:T(8,128)(2,1)S(1)} %get-tuple-element.26), channel_id=1, source_target_pairs={{0,64},{64,128},{128,192},{192,0},{1,65},{65,129},{129,193},{193,1... | collective-permute-start | bytes 1376264 | tf_op jit(solution)/shard_map/far/ppermute | solution.py:404
  59.4 12.0 %collective-permute-start.4 = (bf16[56,32,128]{2,1,0:T(8,128)(2,1)S(1)}, bf16[56,32,128]{2,1,0:T(8,128)(2,1)S(1)}, u32[]{:S(2)}, u32[]{:S(2)}) collective-permute-start(bf16[56,32,128]{2,1,0:T(8,128)(2,1)S(1)} %get-tuple-element.29), channel_id=1, source_target_pairs={{0,192},{64,0},{128,64},{192,128},{1,193},{65,1},{129,65},{193,129... | collective-permute-start | bytes 1376264 | tf_op jit(solution)/shard_map/far/ppermute | solution.py:407
  65.1 15.8 %collective-permute-start = (bf16[56,32,128]{2,1,0:T(8,128)(2,1)S(1)}, bf16[56,32,128]{2,1,0:T(8,128)(2,1)S(1)}, u32[]{:S(2)}, u32[]{:S(2)}) collective-permute-start(bf16[56,32,128]{2,1,0:T(8,128)(2,1)S(1)} %get-tuple-element.23), channel_id=1, source_target_pairs={{0,192},{64,0},{128,64},{192,128},{1,193},{65,1},{129,65},{193,129... | collective-permute-start | bytes 1376264 | tf_op jit(solution)/shard_map/far/ppermute | solution.py:407
  66.5 19.8 %collective-permute-start.6 = (bf16[56,32,128]{2,1,0:T(8,128)(2,1)S(1)}, bf16[56,32,128]{2,1,0:T(8,128)(2,1)S(1)}, u32[]{:S(2)}, u32[]{:S(2)}) collective-permute-start(bf16[56,32,128]{2,1,0:T(8,128)(2,1)S(1)} %get-tuple-element.31), channel_id=1, source_target_pairs={{0,64},{64,128},{128,192},{192,0},{1,65},{65,129},{129,193},{193,1... | collective-permute-start | bytes 1376264 | tf_op jit(solution)/shard_map/far/ppermute | solution.py:404
  71.7 16.6 %collective-permute-start.8 = (bf16[40,32,128]{2,1,0:T(8,128)(2,1)S(1)}, bf16[40,32,128]{2,1,0:T(8,128)(2,1)S(1)}, u32[]{:S(2)}, u32[]{:S(2)}) collective-permute-start(bf16[40,32,128]{2,1,0:T(8,128)(2,1)S(1)} %get-tuple-element.33), channel_id=1, source_target_pairs={{0,64},{64,128},{128,192},{192,0},{1,65},{65,129},{129,193},{193,1... | collective-permute-start | bytes 983048 | tf_op jit(solution)/shard_map/far/ppermute | solution.py:404
  72.7 15.6 %collective-permute-start.9 = (bf16[40,32,128]{2,1,0:T(8,128)(2,1)S(1)}, bf16[40,32,128]{2,1,0:T(8,128)(2,1)S(1)}, u32[]{:S(2)}, u32[]{:S(2)}) collective-permute-start(bf16[40,32,128]{2,1,0:T(8,128)(2,1)S(1)} %get-tuple-element.34), channel_id=1, source_target_pairs={{0,192},{64,0},{128,64},{192,128},{1,193},{65,1},{129,65},{193,129... | collective-permute-start | bytes 983048 | tf_op jit(solution)/shard_map/far/ppermute | solution.py:407
  74.5 16.6 %collective-permute-start.5 = (bf16[16,32,128]{2,1,0:T(8,128)(2,1)S(1)}, bf16[16,32,128]{2,1,0:T(8,128)(2,1)S(1)}, u32[]{:S(2)}, u32[]{:S(2)}) collective-permute-start(bf16[16,32,128]{2,1,0:T(8,128)(2,1)S(1)} %get-tuple-element.30), channel_id=1, source_target_pairs={{0,64},{64,128},{128,192},{192,0},{1,65},{65,129},{129,193},{193,1... | collective-permute-start | bytes 393224 | tf_op jit(solution)/shard_map/far/ppermute | solution.py:404
  80.9 10.2 %collective-permute-start.7 = (bf16[16,32,128]{2,1,0:T(8,128)(2,1)S(1)}, bf16[16,32,128]{2,1,0:T(8,128)(2,1)S(1)}, u32[]{:S(2)}, u32[]{:S(2)}) collective-permute-start(bf16[16,32,128]{2,1,0:T(8,128)(2,1)S(1)} %get-tuple-element.32), channel_id=1, source_target_pairs={{0,192},{64,0},{128,64},{192,128},{1,193},{65,1},{129,65},{193,129... | collective-permute-start | bytes 393224 | tf_op jit(solution)/shard_map/far/ppermute | solution.py:407

commit v7 on v6

--- a/solution.py
+++ b/solution.py
@@ -21,13 +21,14 @@
 BLOCKS = ROWS * SLOTS
 HALF = BLOCKS // 2
 FAR = 192
-CAP = 3 * SPAN
+CAP = 128
 GROUP = 32
-GROUPS = CAP // GROUP
+FAR_GROUP = 64
+GROUPS = CAP // FAR_GROUP
 CHUNKS = 4
-SURE = 2
+SURE = 1
 FIRST = 40
-AREA = CAP + GROUP
+AREA = CAP
 SUMS = 4 * AREA
 COUNTS = 8 * AREA
 PLAN = COUNTS + 1024
@@ -148,7 +149,7 @@
             plan[SUMS + part * AREA + i] = 0
             return carry
 
-        lax.fori_loop(far_counts[-1], (far_counts[-1] + GROUP - 1) // GROUP * GROUP, pad_far, 0)
+        lax.fori_loop(far_counts[-1], (far_counts[-1] + FAR_GROUP - 1) // FAR_GROUP * FAR_GROUP, pad_far, 0)
 
         def pad_near(i, carry):
             near_pairs[part * NEAR_AREA + i] = 4 * E
@@ -190,7 +191,7 @@
             far_pairs[part, i] = jnp.zeros((64, 128), BF16)
             return carry
 
-        lax.fori_loop(many, (many + GROUP - 1) // GROUP * GROUP, clear, 0)
+        lax.fori_loop(many, (many + FAR_GROUP - 1) // FAR_GROUP * FAR_GROUP, clear, 0)
         copies.append(pltpu.make_async_copy(far_pairs.at[part], far_pairs_out.at[part], written.at[part]))
         copies[-1].start()
         sums[part] = jnp.zeros((BLOCKS, 32, 128), F32)
@@ -260,7 +261,7 @@
     low = lax.broadcasted_iota(jnp.int32, (32, 128), 1) < 64
 
     def pairs_copy(n, g):
-        some = pl.ds(g * GROUP, GROUP)
+        some = pl.ds(g * FAR_GROUP, FAR_GROUP)
         return pltpu.make_async_copy(pairs_in.at[parts[n], some], pairs.at[n, some], arrived.at[n, g])
 
     def near_copy(n):
@@ -280,7 +281,7 @@
     for n, part in enumerate(parts):
         for g in range(SURE, GROUPS):
 
-            @pl.when(plan[COUNTS + part] > g * GROUP)
+            @pl.when(plan[COUNTS + part] > g * FAR_GROUP)
             def _(n=n, g=g):
                 pairs_copy(n, g).start()
 
@@ -288,13 +289,13 @@
     for n, part in enumerate(parts):
         sums[...] = jnp.zeros_like(sums)
         start = part * AREA
-        groups = (plan[COUNTS + part] + GROUP - 1) // GROUP
+        groups = (plan[COUNTS + part] + FAR_GROUP - 1) // FAR_GROUP
 
         def group(g, carry):
-            at = g * GROUP
+            at = g * FAR_GROUP
             pairs_copy(n, g).wait()
-            found = [term_of(pairs[n, at + u], doubled(plan[start + at + u])) for u in range(GROUP)]
-            for u in range(GROUP):
+            found = [term_of(pairs[n, at + u], doubled(plan[start + at + u])) for u in range(FAR_GROUP)]
+            for u in range(FAR_GROUP):
                 sums[plan[SUMS + start + at + u]] += found[u]
             return carry
 

time: 92.6 us -> 92.5 us (level)
  transfers between devices with their start and end apart: 11 -> 11, of which waited for: 5 -> 5; matrix products, arithmetic and copies ran while one was open for 0% -> 0% of each run, Pallas kernels for 37% -> 36%
where the time goes in v7:
time: 92.5 us; the launch traced here: 92.2 us
  Pallas kernels  37 us (40%)
  waiting for transfers between devices  29 us (31%)
  starting transfers between devices  25.9 us (28%)
    pallas_call x1, Pallas kernels, near_terms(): pl.pallas_call(near_kernel, out_shape=[jax.ShapeDtypeStruct((4, CAP, 64,...  22.9 us
    all_to_all x1, waiting for transfers between devices, on_device(): lax.all_to_all(outgoing.reshape(64, 96, 128), 'dev', 0, 0, tiled=True)  14 us
    all_to_all x1, starting transfers between devices, on_device(): lax.all_to_all(outgoing.reshape(64, 96, 128), 'dev', 0, 0, tiled=True)  13 us
    ppermute x5, starting transfers between devices, to_last(): return lax.ppermute(x, 'grp', [(i, (i + 3) % 4) for i in range(4)])  9.09 us
    ppermute x5, waiting for transfers between devices, to_next(): return lax.ppermute(x, 'grp', [(i, (i + 1) % 4) for i in range(4)])  8.52 us
    pallas_call x3, Pallas kernels, far_terms(): pl.pallas_call(functools.partial(far_kernel, parts, kinds), in_specs=[pl....  8.24 us
    ppermute x5, waiting for transfers between devices, to_last(): return lax.ppermute(x, 'grp', [(i, (i + 3) % 4) for i in range(4)])  6.45 us
    ppermute x5, starting transfers between devices, to_next(): return lax.ppermute(x, 'grp', [(i, (i + 1) % 4) for i in range(4)])  3.86 us
  transfers between devices with their start and end apart: 11, of which 5 were waited for; matrix products, arithmetic and copies ran while one was open for 0% of the time, Pallas kernels for 36%

profile of v7, /device:TPU:1, one launch (start us, length us, event | category | flops | bytes accessed | tf_op | source)
XLA Modules:
  0.0 92.2 jit_solution(2302603248822608726)
XLA Ops:
  0.0 2.8 %send_blocks.1 = bf16[192,32,128]{2,1,0:T(8,128)(2,1)} custom-call(s32[3,1,64]{2,1,0:T(1,128)} %bitcast.29, bf16[2,32,64,128]{3,2,1,0:T(8,128)(2,1)} %bitcast.24), custom_call_target="tpu_custom_call" | custom-call | tf_op jit(solution)/shard_map/exchange/send_blocks/pallas_call | solution.py:82
  2.8 13.0 %all-to-all-start = ((bf16[64,96,128]{2,1,0:T(8,128)(2,1)}), bf16[64,96,128]{2,1,0:T(8,128)(2,1)S(1)}, u32[]{:S(2)}, u32[]{:S(2)}) async-start(bf16[64,96,128]{2,1,0:T(8,128)(2,1)} %bitcast.22), calls=%async_computation | async-start | bytes 3145728 | tf_op jit(solution)/shard_map/exchange/all_to_all | solution.py:398
  15.8 22.9 %near_terms.1 = (bf16[4,128,64,128]{3,2,1,0:T(8,128)(2,1)}, f32[4,112,32,128]{3,2,1,0:T(8,128)}, bf16[56,32,128]{2,1,0:T(8,128)(2,1)}, bf16[56,32,128]{2,1,0:T(8,128)(2,1)}, s32[3145728]{0:T(1024)}) custom-call(s32[1]{0:T(128)} %bitcast.me, s32[3,128]{1,0:T(4,128)} %bitcast.27, s32[4,128]{1,0:T(4,128)} %bitcast.28, s32[1,128]{1,0:T(1,128)} %bitcast.30, ...), custom_call_target="tpu_custom_call" | custom-call | flops 700000000 | bytes 40000000 | tf_op jit(solution)/shard_map/near/near_terms/pallas_call | solution.py:221
  38.7 1.4 %collective-permute-start.1 = (bf16[56,32,128]{2,1,0:T(8,128)(2,1)}, bf16[56,32,128]{2,1,0:T(8,128)(2,1)S(1)}, u32[]{:S(2)}, u32[]{:S(2)}) collective-permute-start(bf16[56,32,128]{2,1,0:T(8,128)(2,1)} %get-tuple-element.25), channel_id=1, source_target_pairs={{0,64},{64,128},{128,192},{192,0},{1,65},{65,129},{129,193},{193,1... | collective-permute-start | bytes 1376264 | tf_op jit(solution)/shard_map/early/ppermute | solution.py:405
  40.1 1.5 %collective-permute-start.3 = (bf16[56,32,128]{2,1,0:T(8,128)(2,1)}, bf16[56,32,128]{2,1,0:T(8,128)(2,1)S(1)}, u32[]{:S(2)}, u32[]{:S(2)}) collective-permute-start(bf16[56,32,128]{2,1,0:T(8,128)(2,1)} %get-tuple-element.28), channel_id=1, source_target_pairs={{0,192},{64,0},{128,64},{192,128},{1,193},{65,1},{129,65},{193,129... | collective-permute-start | bytes 1376264 | tf_op jit(solution)/shard_map/early/ppermute | solution.py:408
  41.6 14.0 %all-to-all-done = bf16[64,96,128]{2,1,0:T(8,128)(2,1)S(1)} async-done(((bf16[64,96,128]{2,1,0:T(8,128)(2,1)}), bf16[64,96,128]{2,1,0:T(8,128)(2,1)S(1)}, u32[]{:S(2)}, u32[]{:S(2)}) %all-to-all-start) | async-done | bytes 1572896 | tf_op jit(solution)/shard_map/exchange/all_to_all | solution.py:398
  55.6 2.2 %far_two.1 = (bf16[56,32,128]{2,1,0:T(8,128)(2,1)S(1)}, bf16[56,32,128]{2,1,0:T(8,128)(2,1)S(1)}) custom-call(s32[3145728]{0:T(1024)} %get-tuple-element.20.plan_in, bf16[192,32,128]{2,1,0:T(8,128)(2,1)S(1)} %bitcast.19, bf16[4,128,64,128]{3,2,1,0:T(8,128)(2,1)} %get-tuple-element.21.refs_0_, f32[4,112,32,128]{3,2,1,0:T(8,128)} %get-tuple-element.22.refs_1_), custom_call_target="tpu_custom_call" | custom-call | flops 100000000 | bytes 6000000 | tf_op jit(solution)/shard_map/far/far_two/pallas_call | solution.py:321
  57.9 1.4 %collective-permute-start.2 = (bf16[56,32,128]{2,1,0:T(8,128)(2,1)S(1)}, bf16[56,32,128]{2,1,0:T(8,128)(2,1)S(1)}, u32[]{:S(2)}, u32[]{:S(2)}) collective-permute-start(bf16[56,32,128]{2,1,0:T(8,128)(2,1)S(1)} %get-tuple-element.26), channel_id=1, source_target_pairs={{0,64},{64,128},{128,192},{192,0},{1,65},{65,129},{129,193},{193,1... | collective-permute-start | bytes 1376264 | tf_op jit(solution)/shard_map/far/ppermute | solution.py:405
  59.3 1.5 %collective-permute-start.4 = (bf16[56,32,128]{2,1,0:T(8,128)(2,1)S(1)}, bf16[56,32,128]{2,1,0:T(8,128)(2,1)S(1)}, u32[]{:S(2)}, u32[]{:S(2)}) collective-permute-start(bf16[56,32,128]{2,1,0:T(8,128)(2,1)S(1)} %get-tuple-element.29), channel_id=1, source_target_pairs={{0,192},{64,0},{128,64},{192,128},{1,193},{65,1},{129,65},{193,129... | collective-permute-start | bytes 1376264 | tf_op jit(solution)/shard_map/far/ppermute | solution.py:408
  60.8 3.7 %far_one.1 = (f32[56,32,128]{2,1,0:T(8,128)S(1)}, bf16[56,32,128]{2,1,0:T(8,128)(2,1)S(1)}, bf16[56,32,128]{2,1,0:T(8,128)(2,1)S(1)}, f32[56,32,128]{2,1,0:T(8,128)S(1)}) custom-call(s32[3145728]{0:T(1024)} %get-tuple-element.20.plan_in, bf16[192,32,128]{2,1,0:T(8,128)(2,1)S(1)} %bitcast.20, bf16[4,128,64,128]{3,2,1,0:T(8,128)(2,1)} %get-tuple-element.21.refs_0_, ...), custom_call_target="tpu_custom_call" | custom-call | flops 100000000 | bytes 6000000 | tf_op jit(solution)/shard_map/far/far_one/pallas_call | solution.py:321
  64.4 1.5 %collective-permute-start = (bf16[56,32,128]{2,1,0:T(8,128)(2,1)S(1)}, bf16[56,32,128]{2,1,0:T(8,128)(2,1)S(1)}, u32[]{:S(2)}, u32[]{:S(2)}) collective-permute-start(bf16[56,32,128]{2,1,0:T(8,128)(2,1)S(1)} %get-tuple-element.23), channel_id=1, source_target_pairs={{0,192},{64,0},{128,64},{192,128},{1,193},{65,1},{129,65},{193,129... | collective-permute-start | bytes 1376264 | tf_op jit(solution)/shard_map/far/ppermute | solution.py:408
  65.9 0.0 collective-permute-done.1.early_a
  65.9 0.1 collective-permute-start.6
  66.0 0.0 collective-permute-done.3.early_b
  66.0 5.3 %collective-permute-done.2.passed_a = bf16[56,32,128]{2,1,0:T(8,128)(2,1)S(1)} collective-permute-done((bf16[56,32,128]{2,1,0:T(8,128)(2,1)S(1)}, bf16[56,32,128]{2,1,0:T(8,128)(2,1)S(1)}, u32[]{:S(2)}, u32[]{:S(2)}) %collective-permute-start.2) | collective-permute-done | bytes 458784 | tf_op jit(solution)/shard_map/far/ppermute | solution.py:405
  71.3 0.0 collective-permute-done.4.passed_b
  71.3 0.3 add_passed.1
  71.5 1.0 %collective-permute-start.8 = (bf16[40,32,128]{2,1,0:T(8,128)(2,1)S(1)}, bf16[40,32,128]{2,1,0:T(8,128)(2,1)S(1)}, u32[]{:S(2)}, u32[]{:S(2)}) collective-permute-start(bf16[40,32,128]{2,1,0:T(8,128)(2,1)S(1)} %get-tuple-element.33), channel_id=1, source_target_pairs={{0,64},{64,128},{128,192},{192,0},{1,65},{65,129},{129,193},{193,1... | collective-permute-start | bytes 983048 | tf_op jit(solution)/shard_map/far/ppermute | solution.py:405
  72.6 1.7 %collective-permute-start.9 = (bf16[40,32,128]{2,1,0:T(8,128)(2,1)S(1)}, bf16[40,32,128]{2,1,0:T(8,128)(2,1)S(1)}, u32[]{:S(2)}, u32[]{:S(2)}) collective-permute-start(bf16[40,32,128]{2,1,0:T(8,128)(2,1)S(1)} %get-tuple-element.34), channel_id=1, source_target_pairs={{0,192},{64,0},{128,64},{192,128},{1,193},{65,1},{129,65},{193,129... | collective-permute-start | bytes 983048 | tf_op jit(solution)/shard_map/far/ppermute | solution.py:408
  74.3 0.0 collective-permute-start.5
  74.3 6.4 %collective-permute-done.low_a = bf16[56,32,128]{2,1,0:T(8,128)(2,1)S(1)} collective-permute-done((bf16[56,32,128]{2,1,0:T(8,128)(2,1)S(1)}, bf16[56,32,128]{2,1,0:T(8,128)(2,1)S(1)}, u32[]{:S(2)}, u32[]{:S(2)}) %collective-permute-start) | collective-permute-done | bytes 458784 | tf_op jit(solution)/shard_map/far/ppermute | solution.py:408
  80.7 2.9 %collective-permute-start.7 = (bf16[16,32,128]{2,1,0:T(8,128)(2,1)S(1)}, bf16[16,32,128]{2,1,0:T(8,128)(2,1)S(1)}, u32[]{:S(2)}, u32[]{:S(2)}) collective-permute-start(bf16[16,32,128]{2,1,0:T(8,128)(2,1)S(1)} %get-tuple-element.32), channel_id=1, source_target_pairs={{0,192},{64,0},{128,64},{192,128},{1,193},{65,1},{129,65},{193,129... | collective-permute-start | bytes 393224 | tf_op jit(solution)/shard_map/far/ppermute | solution.py:408
  83.6 2.3 %far_own.1.own = f32[112,32,128]{2,1,0:T(8,128)S(1)} custom-call(s32[3145728]{0:T(1024)} %get-tuple-element.20.plan_in, bf16[192,32,128]{2,1,0:T(8,128)(2,1)S(1)} %bitcast.21, bf16[4,128,64,128]{3,2,1,0:T(8,128)(2,1)} %get-tuple-element.21.refs_0_, f32[4,112,32,128]{3,2,1,0:T(8,128)} %get-tuple-element.22.refs_1_), custom_call_target="tpu_custom_call" | custom-call | flops 100000000 | bytes 6000000 | tf_op jit(solution)/shard_map/far/far_own/pallas_call | solution.py:321
  86.0 0.0 collective-permute-done.6.high_a
  86.0 2.1 %collective-permute-done.8.low_b = bf16[40,32,128]{2,1,0:T(8,128)(2,1)S(1)} collective-permute-done((bf16[40,32,128]{2,1,0:T(8,128)(2,1)S(1)}, bf16[40,32,128]{2,1,0:T(8,128)(2,1)S(1)}, u32[]{:S(2)}, u32[]{:S(2)}) %collective-permute-start.8) | collective-permute-done | bytes 327712 | tf_op jit(solution)/shard_map/far/ppermute | solution.py:405
  88.1 0.0 collective-permute-done.9.high_b
  88.1 1.7 %finish_0.1.refs_0_ = f32[112,64,64]{2,1,0:T(8,128)} custom-call(f32[112,32,128]{2,1,0:T(8,128)S(1)} %far_own.1.own, bf16[56,32,128]{2,1,0:T(8,128)(2,1)S(1)} %collective-permute-done.low_a, bf16[40,32,128]{2,1,0:T(8,128)(2,1)S(1)} %collective-permute-done.8.low_b, bf16[56,32,128]{2,1,0:T(8,128)(2,1)S(1)} %collective-permute-done.6.high_a, ...), custom_call_target="tpu_custom_call" | custom-call | tf_op jit(solution)/shard_map/finish/finish_0/pallas_call | solution.py:379
  89.8 1.1 %collective-permute-done.5.low_b = bf16[16,32,128]{2,1,0:T(8,128)(2,1)S(1)} collective-permute-done((bf16[16,32,128]{2,1,0:T(8,128)(2,1)S(1)}, bf16[16,32,128]{2,1,0:T(8,128)(2,1)S(1)}, u32[]{:S(2)}, u32[]{:S(2)}) %collective-permute-start.5) | collective-permute-done | bytes 131104 | tf_op jit(solution)/shard_map/far/ppermute | solution.py:405
  90.9 0.0 collective-permute-done.7.high_b
  90.9 1.1 %finish_40.1 = f32[112,64,64]{2,1,0:T(8,128)} custom-call(f32[112,32,128]{2,1,0:T(8,128)S(1)} %far_own.1.own, bf16[56,32,128]{2,1,0:T(8,128)(2,1)S(1)} %collective-permute-done.low_a, bf16[16,32,128]{2,1,0:T(8,128)(2,1)S(1)} %collective-permute-done.5.low_b, bf16[56,32,128]{2,1,0:T(8,128)(2,1)S(1)} %collective-permute-done.6.high_a, ...), custom_call_target="tpu_custom_call", output_to_operand_aliasing={{}: (5, {})} | custom-call | tf_op jit(solution)/shard_map/finish/finish_40/pallas_call | solution.py:379
Async XLA Ops:
  2.8 52.8 %all-to-all-start = ((bf16[64,96,128]{2,1,0:T(8,128)(2,1)}), bf16[64,96,128]{2,1,0:T(8,128)(2,1)S(1)}, u32[]{:S(2)}, u32[]{:S(2)}) async-start(bf16[64,96,128]{2,1,0:T(8,128)(2,1)} %bitcast.22), calls=%async_computation | async-start | bytes 3145728 | tf_op jit(solution)/shard_map/exchange/all_to_all | solution.py:398
  38.7 27.2 %collective-permute-start.1 = (bf16[56,32,128]{2,1,0:T(8,128)(2,1)}, bf16[56,32,128]{2,1,0:T(8,128)(2,1)S(1)}, u32[]{:S(2)}, u32[]{:S(2)}) collective-permute-start(bf16[56,32,128]{2,1,0:T(8,128)(2,1)} %get-tuple-element.25), channel_id=1, source_target_pairs={{0,64},{64,128},{128,192},{192,0},{1,65},{65,129},{129,193},{193,1... | collective-permute-start | bytes 1376264 | tf_op jit(solution)/shard_map/early/ppermute | solution.py:405
  40.1 25.9 %collective-permute-start.3 = (bf16[56,32,128]{2,1,0:T(8,128)(2,1)}, bf16[56,32,128]{2,1,0:T(8,128)(2,1)S(1)}, u32[]{:S(2)}, u32[]{:S(2)}) collective-permute-start(bf16[56,32,128]{2,1,0:T(8,128)(2,1)} %get-tuple-element.28), channel_id=1, source_target_pairs={{0,192},{64,0},{128,64},{192,128},{1,193},{65,1},{129,65},{193,129... | collective-permute-start | bytes 1376264 | tf_op jit(solution)/shard_map/early/ppermute | solution.py:408
  57.9 13.4 %collective-permute-start.2 = (bf16[56,32,128]{2,1,0:T(8,128)(2,1)S(1)}, bf16[56,32,128]{2,1,0:T(8,128)(2,1)S(1)}, u32[]{:S(2)}, u32[]{:S(2)}) collective-permute-start(bf16[56,32,128]{2,1,0:T(8,128)(2,1)S(1)} %get-tuple-element.26), channel_id=1, source_target_pairs={{0,64},{64,128},{128,192},{192,0},{1,65},{65,129},{129,193},{193,1... | collective-permute-start | bytes 1376264 | tf_op jit(solution)/shard_map/far/ppermute | solution.py:405
  59.3 12.0 %collective-permute-start.4 = (bf16[56,32,128]{2,1,0:T(8,128)(2,1)S(1)}, bf16[56,32,128]{2,1,0:T(8,128)(2,1)S(1)}, u32[]{:S(2)}, u32[]{:S(2)}) collective-permute-start(bf16[56,32,128]{2,1,0:T(8,128)(2,1)S(1)} %get-tuple-element.29), channel_id=1, source_target_pairs={{0,192},{64,0},{128,64},{192,128},{1,193},{65,1},{129,65},{193,129... | collective-permute-start | bytes 1376264 | tf_op jit(solution)/shard_map/far/ppermute | solution.py:408
  64.4 16.3 %collective-permute-start = (bf16[56,32,128]{2,1,0:T(8,128)(2,1)S(1)}, bf16[56,32,128]{2,1,0:T(8,128)(2,1)S(1)}, u32[]{:S(2)}, u32[]{:S(2)}) collective-permute-start(bf16[56,32,128]{2,1,0:T(8,128)(2,1)S(1)} %get-tuple-element.23), channel_id=1, source_target_pairs={{0,192},{64,0},{128,64},{192,128},{1,193},{65,1},{129,65},{193,129... | collective-permute-start | bytes 1376264 | tf_op jit(solution)/shard_map/far/ppermute | solution.py:408
  65.9 20.1 %collective-permute-start.6 = (bf16[56,32,128]{2,1,0:T(8,128)(2,1)S(1)}, bf16[56,32,128]{2,1,0:T(8,128)(2,1)S(1)}, u32[]{:S(2)}, u32[]{:S(2)}) collective-permute-start(bf16[56,32,128]{2,1,0:T(8,128)(2,1)S(1)} %get-tuple-element.31), channel_id=1, source_target_pairs={{0,64},{64,128},{128,192},{192,0},{1,65},{65,129},{129,193},{193,1... | collective-permute-start | bytes 1376264 | tf_op jit(solution)/shard_map/far/ppermute | solution.py:405
  71.5 16.6 %collective-permute-start.8 = (bf16[40,32,128]{2,1,0:T(8,128)(2,1)S(1)}, bf16[40,32,128]{2,1,0:T(8,128)(2,1)S(1)}, u32[]{:S(2)}, u32[]{:S(2)}) collective-permute-start(bf16[40,32,128]{2,1,0:T(8,128)(2,1)S(1)} %get-tuple-element.33), channel_id=1, source_target_pairs={{0,64},{64,128},{128,192},{192,0},{1,65},{65,129},{129,193},{193,1... | collective-permute-start | bytes 983048 | tf_op jit(solution)/shard_map/far/ppermute | solution.py:405
  72.6 15.6 %collective-permute-start.9 = (bf16[40,32,128]{2,1,0:T(8,128)(2,1)S(1)}, bf16[40,32,128]{2,1,0:T(8,128)(2,1)S(1)}, u32[]{:S(2)}, u32[]{:S(2)}) collective-permute-start(bf16[40,32,128]{2,1,0:T(8,128)(2,1)S(1)} %get-tuple-element.34), channel_id=1, source_target_pairs={{0,192},{64,0},{128,64},{192,128},{1,193},{65,1},{129,65},{193,129... | collective-permute-start | bytes 983048 | tf_op jit(solution)/shard_map/far/ppermute | solution.py:408
  74.3 16.6 %collective-permute-start.5 = (bf16[16,32,128]{2,1,0:T(8,128)(2,1)S(1)}, bf16[16,32,128]{2,1,0:T(8,128)(2,1)S(1)}, u32[]{:S(2)}, u32[]{:S(2)}) collective-permute-start(bf16[16,32,128]{2,1,0:T(8,128)(2,1)S(1)} %get-tuple-element.30), channel_id=1, source_target_pairs={{0,64},{64,128},{128,192},{192,0},{1,65},{65,129},{129,193},{193,1... | collective-permute-start | bytes 393224 | tf_op jit(solution)/shard_map/far/ppermute | solution.py:405
  80.7 10.2 %collective-permute-start.7 = (bf16[16,32,128]{2,1,0:T(8,128)(2,1)S(1)}, bf16[16,32,128]{2,1,0:T(8,128)(2,1)S(1)}, u32[]{:S(2)}, u32[]{:S(2)}) collective-permute-start(bf16[16,32,128]{2,1,0:T(8,128)(2,1)S(1)} %get-tuple-element.32), channel_id=1, source_target_pairs={{0,192},{64,0},{128,64},{192,128},{1,193},{65,1},{129,65},{193,129... | collective-permute-start | bytes 393224 | tf_op jit(solution)/shard_map/far/ppermute | solution.py:408

commit v8 on v7

--- a/solution.py
+++ b/solution.py
@@ -27,7 +27,7 @@
 GROUPS = CAP // FAR_GROUP
 CHUNKS = 4
 SURE = 1
-FIRST = 40
+FIRST = 44
 AREA = CAP
 SUMS = 4 * AREA
 COUNTS = 8 * AREA

time: 92.5 us -> 92.4 us (level)
  no operation moved by 1% of the time
where the time goes in v8:
time: 92.4 us; the launch traced here: 92.1 us
  Pallas kernels  37 us (40%)
  waiting for transfers between devices  28.8 us (31%)
  starting transfers between devices  26 us (28%)
    pallas_call x1, Pallas kernels, near_terms(): pl.pallas_call(near_kernel, out_shape=[jax.ShapeDtypeStruct((4, CAP, 64,...  22.9 us
    all_to_all x1, waiting for transfers between devices, on_device(): lax.all_to_all(outgoing.reshape(64, 96, 128), 'dev', 0, 0, tiled=True)  14 us
    all_to_all x1, starting transfers between devices, on_device(): lax.all_to_all(outgoing.reshape(64, 96, 128), 'dev', 0, 0, tiled=True)  13 us
    ppermute x5, starting transfers between devices, to_last(): return lax.ppermute(x, 'grp', [(i, (i + 3) % 4) for i in range(4)])  9.17 us
    ppermute x5, waiting for transfers between devices, to_next(): return lax.ppermute(x, 'grp', [(i, (i + 1) % 4) for i in range(4)])  8.44 us
    pallas_call x3, Pallas kernels, far_terms(): pl.pallas_call(functools.partial(far_kernel, parts, kinds), in_specs=[pl....  8.24 us
    ppermute x5, waiting for transfers between devices, to_last(): return lax.ppermute(x, 'grp', [(i, (i + 3) % 4) for i in range(4)])  6.43 us
    ppermute x5, starting transfers between devices, to_next(): return lax.ppermute(x, 'grp', [(i, (i + 1) % 4) for i in range(4)])  3.86 us
  transfers between devices with their start and end apart: 11, of which 5 were waited for; matrix products, arithmetic and copies ran while one was open for 0% of the time, Pallas kernels for 36%

profile of v8, /device:TPU:1, one launch (start us, length us, event | category | flops | bytes accessed | tf_op | source)
XLA Modules:
  0.0 92.1 jit_solution(17044527394440951769)
XLA Ops:
  0.0 2.8 %send_blocks.1 = bf16[192,32,128]{2,1,0:T(8,128)(2,1)} custom-call(s32[3,1,64]{2,1,0:T(1,128)} %bitcast.29, bf16[2,32,64,128]{3,2,1,0:T(8,128)(2,1)} %bitcast.24), custom_call_target="tpu_custom_call" | custom-call | tf_op jit(solution)/shard_map/exchange/send_blocks/pallas_call | solution.py:82
  2.8 13.0 %all-to-all-start = ((bf16[64,96,128]{2,1,0:T(8,128)(2,1)}), bf16[64,96,128]{2,1,0:T(8,128)(2,1)S(1)}, u32[]{:S(2)}, u32[]{:S(2)}) async-start(bf16[64,96,128]{2,1,0:T(8,128)(2,1)} %bitcast.22), calls=%async_computation | async-start | bytes 3145728 | tf_op jit(solution)/shard_map/exchange/all_to_all | solution.py:398
  15.8 22.9 %near_terms.1 = (bf16[4,128,64,128]{3,2,1,0:T(8,128)(2,1)}, f32[4,112,32,128]{3,2,1,0:T(8,128)}, bf16[56,32,128]{2,1,0:T(8,128)(2,1)}, bf16[56,32,128]{2,1,0:T(8,128)(2,1)}, s32[3145728]{0:T(1024)}) custom-call(s32[1]{0:T(128)} %bitcast.me, s32[3,128]{1,0:T(4,128)} %bitcast.27, s32[4,128]{1,0:T(4,128)} %bitcast.28, s32[1,128]{1,0:T(1,128)} %bitcast.30, ...), custom_call_target="tpu_custom_call" | custom-call | flops 700000000 | bytes 40000000 | tf_op jit(solution)/shard_map/near/near_terms/pallas_call | solution.py:221
  38.7 1.4 %collective-permute-start.1 = (bf16[56,32,128]{2,1,0:T(8,128)(2,1)}, bf16[56,32,128]{2,1,0:T(8,128)(2,1)S(1)}, u32[]{:S(2)}, u32[]{:S(2)}) collective-permute-start(bf16[56,32,128]{2,1,0:T(8,128)(2,1)} %get-tuple-element.25), channel_id=1, source_target_pairs={{0,64},{64,128},{128,192},{192,0},{1,65},{65,129},{129,193},{193,1... | collective-permute-start | bytes 1376264 | tf_op jit(solution)/shard_map/early/ppermute | solution.py:405
  40.1 1.5 %collective-permute-start.3 = (bf16[56,32,128]{2,1,0:T(8,128)(2,1)}, bf16[56,32,128]{2,1,0:T(8,128)(2,1)S(1)}, u32[]{:S(2)}, u32[]{:S(2)}) collective-permute-start(bf16[56,32,128]{2,1,0:T(8,128)(2,1)} %get-tuple-element.28), channel_id=1, source_target_pairs={{0,192},{64,0},{128,64},{192,128},{1,193},{65,1},{129,65},{193,129... | collective-permute-start | bytes 1376264 | tf_op jit(solution)/shard_map/early/ppermute | solution.py:408
  41.7 14.0 %all-to-all-done = bf16[64,96,128]{2,1,0:T(8,128)(2,1)S(1)} async-done(((bf16[64,96,128]{2,1,0:T(8,128)(2,1)}), bf16[64,96,128]{2,1,0:T(8,128)(2,1)S(1)}, u32[]{:S(2)}, u32[]{:S(2)}) %all-to-all-start) | async-done | bytes 1572896 | tf_op jit(solution)/shard_map/exchange/all_to_all | solution.py:398
  55.6 2.2 %far_two.1 = (bf16[56,32,128]{2,1,0:T(8,128)(2,1)S(1)}, bf16[56,32,128]{2,1,0:T(8,128)(2,1)S(1)}) custom-call(s32[3145728]{0:T(1024)} %get-tuple-element.20.plan_in, bf16[192,32,128]{2,1,0:T(8,128)(2,1)S(1)} %bitcast.19, bf16[4,128,64,128]{3,2,1,0:T(8,128)(2,1)} %get-tuple-element.21.refs_0_, f32[4,112,32,128]{3,2,1,0:T(8,128)} %get-tuple-element.22.refs_1_), custom_call_target="tpu_custom_call" | custom-call | flops 100000000 | bytes 6000000 | tf_op jit(solution)/shard_map/far/far_two/pallas_call | solution.py:321
  57.9 1.4 %collective-permute-start.2 = (bf16[56,32,128]{2,1,0:T(8,128)(2,1)S(1)}, bf16[56,32,128]{2,1,0:T(8,128)(2,1)S(1)}, u32[]{:S(2)}, u32[]{:S(2)}) collective-permute-start(bf16[56,32,128]{2,1,0:T(8,128)(2,1)S(1)} %get-tuple-element.26), channel_id=1, source_target_pairs={{0,64},{64,128},{128,192},{192,0},{1,65},{65,129},{129,193},{193,1... | collective-permute-start | bytes 1376264 | tf_op jit(solution)/shard_map/far/ppermute | solution.py:405
  59.3 1.5 %collective-permute-start.4 = (bf16[56,32,128]{2,1,0:T(8,128)(2,1)S(1)}, bf16[56,32,128]{2,1,0:T(8,128)(2,1)S(1)}, u32[]{:S(2)}, u32[]{:S(2)}) collective-permute-start(bf16[56,32,128]{2,1,0:T(8,128)(2,1)S(1)} %get-tuple-element.29), channel_id=1, source_target_pairs={{0,192},{64,0},{128,64},{192,128},{1,193},{65,1},{129,65},{193,129... | collective-permute-start | bytes 1376264 | tf_op jit(solution)/shard_map/far/ppermute | solution.py:408
  60.8 3.7 %far_one.1 = (f32[56,32,128]{2,1,0:T(8,128)S(1)}, bf16[56,32,128]{2,1,0:T(8,128)(2,1)S(1)}, bf16[56,32,128]{2,1,0:T(8,128)(2,1)S(1)}, f32[56,32,128]{2,1,0:T(8,128)S(1)}) custom-call(s32[3145728]{0:T(1024)} %get-tuple-element.20.plan_in, bf16[192,32,128]{2,1,0:T(8,128)(2,1)S(1)} %bitcast.20, bf16[4,128,64,128]{3,2,1,0:T(8,128)(2,1)} %get-tuple-element.21.refs_0_, ...), custom_call_target="tpu_custom_call" | custom-call | flops 100000000 | bytes 6000000 | tf_op jit(solution)/shard_map/far/far_one/pallas_call | solution.py:321
  64.5 1.5 %collective-permute-start = (bf16[56,32,128]{2,1,0:T(8,128)(2,1)S(1)}, bf16[56,32,128]{2,1,0:T(8,128)(2,1)S(1)}, u32[]{:S(2)}, u32[]{:S(2)}) collective-permute-start(bf16[56,32,128]{2,1,0:T(8,128)(2,1)S(1)} %get-tuple-element.23), channel_id=1, source_target_pairs={{0,192},{64,0},{128,64},{192,128},{1,193},{65,1},{129,65},{193,129... | collective-permute-start | bytes 1376264 | tf_op jit(solution)/shard_map/far/ppermute | solution.py:408
  65.9 0.0 collective-permute-done.1.early_a
  65.9 0.1 collective-permute-start.6
  66.0 0.0 collective-permute-done.3.early_b
  66.0 5.3 %collective-permute-done.2.passed_a = bf16[56,32,128]{2,1,0:T(8,128)(2,1)S(1)} collective-permute-done((bf16[56,32,128]{2,1,0:T(8,128)(2,1)S(1)}, bf16[56,32,128]{2,1,0:T(8,128)(2,1)S(1)}, u32[]{:S(2)}, u32[]{:S(2)}) %collective-permute-start.2) | collective-permute-done | bytes 458784 | tf_op jit(solution)/shard_map/far/ppermute | solution.py:405
  71.3 0.0 collective-permute-done.4.passed_b
  71.3 0.3 add_passed.1
  71.6 1.0 %collective-permute-start.8 = (bf16[44,32,128]{2,1,0:T(8,128)(2,1)S(1)}, bf16[44,32,128]{2,1,0:T(8,128)(2,1)S(1)}, u32[]{:S(2)}, u32[]{:S(2)}) collective-permute-start(bf16[44,32,128]{2,1,0:T(8,128)(2,1)S(1)} %get-tuple-element.33), channel_id=1, source_target_pairs={{0,64},{64,128},{128,192},{192,0},{1,65},{65,129},{129,193},{193,1... | collective-permute-start | bytes 1081352 | tf_op jit(solution)/shard_map/far/ppermute | solution.py:405
  72.6 1.8 %collective-permute-start.9 = (bf16[44,32,128]{2,1,0:T(8,128)(2,1)S(1)}, bf16[44,32,128]{2,1,0:T(8,128)(2,1)S(1)}, u32[]{:S(2)}, u32[]{:S(2)}) collective-permute-start(bf16[44,32,128]{2,1,0:T(8,128)(2,1)S(1)} %get-tuple-element.34), channel_id=1, source_target_pairs={{0,192},{64,0},{128,64},{192,128},{1,193},{65,1},{129,65},{193,129... | collective-permute-start | bytes 1081352 | tf_op jit(solution)/shard_map/far/ppermute | solution.py:408
  74.3 0.0 collective-permute-start.5
  74.3 6.4 %collective-permute-done.low_a = bf16[56,32,128]{2,1,0:T(8,128)(2,1)S(1)} collective-permute-done((bf16[56,32,128]{2,1,0:T(8,128)(2,1)S(1)}, bf16[56,32,128]{2,1,0:T(8,128)(2,1)S(1)}, u32[]{:S(2)}, u32[]{:S(2)}) %collective-permute-start) | collective-permute-done | bytes 458784 | tf_op jit(solution)/shard_map/far/ppermute | solution.py:408
  80.7 2.9 %collective-permute-start.7 = (bf16[12,32,128]{2,1,0:T(8,128)(2,1)S(1)}, bf16[12,32,128]{2,1,0:T(8,128)(2,1)S(1)}, u32[]{:S(2)}, u32[]{:S(2)}) collective-permute-start(bf16[12,32,128]{2,1,0:T(8,128)(2,1)S(1)} %get-tuple-element.32), channel_id=1, source_target_pairs={{0,192},{64,0},{128,64},{192,128},{1,193},{65,1},{129,65},{193,129... | collective-permute-start | bytes 294920 | tf_op jit(solution)/shard_map/far/ppermute | solution.py:408
  83.7 2.3 %far_own.1.own = f32[112,32,128]{2,1,0:T(8,128)S(1)} custom-call(s32[3145728]{0:T(1024)} %get-tuple-element.20.plan_in, bf16[192,32,128]{2,1,0:T(8,128)(2,1)S(1)} %bitcast.21, bf16[4,128,64,128]{3,2,1,0:T(8,128)(2,1)} %get-tuple-element.21.refs_0_, f32[4,112,32,128]{3,2,1,0:T(8,128)} %get-tuple-element.22.refs_1_), custom_call_target="tpu_custom_call" | custom-call | flops 100000000 | bytes 6000000 | tf_op jit(solution)/shard_map/far/far_own/pallas_call | solution.py:321
  86.0 0.0 collective-permute-done.6.high_a
  86.0 2.8 %collective-permute-done.8.low_b = bf16[44,32,128]{2,1,0:T(8,128)(2,1)S(1)} collective-permute-done((bf16[44,32,128]{2,1,0:T(8,128)(2,1)S(1)}, bf16[44,32,128]{2,1,0:T(8,128)(2,1)S(1)}, u32[]{:S(2)}, u32[]{:S(2)}) %collective-permute-start.8) | collective-permute-done | bytes 360480 | tf_op jit(solution)/shard_map/far/ppermute | solution.py:405
  88.8 0.0 collective-permute-done.9.high_b
  88.8 1.8 %finish_0.1.refs_0_ = f32[112,64,64]{2,1,0:T(8,128)} custom-call(f32[112,32,128]{2,1,0:T(8,128)S(1)} %far_own.1.own, bf16[56,32,128]{2,1,0:T(8,128)(2,1)S(1)} %collective-permute-done.low_a, bf16[44,32,128]{2,1,0:T(8,128)(2,1)S(1)} %collective-permute-done.8.low_b, bf16[56,32,128]{2,1,0:T(8,128)(2,1)S(1)} %collective-permute-done.6.high_a, ...), custom_call_target="tpu_custom_call" | custom-call | tf_op jit(solution)/shard_map/finish/finish_0/pallas_call | solution.py:379
  90.6 0.3 collective-permute-done.5.low_b
  91.0 0.0 collective-permute-done.7.high_b
  91.0 1.0 %finish_44.1 = f32[112,64,64]{2,1,0:T(8,128)} custom-call(f32[112,32,128]{2,1,0:T(8,128)S(1)} %far_own.1.own, bf16[56,32,128]{2,1,0:T(8,128)(2,1)S(1)} %collective-permute-done.low_a, bf16[12,32,128]{2,1,0:T(8,128)(2,1)S(1)} %collective-permute-done.5.low_b, bf16[56,32,128]{2,1,0:T(8,128)(2,1)S(1)} %collective-permute-done.6.high_a, ...), custom_call_target="tpu_custom_call", output_to_operand_aliasing={{}: (5, {})} | custom-call | tf_op jit(solution)/shard_map/finish/finish_44/pallas_call | solution.py:379
Async XLA Ops:
  2.8 52.8 %all-to-all-start = ((bf16[64,96,128]{2,1,0:T(8,128)(2,1)}), bf16[64,96,128]{2,1,0:T(8,128)(2,1)S(1)}, u32[]{:S(2)}, u32[]{:S(2)}) async-start(bf16[64,96,128]{2,1,0:T(8,128)(2,1)} %bitcast.22), calls=%async_computation | async-start | bytes 3145728 | tf_op jit(solution)/shard_map/exchange/all_to_all | solution.py:398
  38.7 27.2 %collective-permute-start.1 = (bf16[56,32,128]{2,1,0:T(8,128)(2,1)}, bf16[56,32,128]{2,1,0:T(8,128)(2,1)S(1)}, u32[]{:S(2)}, u32[]{:S(2)}) collective-permute-start(bf16[56,32,128]{2,1,0:T(8,128)(2,1)} %get-tuple-element.25), channel_id=1, source_target_pairs={{0,64},{64,128},{128,192},{192,0},{1,65},{65,129},{129,193},{193,1... | collective-permute-start | bytes 1376264 | tf_op jit(solution)/shard_map/early/ppermute | solution.py:405
  40.1 25.9 %collective-permute-start.3 = (bf16[56,32,128]{2,1,0:T(8,128)(2,1)}, bf16[56,32,128]{2,1,0:T(8,128)(2,1)S(1)}, u32[]{:S(2)}, u32[]{:S(2)}) collective-permute-start(bf16[56,32,128]{2,1,0:T(8,128)(2,1)} %get-tuple-element.28), channel_id=1, source_target_pairs={{0,192},{64,0},{128,64},{192,128},{1,193},{65,1},{129,65},{193,129... | collective-permute-start | bytes 1376264 | tf_op jit(solution)/shard_map/early/ppermute | solution.py:408
  57.9 13.4 %collective-permute-start.2 = (bf16[56,32,128]{2,1,0:T(8,128)(2,1)S(1)}, bf16[56,32,128]{2,1,0:T(8,128)(2,1)S(1)}, u32[]{:S(2)}, u32[]{:S(2)}) collective-permute-start(bf16[56,32,128]{2,1,0:T(8,128)(2,1)S(1)} %get-tuple-element.26), channel_id=1, source_target_pairs={{0,64},{64,128},{128,192},{192,0},{1,65},{65,129},{129,193},{193,1... | collective-permute-start | bytes 1376264 | tf_op jit(solution)/shard_map/far/ppermute | solution.py:405
  59.3 12.0 %collective-permute-start.4 = (bf16[56,32,128]{2,1,0:T(8,128)(2,1)S(1)}, bf16[56,32,128]{2,1,0:T(8,128)(2,1)S(1)}, u32[]{:S(2)}, u32[]{:S(2)}) collective-permute-start(bf16[56,32,128]{2,1,0:T(8,128)(2,1)S(1)} %get-tuple-element.29), channel_id=1, source_target_pairs={{0,192},{64,0},{128,64},{192,128},{1,193},{65,1},{129,65},{193,129... | collective-permute-start | bytes 1376264 | tf_op jit(solution)/shard_map/far/ppermute | solution.py:408
  64.5 16.3 %collective-permute-start = (bf16[56,32,128]{2,1,0:T(8,128)(2,1)S(1)}, bf16[56,32,128]{2,1,0:T(8,128)(2,1)S(1)}, u32[]{:S(2)}, u32[]{:S(2)}) collective-permute-start(bf16[56,32,128]{2,1,0:T(8,128)(2,1)S(1)} %get-tuple-element.23), channel_id=1, source_target_pairs={{0,192},{64,0},{128,64},{192,128},{1,193},{65,1},{129,65},{193,129... | collective-permute-start | bytes 1376264 | tf_op jit(solution)/shard_map/far/ppermute | solution.py:408
  65.9 20.1 %collective-permute-start.6 = (bf16[56,32,128]{2,1,0:T(8,128)(2,1)S(1)}, bf16[56,32,128]{2,1,0:T(8,128)(2,1)S(1)}, u32[]{:S(2)}, u32[]{:S(2)}) collective-permute-start(bf16[56,32,128]{2,1,0:T(8,128)(2,1)S(1)} %get-tuple-element.31), channel_id=1, source_target_pairs={{0,64},{64,128},{128,192},{192,0},{1,65},{65,129},{129,193},{193,1... | collective-permute-start | bytes 1376264 | tf_op jit(solution)/shard_map/far/ppermute | solution.py:405
  71.6 17.3 %collective-permute-start.8 = (bf16[44,32,128]{2,1,0:T(8,128)(2,1)S(1)}, bf16[44,32,128]{2,1,0:T(8,128)(2,1)S(1)}, u32[]{:S(2)}, u32[]{:S(2)}) collective-permute-start(bf16[44,32,128]{2,1,0:T(8,128)(2,1)S(1)} %get-tuple-element.33), channel_id=1, source_target_pairs={{0,64},{64,128},{128,192},{192,0},{1,65},{65,129},{129,193},{193,1... | collective-permute-start | bytes 1081352 | tf_op jit(solution)/shard_map/far/ppermute | solution.py:405
  72.6 16.3 %collective-permute-start.9 = (bf16[44,32,128]{2,1,0:T(8,128)(2,1)S(1)}, bf16[44,32,128]{2,1,0:T(8,128)(2,1)S(1)}, u32[]{:S(2)}, u32[]{:S(2)}) collective-permute-start(bf16[44,32,128]{2,1,0:T(8,128)(2,1)S(1)} %get-tuple-element.34), channel_id=1, source_target_pairs={{0,192},{64,0},{128,64},{192,128},{1,193},{65,1},{129,65},{193,129... | collective-permute-start | bytes 1081352 | tf_op jit(solution)/shard_map/far/ppermute | solution.py:408
  74.3 16.6 %collective-permute-start.5 = (bf16[12,32,128]{2,1,0:T(8,128)(2,1)S(1)}, bf16[12,32,128]{2,1,0:T(8,128)(2,1)S(1)}, u32[]{:S(2)}, u32[]{:S(2)}) collective-permute-start(bf16[12,32,128]{2,1,0:T(8,128)(2,1)S(1)} %get-tuple-element.30), channel_id=1, source_target_pairs={{0,64},{64,128},{128,192},{192,0},{1,65},{65,129},{129,193},{193,1... | collective-permute-start | bytes 294920 | tf_op jit(solution)/shard_map/far/ppermute | solution.py:405
  80.7 10.2 %collective-permute-start.7 = (bf16[12,32,128]{2,1,0:T(8,128)(2,1)S(1)}, bf16[12,32,128]{2,1,0:T(8,128)(2,1)S(1)}, u32[]{:S(2)}, u32[]{:S(2)}) collective-permute-start(bf16[12,32,128]{2,1,0:T(8,128)(2,1)S(1)} %get-tuple-element.32), channel_id=1, source_target_pairs={{0,192},{64,0},{128,64},{192,128},{1,193},{65,1},{129,65},{193,129... | collective-permute-start | bytes 294920 | tf_op jit(solution)/shard_map/far/ppermute | solution.py:408
